TPU v7x, 512 devices: a whole 4x4x16 slice. The times are simulated.
512 devices in a mesh: slab: 64 (over z, y), atom: 8 (over x, core).
Axes of the slice: x: 4, y: 4, z: 16, core: 2. Of those that a mesh axis runs over, the one named last changes fastest.
Arguments:
- atom_feats: bfloat16 [32768, 3200], P(('slab', 'atom')), may hold values from -6 to 6
- species: int32 [32768], P(('slab', 'atom')), may hold values from 0 to 7
- send_rows: int32 [64, 8, 4, 64], P('slab', 'atom'), may hold values from 0 to 64
- neighbours: int32 [16, 8192], P('atom', 'slab'), may hold values from 0 to 320, as said below
- harmonics: float32 [25, 16, 8192], P(None, 'atom', 'slab'), may hold values from -1 to 1
- distances: float32 [16, 8192], P('atom', 'slab'), may hold values from 0.5 to 3.8
- target: float32 [8192], P('slab'), may hold values from -6 to 6
- w_deg: bfloat16 [5, 128, 128], replicated, may hold values from -0.5 to 0.5
- w_gate: bfloat16 [128, 512], replicated, may hold values from -0.5 to 0.5
- embed: float32 [8, 128], replicated, may hold values from -3 to 3
- w_radial: float32 [8, 640], replicated, may hold values from -2 to 2
- w_hidden: float32 [128, 128], replicated, may hold values from -0.5 to 0.5
- b_hidden: float32 [128], replicated, may hold values from -3 to 3
- w_out: float32 [128], replicated, may hold values from -0.5 to 0.5
Outputs:
- loss: float32 [], replicated
- density: float32 [8192], P('slab')
- grad_deg: float32 [5, 128, 128], replicated
- grad_gate: float32 [128, 512], replicated
- grad_embed: float32 [8, 128], replicated
- grad_radial: float32 [8, 640], replicated
- grad_hidden: float32 [128, 128], replicated
- grad_hbias: float32 [128], replicated
- grad_out: float32 [128], replicated
Inputs may be any that keep to these rules, and one draw needn't show every extreme that they name: `send_rows`: entries name rows of one device's atoms; the value 64 marks an empty slot. `neighbours`: entries name rows of the buffer of the probe's slab and the row's shard; 320 is its zero row and marks an empty slot.
All inputs are finite; a program needn't handle non-finite values.
Results may differ from a plain program's by a relative error of at most 0.0055.
Values may be sent and summed in bfloat16 or wider, within the bound.
No kernel may reach another device: no remote copies, remote signals or barrier semaphores. Data moves between devices by JAX's collectives and lax.ppermute only.
A program may use at most 128 MiB of HBM per device.

v0:
```python
import math

import jax
import jax.numpy as jnp
from jax import lax
from jax.sharding import PartitionSpec as P

OFFSETS = (-2, -1, 1, 2)
CUTOFF = 4.0
PRECISE = lax.Precision.HIGHEST


def passed_along(block, axis, distance):
    devices = range(lax.axis_size(axis))
    route = [((i - distance) % len(devices), i) for i in devices]
    return lax.ppermute(block, axis, route)


def silu_slope(values):
    logistic = jax.nn.sigmoid(values)
    return logistic * (1.0 + values * (1.0 - logistic))


def contract_rows(left, right, precision=None):
    return lax.dot_general(
        left,
        right,
        (((0,), (0,)), ((), ())),
        preferred_element_type=jnp.float32,
        precision=precision,
    )


def encode(features, species, w_deg, w_gate, embed):
    atoms = features.shape[0]
    chans = w_deg.shape[1]
    degrees = w_deg.shape[0]
    kinds = embed.shape[0]
    blocks = features.reshape(atoms, degrees * degrees, chans)
    mixed = []
    for degree in range(degrees):
        lower = degree * degree
        upper = (degree + 1) * (degree + 1)
        flat = blocks[:, lower:upper, :].reshape(-1, chans)
        mixed.append(
            jnp.dot(flat, w_deg[degree], preferred_element_type=jnp.float32).reshape(
                atoms, upper - lower, chans
            )
        )
    gates = jax.nn.sigmoid(jnp.dot(blocks[:, 0, :], w_gate, preferred_element_type=jnp.float32))
    onehot = (species[:, None] == jnp.arange(kinds, dtype=jnp.int32)[None, :]).astype(jnp.float32)
    looked_up = jnp.dot(onehot, embed, precision=PRECISE)
    pieces = [blocks[:, 0:1, :].astype(jnp.float32) + jax.nn.silu(mixed[0]) + looked_up[:, None, :]]
    for degree in range(1, degrees):
        lower = degree * degree
        upper = (degree + 1) * (degree + 1)
        gate = gates[:, (degree - 1) * chans : degree * chans]
        pieces.append(
            blocks[:, lower:upper, :].astype(jnp.float32) + mixed[degree] * gate[:, None, :]
        )
    updated = jnp.concatenate(pieces, axis=1).reshape(atoms, -1).astype(jnp.bfloat16)
    return (updated, (mixed, gates, onehot))


def encode_grads(features, saved, cotangent, w_deg):
    mixed, gates, onehot = saved
    atoms = features.shape[0]
    chans = w_deg.shape[1]
    degrees = w_deg.shape[0]
    blocks = features.reshape(atoms, degrees * degrees, chans)
    upstream = cotangent.reshape(atoms, degrees * degrees, chans)
    scalar_up = upstream[:, 0, :]
    grad_embed = contract_rows(onehot, scalar_up, PRECISE)
    first = (scalar_up * silu_slope(mixed[0][:, 0, :])).astype(jnp.bfloat16)
    grad_list = [contract_rows(blocks[:, 0, :], first)]
    pre_list = []
    for degree in range(1, degrees):
        lower = degree * degree
        upper = (degree + 1) * (degree + 1)
        gate = gates[:, (degree - 1) * chans : degree * chans]
        local_up = upstream[:, lower:upper, :]
        mixed_grad = (local_up * gate[:, None, :]).astype(jnp.bfloat16).reshape(-1, chans)
        grad_list.append(contract_rows(blocks[:, lower:upper, :].reshape(-1, chans), mixed_grad))
        pre_list.append(jnp.sum(local_up * mixed[degree], axis=1) * gate * (1.0 - gate))
    gate_input = jnp.concatenate(pre_list, axis=1).astype(jnp.bfloat16)
    grad_gate = contract_rows(blocks[:, 0, :], gate_input)
    return (jnp.stack(grad_list), grad_gate, grad_embed)


def radial_basis(distance, count):
    orders = jnp.arange(1, count + 1).astype(jnp.float32)
    phase = math.pi * distance / CUTOFF
    envelope = 0.5 * (jnp.cos(phase) + 1.0) / distance
    return jnp.sin(phase[:, None] * orders[None, :]) * envelope[:, None]


def pair_sums(gathered, harm, chans):
    degrees = math.isqrt(harm.shape[0])
    sums = []
    for degree in range(degrees):
        total = None
        for comp in range(degree * degree, (degree + 1) * (degree + 1)):
            term = harm[comp][:, None] * gathered[:, comp * chans : (comp + 1) * chans].astype(
                jnp.float32
            )
            total = term if total is None else total + term
        sums.append(total)
    return sums


def probe_forward(gathered, harm, basis, w_radial):
    degrees = math.isqrt(harm.shape[0])
    chans = w_radial.shape[1] // degrees
    radial = jnp.dot(basis, w_radial, precision=PRECISE)
    sums = pair_sums(gathered, harm, chans)
    result = None
    for degree in range(degrees):
        term = radial[:, degree * chans : (degree + 1) * chans] * sums[degree]
        result = term if result is None else result + term
    return result


def probe_backward(gathered, harm, basis, w_radial, upstream):
    degrees = math.isqrt(harm.shape[0])
    chans = w_radial.shape[1] // degrees
    radial = jnp.dot(basis, w_radial, precision=PRECISE)
    sums = pair_sums(gathered, harm, chans)
    radial_up = jnp.concatenate([sums[degree] * upstream for degree in range(degrees)], axis=1)
    row_parts = []
    for degree in range(degrees):
        inner = radial[:, degree * chans : (degree + 1) * chans] * upstream
        for comp in range(degree * degree, (degree + 1) * (degree + 1)):
            row_parts.append(harm[comp][:, None] * inner)
    return (jnp.concatenate(row_parts, axis=1), contract_rows(basis, radial_up, PRECISE))


def readout(summed, target, w_hidden, b_hidden, w_out, scale):
    hidden_pre = jnp.dot(summed, w_hidden, precision=PRECISE) + b_hidden[None, :]
    activated = jax.nn.silu(hidden_pre)
    density = jnp.dot(activated, w_out, precision=PRECISE)
    error = density - target
    loss = 0.5 * scale * jnp.sum(error * error)
    error_grad = error * scale
    grad_out = jnp.dot(error_grad, activated, precision=PRECISE)
    pre_grad = error_grad[:, None] * w_out[None, :] * silu_slope(hidden_pre)
    grad_hidden = contract_rows(summed, pre_grad, PRECISE)
    grad_hbias = jnp.sum(pre_grad, axis=0)
    summed_grad = jnp.dot(pre_grad, w_hidden.T, precision=PRECISE)
    return (density, summed_grad, (grad_hidden, grad_hbias, grad_out), loss)


def split_blocks(rows_index, harm, dist, block):
    slots, probes = rows_index.shape
    comps = harm.shape[0]
    block_count = probes // block
    nbr_blocks = (
        rows_index.reshape(slots, block_count, block)
        .transpose(1, 0, 2)
        .reshape(block_count, slots * block)
    )
    harm_blocks = (
        harm.reshape(comps, slots, block_count, block)
        .transpose(2, 0, 1, 3)
        .reshape(block_count, comps, slots * block)
    )
    dist_blocks = (
        dist.reshape(slots, block_count, block)
        .transpose(1, 0, 2)
        .reshape(block_count, slots * block)
    )
    return (nbr_blocks, harm_blocks, dist_blocks)


def probe_block_sums(table, pieces, w_radial, slots, block, chans):
    basis_count = w_radial.shape[0]

    def forward_block(item):
        rows_index, harm, dist = item
        contrib = probe_forward(table[rows_index], harm, radial_basis(dist, basis_count), w_radial)
        return contrib.reshape(slots, block, chans).sum(axis=0)

    return lax.map(forward_block, pieces).reshape(-1, chans)


def pair_block_grads(table, pieces, upstream, w_radial, slots, block, chans, start):
    basis_count = w_radial.shape[0]
    grad_blocks = upstream.reshape(-1, block, chans)

    def backward_block(carry, item):
        row_grads, radial_grad = carry
        rows_index, harm, dist, probe_grad = item
        spread = jnp.broadcast_to(probe_grad[None], (slots, block, chans)).reshape(-1, chans)
        pair_grads, weight_grad = probe_backward(
            table[rows_index], harm, radial_basis(dist, basis_count), w_radial, spread
        )
        return ((row_grads.at[rows_index].add(pair_grads), radial_grad + weight_grad), None)

    result, unused = lax.scan(backward_block, start, (pieces[0], pieces[1], pieces[2], grad_blocks))
    return result


def on_device(
    atom_feats,
    species,
    send_rows,
    neighbours,
    harmonics,
    distances,
    target,
    w_deg,
    w_gate,
    embed,
    w_radial,
    w_hidden,
    b_hidden,
    w_out,
):
    count, width = atom_feats.shape
    chans = w_deg.shape[1]
    slots, probes = neighbours.shape
    capacity = send_rows.shape[3]
    encoded, saved = encode(atom_feats, species, w_deg, w_gate, embed)
    padded = jnp.concatenate([encoded, jnp.zeros((1, width), jnp.bfloat16)], axis=0)
    lists = send_rows[0, 0]
    outgoing = [padded[lists[which]] for which in range(len(OFFSETS))]
    incoming = [
        passed_along(outgoing[which], "slab", OFFSETS[which]) for which in range(len(OFFSETS))
    ]
    buffer = jnp.concatenate([encoded] + incoming + [jnp.zeros((1, width), jnp.bfloat16)], axis=0)
    own_pieces = split_blocks(neighbours, harmonics, distances, probes)
    partial_value = probe_block_sums(buffer, own_pieces, w_radial, slots, probes, chans)
    slab_count = lax.axis_size("slab")
    shard_count = lax.axis_size("atom")
    scale = 1.0 / math.sqrt(probes * slab_count)
    summed = lax.psum(partial_value, "atom")
    density, summed_grad, head_grads, loss = readout(
        summed, target, w_hidden, b_hidden, w_out, scale
    )
    weight = 1.0 / shard_count
    head_grads = (head_grads[0] * weight, head_grads[1] * weight, head_grads[2] * weight)
    loss = loss * weight
    start = (
        jnp.zeros((buffer.shape[0], width), jnp.float32),
        jnp.zeros(w_radial.shape, jnp.float32),
    )
    row_grads, grad_radial = pair_block_grads(
        buffer, own_pieces, summed_grad, w_radial, slots, probes, chans, start
    )
    returned = [
        row_grads[count + which * capacity : count + (which + 1) * capacity]
        for which in range(len(OFFSETS))
    ]
    back = [passed_along(returned[which], "slab", -OFFSETS[which]) for which in range(len(OFFSETS))]
    atom_grad = jnp.concatenate([row_grads[:count], jnp.zeros((1, width), jnp.float32)], axis=0)
    for which in range(len(OFFSETS)):
        atom_grad = atom_grad.at[lists[which]].add(back[which])
    grad_deg, grad_gate, grad_embed = encode_grads(atom_feats, saved, atom_grad[:count], w_deg)
    totals = lax.psum(
        (
            grad_deg,
            grad_gate,
            grad_embed,
            grad_radial,
            head_grads[0],
            head_grads[1],
            head_grads[2],
            loss,
        ),
        ("slab", "atom"),
    )
    return (
        totals[7],
        density,
        totals[0],
        totals[1],
        totals[2],
        totals[3],
        totals[4],
        totals[5],
        totals[6],
    )


def solution(mesh):
    in_specs = (
        P(("slab", "atom"), None),
        P(("slab", "atom")),
        P("slab", "atom", None, None),
        P("atom", "slab"),
        P(None, "atom", "slab"),
        P("atom", "slab"),
        P("slab"),
        P(),
        P(),
        P(),
        P(),
        P(),
        P(),
        P(),
    )
    out_specs = (P(), P("slab"), P(), P(), P(), P(), P(), P(), P())
    return jax.shard_map(
        on_device, mesh=mesh, in_specs=in_specs, out_specs=out_specs, check_vma=False
    )
```

profile of v0, /device:TPU:1, one launch (start us, length us, event | category | flops | bytes accessed | tf_op | source)
XLA Modules:
  0.0 722.3 jit_solution(14987680194921424710)
XLA Ops:
  14.6 1.6 gather_fusion
  16.2 14.6 %collective-permute-start = (bf16[64,3200]{1,0:T(8,128)(2,1)}, bf16[64,3200]{1,0:T(8,128)(2,1)}, u32[]{:S(2)}, u32[]{:S(2)}) collective-permute-start(bf16[64,3200]{1,0:T(8,128)(2,1)} %gather_fusion), channel_id=1, source_target_pairs={{16,0},{24,8},{32,16},{40,24},{48,32},{56,40},{64,48},{72,56},{80,... | collective-permute-start | bytes 1228808 | tf_op jit(solution)/shard_map/ppermute | solution.py:16
  30.8 1.6 gather_fusion.1
  32.4 2.7 collective-permute-start.1
  35.1 1.6 gather_fusion.2
  36.7 2.6 collective-permute-start.2
  39.3 1.6 gather_fusion.3
  40.9 2.6 collective-permute-start.3
  45.6 1.8 fusion.18
  49.6 4.2 collective-permute-done.2
  54.8 5.2 collective-permute-done.3
  60.1 3.0 gather_fusion.4
  63.2 2.5 multiply_add_fusion
  66.6 68.7 %all-reduce.6.cloned.1.call-done = f32[128,128]{1,0:T(8,128)} async-done(((f32[128,128]{1,0:T(8,128)}), f32[128,128]{1,0:T(8,128)}) %all-reduce.6.cloned.1.call-update) | async-done | bytes 65552 | tf_op jit(solution)/shard_map/psum | solution.py:235
  136.5 1.3 broadcast_multiply_fusion.1
  143.6 1.6 fusion.17
  145.3 8.6 %scatter_custom_fusion = f32[321,3200]{1,0:T(8,128)} fusion(s32[256]{0:T(256)} %bitcast.214, f32[256,3200]{1,0:T(8,128)} %copy-done.49, f32[]{:T(128)} %constant.53.clone.1), kind=kCustom, calls=%fused_computation.10 | custom fusion | flops 819200 | bytes 4109312 | tf_op jit(solution)/shard_map/while/body/eval_jaxpr/scatter-add | solution.py:196
  153.9 3.0 fusion.82
  156.9 7.3 %collective-permute-start.7 = (f32[64,3200]{1,0:T(8,128)S(1)}, f32[64,3200]{1,0:T(8,128)}, u32[]{:S(2)}, u32[]{:S(2)}) collective-permute-start(f32[64,3200]{1,0:T(8,128)S(1)} %get-tuple-element.87), channel_id=1, source_target_pairs={{16,0},{24,8},{32,16},{40,24},{48,32},{56,40},{64,48},{72,56},{80,... | collective-permute-start | bytes 2457608 | tf_op jit(solution)/shard_map/ppermute | solution.py:16
  164.3 2.8 collective-permute-start.6
  167.1 2.5 collective-permute-start.5
  169.6 2.5 collective-permute-start.4
  174.4 40.3 %collective-permute-done.4 = f32[64,3200]{1,0:T(8,128)} collective-permute-done((f32[64,3200]{1,0:T(8,128)S(1)}, f32[64,3200]{1,0:T(8,128)}, u32[]{:S(2)}, u32[]{:S(2)}) %collective-permute-start.4) | collective-permute-done | bytes 819232 | tf_op jit(solution)/shard_map/ppermute | solution.py:16
  214.8 2.6 scatter_fusion
  217.4 2.6 scatter_fusion.1
  220.1 2.8 scatter_fusion.2
  222.9 2.6 scatter_fusion.3
  231.8 119.6 %all-reduce.1 = (f32[]{:T(128)}, f32[8,128]{1,0:T(8,128)}, f32[8,640]{1,0:T(8,128)}, f32[128]{0:T(128)}, f32[128]{0:T(128)}) all-reduce(f32[]{:T(128)S(6)} %mul.1109, f32[8,128]{1,0:T(8,128)S(1)} %fusion.53, f32[8,640]{1,0:T(8,128)S(1)} %copy-done.18, ...), channel_id=1, replica_groups=mesh['slab'=64,'atom'=8] {'slab','atom'}, use_global_device_ids=true, to_apply=%region_3.4 | all-reduce | flops 6401 | bytes 51208 | tf_op jit(solution)/shard_map/psum | solution.py:258
  351.4 358.9 %all-reduce.8.cloned.1.call-done = (f32[5,128,128]{1,2,0:T(8,128)}, f32[128,512]{0,1:T(8,128)}, f32[128,128]{1,0:T(8,128)}) async-done(((f32[5,128,128]{1,2,0:T(8,128)}, f32[128,512]{0,1:T(8,128)}, f32[128,128]{1,0:T(8,128)}), (f32[5,128,128]{1,2,0:T(8,128)}, f32[128,512]{0,1:T(8,128)}, f32[128,128]{1,0:T(8,128)})) %all-reduce.8.cloned.1.call-update) | async-done | bytes 655376 | tf_op jit(solution)/shard_map/psum | solution.py:258
  710.3 1.9 copy.36
  712.2 1.8 copy.37
  713.9 1.5 copy.141
  (238 shorter events, 27.2 us)
Async XLA Ops:
  7.2 128.1 %all-reduce.6.cloned.1.call-start = ((), (), s32[]{:S(2)}) async-start(), calls=%async_computation | async-start | bytes 131072 | tf_op jit(solution)/shard_map/psum | solution.py:235
  9.6 21.2 %copy-start.54 = (s32[64]{0:T(128)}, s32[64]{0:T(128)S(1)}, u32[]{:S(2)}) copy-start(s32[64]{0:T(128)S(1)} %get-tuple-element.144) | copy-start | bytes 772
  9.6 25.5 %copy-start.52 = (s32[64]{0:T(128)}, s32[64]{0:T(128)S(1)}, u32[]{:S(2)}) copy-start(s32[64]{0:T(128)S(1)} %get-tuple-element.146) | copy-start | bytes 772
  9.6 29.7 %copy-start.50 = (s32[64]{0:T(128)}, s32[64]{0:T(128)S(1)}, u32[]{:S(2)}) copy-start(s32[64]{0:T(128)S(1)} %get-tuple-element.143) | copy-start | bytes 772
  10.8 34.8 %copy-start.13 = (f32[64,128]{1,0:T(8,128)}, f32[64,128]{1,0:T(8,128)S(1)}, u32[]{:S(2)}) copy-start(f32[64,128]{1,0:T(8,128)S(1)} %get-tuple-element.104) | copy-start | bytes 98308
  10.8 34.8 %copy-start.14 = (f32[64,128]{1,0:T(8,128)}, f32[64,128]{1,0:T(8,128)S(1)}, u32[]{:S(2)}) copy-start(f32[64,128]{1,0:T(8,128)S(1)} %get-tuple-element.105) | copy-start | bytes 98308
  16.2 31.2 %collective-permute-start = (bf16[64,3200]{1,0:T(8,128)(2,1)}, bf16[64,3200]{1,0:T(8,128)(2,1)}, u32[]{:S(2)}, u32[]{:S(2)}) collective-permute-start(bf16[64,3200]{1,0:T(8,128)(2,1)} %gather_fusion), channel_id=1, source_target_pairs={{16,0},{24,8},{32,16},{40,24},{48,32},{56,40},{64,48},{72,56},{80,... | collective-permute-start | bytes 1228808 | tf_op jit(solution)/shard_map/ppermute | solution.py:16
  32.4 16.1 %collective-permute-start.1 = (bf16[64,3200]{1,0:T(8,128)(2,1)}, bf16[64,3200]{1,0:T(8,128)(2,1)}, u32[]{:S(2)}, u32[]{:S(2)}) collective-permute-start(bf16[64,3200]{1,0:T(8,128)(2,1)} %gather_fusion.1), channel_id=1, source_target_pairs={{8,0},{16,8},{24,16},{32,24},{40,32},{48,40},{56,48},{64,56},{72,6... | collective-permute-start | bytes 1228808 | tf_op jit(solution)/shard_map/ppermute | solution.py:16
  35.1 9.8 %copy-start.62 = (s32[2,128]{1,0:T(2,128)S(1)}, s32[2,128]{1,0:T(2,128)}, u32[]{:S(2)}) copy-start(s32[2,128]{1,0:T(2,128)} %param.17) | copy-start | bytes 3076
  35.1 10.4 %copy-start.61 = (f32[2,128]{1,0:T(2,128)S(1)}, f32[2,128]{1,0:T(2,128)}, u32[]{:S(2)}) copy-start(f32[2,128]{1,0:T(2,128)} %param.19) | copy-start | bytes 3076
  36.7 17.1 %collective-permute-start.2 = (bf16[64,3200]{1,0:T(8,128)(2,1)}, bf16[64,3200]{1,0:T(8,128)(2,1)}, u32[]{:S(2)}, u32[]{:S(2)}) collective-permute-start(bf16[64,3200]{1,0:T(8,128)(2,1)} %gather_fusion.2), channel_id=1, source_target_pairs={{504,0},{0,8},{8,16},{16,24},{24,32},{32,40},{40,48},{48,56},{56,6... | collective-permute-start | bytes 1228808 | tf_op jit(solution)/shard_map/ppermute | solution.py:16
  40.9 19.2 %collective-permute-start.3 = (bf16[64,3200]{1,0:T(8,128)(2,1)}, bf16[64,3200]{1,0:T(8,128)(2,1)S(1)}, u32[]{:S(2)}, u32[]{:S(2)}) collective-permute-start(bf16[64,3200]{1,0:T(8,128)(2,1)} %gather_fusion.3), channel_id=1, source_target_pairs={{496,0},{504,8},{0,16},{8,24},{16,32},{24,40},{32,48},{40,56},{48,... | collective-permute-start | bytes 1228808 | tf_op jit(solution)/shard_map/ppermute | solution.py:16
  43.6 16.5 %copy-start.59 = (f32[8]{0:T(128)}, f32[8]{0:T(128)S(1)}, u32[]{:S(2)}) copy-start(f32[8]{0:T(128)S(1)} %add_convert_fusion.4) | copy-start | bytes 100
  63.2 73.3 %copy-start.63 = (f32[128]{0:T(128)S(1)}, f32[128]{0:T(128)}, u32[]{:S(2)}) copy-start(f32[128]{0:T(128)} %param.27) | copy-start | bytes 1540
  63.2 73.3 %copy-start.67 = (f32[128]{0:T(128)S(1)}, f32[128]{0:T(128)}, u32[]{:S(2)}) copy-start(f32[128]{0:T(128)} %param.20) | copy-start | bytes 1540
  63.2 75.9 %copy-start.19 = (f32[128,128]{1,0:T(8,128)S(1)}, f32[128,128]{1,0:T(8,128)}, u32[]{:S(2)}) copy-start(f32[128,128]{1,0:T(8,128)} %param.25) | copy-start | bytes 196612
  63.2 76.3 %copy-start.48 = (f32[256]{0:T(256)S(1)}, f32[256]{0:T(256)}, u32[]{:S(2)}) copy-start(f32[256]{0:T(256)} %get-tuple-element.141) | copy-start | bytes 3076
  65.7 75.4 %copy-start.47 = (f32[256]{0:T(256)S(1)}, f32[256]{0:T(256)}, u32[]{:S(2)}) copy-start(f32[256]{0:T(256)} %get-tuple-element.136) | copy-start | bytes 3076
  65.7 75.6 %copy-start.46 = (f32[256]{0:T(256)S(1)}, f32[256]{0:T(256)}, u32[]{:S(2)}) copy-start(f32[256]{0:T(256)} %get-tuple-element.135) | copy-start | bytes 3076
  65.7 75.7 %copy-start.45 = (f32[256]{0:T(256)S(1)}, f32[256]{0:T(256)}, u32[]{:S(2)}) copy-start(f32[256]{0:T(256)} %get-tuple-element.134) | copy-start | bytes 3076
  65.7 75.8 %copy-start.44 = (f32[256]{0:T(256)S(1)}, f32[256]{0:T(256)}, u32[]{:S(2)}) copy-start(f32[256]{0:T(256)} %get-tuple-element.133) | copy-start | bytes 3076
  65.7 75.9 %copy-start.43 = (f32[256]{0:T(256)S(1)}, f32[256]{0:T(256)}, u32[]{:S(2)}) copy-start(f32[256]{0:T(256)} %get-tuple-element.132) | copy-start | bytes 3076
  66.4 75.3 %copy-start.42 = (f32[256]{0:T(256)S(1)}, f32[256]{0:T(256)}, u32[]{:S(2)}) copy-start(f32[256]{0:T(256)} %get-tuple-element.131) | copy-start | bytes 3076
  66.4 643.9 %all-reduce.8.cloned.1.call-start = ((), (), s32[]{:S(2)}) async-start(), calls=%async_computation.1 | async-start | bytes 1310720 | tf_op jit(solution)/shard_map/psum | solution.py:258
  153.9 18.2 %copy-start.20 = (f32[128,128]{1,0:T(8,128)S(1)}, f32[128,128]{1,0:T(8,128)}, u32[]{:S(2)}) copy-start(f32[128,128]{1,0:T(8,128)} %all-reduce.6.cloned.1.call-done) | copy-start | bytes 196612
  153.9 19.2 %copy-start.66 = (pred[65]{0:T(512)(128)(4,1)S(1)}, pred[65]{0:T(512)(128)(4,1)}, u32[]{:S(2)}) copy-start(pred[65]{0:T(512)(128)(4,1)} %constant.55.clone.1) | copy-start | bytes 199
  153.9 60.9 %copy-start.57 = (s32[64]{0:T(128)S(1)}, s32[64]{0:T(128)}, u32[]{:S(2)}) copy-start(s32[64]{0:T(128)} %copy-done.56) | copy-start | bytes 772
  156.9 66.0 %collective-permute-start.7 = (f32[64,3200]{1,0:T(8,128)S(1)}, f32[64,3200]{1,0:T(8,128)}, u32[]{:S(2)}, u32[]{:S(2)}) collective-permute-start(f32[64,3200]{1,0:T(8,128)S(1)} %get-tuple-element.87), channel_id=1, source_target_pairs={{16,0},{24,8},{32,16},{40,24},{48,32},{56,40},{64,48},{72,56},{80,... | collective-permute-start | bytes 2457608 | tf_op jit(solution)/shard_map/ppermute | solution.py:16
  164.3 55.8 %collective-permute-start.6 = (f32[64,3200]{1,0:T(8,128)S(1)}, f32[64,3200]{1,0:T(8,128)}, u32[]{:S(2)}, u32[]{:S(2)}) collective-permute-start(f32[64,3200]{1,0:T(8,128)S(1)} %get-tuple-element.88), channel_id=1, source_target_pairs={{8,0},{16,8},{24,16},{32,24},{40,32},{48,40},{56,48},{64,56},{72,6... | collective-permute-start | bytes 2457608 | tf_op jit(solution)/shard_map/ppermute | solution.py:16
  167.1 50.3 %collective-permute-start.5 = (f32[64,3200]{1,0:T(8,128)}, f32[64,3200]{1,0:T(8,128)}, u32[]{:S(2)}, u32[]{:S(2)}) collective-permute-start(f32[64,3200]{1,0:T(8,128)} %get-tuple-element.89), channel_id=1, source_target_pairs={{504,0},{0,8},{8,16},{16,24},{24,32},{32,40},{40,48},{48,56},{56,6... | collective-permute-start | bytes 2457608 | tf_op jit(solution)/shard_map/ppermute | solution.py:16
  169.6 45.2 %collective-permute-start.4 = (f32[64,3200]{1,0:T(8,128)S(1)}, f32[64,3200]{1,0:T(8,128)}, u32[]{:S(2)}, u32[]{:S(2)}) collective-permute-start(f32[64,3200]{1,0:T(8,128)S(1)} %get-tuple-element.90), channel_id=1, source_target_pairs={{496,0},{504,8},{0,16},{8,24},{16,32},{24,40},{32,48},{40,56},{48,... | collective-permute-start | bytes 2457608 | tf_op jit(solution)/shard_map/ppermute | solution.py:16
  174.4 43.0 %copy-start.55 = (s32[64]{0:T(128)S(1)}, s32[64]{0:T(128)}, u32[]{:S(2)}) copy-start(s32[64]{0:T(128)} %copy-done.54) | copy-start | bytes 772
  (47 other events, 161.6 us)
Sparse Core Ops, SparseCore 0:
  66.5 68.8 all-reduce.5
  231.0 479.2 all-reduce.7
where the time goes:
time: 724 us; the launch traced here: 722 us
  waiting for transfers between devices  477 us (66%)
  blocking collectives  120 us (17%)
  starting transfers between devices  37.9 us (5%)
  other arithmetic  29.6 us (4%)
  local copies, waits for them, and re-layouts  24.3 us (3%)
  matrix products  17.1 us (2%)
  between operations  16.3 us (2%)
    psum x1, waiting for transfers between devices, on_device(): lax.psum((grad_deg, grad_gate, grad_embed, grad_radial, head_grads[0], he...  359 us
    psum x1, blocking collectives, on_device(): lax.psum((grad_deg, grad_gate, grad_embed, grad_radial, head_grads[0], he...  120 us
    psum x1, waiting for transfers between devices, on_device(): summed = lax.psum(partial_value, 'atom')  68.7 us
    ppermute x8, waiting for transfers between devices, passed_along(): return lax.ppermute(block, axis, route)  49.8 us
    ppermute x8, starting transfers between devices, passed_along(): return lax.ppermute(block, axis, route)  37.6 us
  transfers between devices with their start and end apart: 10, of which 5 were waited for; matrix products, arithmetic and copies ran while one was open for 3% of the time, Pallas kernels for 0%

commit v1 on v0

v1 whole, which is shorter than its diff:
```python
import functools
import math

import jax
import jax.numpy as jnp
from jax import lax
from jax.experimental import pallas as pl
from jax.experimental.pallas import tpu as pltpu
from jax.sharding import Mesh, PartitionSpec as P

OFFSETS = (-2, -1, 1, 2)
CUTOFF = 4.0
PRECISE = lax.Precision.HIGHEST
F32 = jnp.float32
BF16 = jnp.bfloat16
SLAB = ("z", "y")
ATOM = ("x", "c")
PLANE = ("y", "x", "c")
DEGREES = 5
COMPS = DEGREES * DEGREES
CHANS = 128
ATOMS = 64
SLOTS = 2
PROBES = 128
SOURCES = 1 + len(OFFSETS)
SPAN = SLOTS * PROBES
PAIRS = SOURCES * SPAN
FIELDS = 32
BASES = 8
KINDS = 8
PAYLOAD = 1536


def first_rows(degree):
    return degree * degree * ATOMS, (degree + 1) * (degree + 1) * ATOMS


def lanes(block):
    return slice(block * CHANS, (block + 1) * CHANS)


def along_first(left, right, precision=None):
    return lax.dot_general(
        left, right, (((0,), (0,)), ((), ())), preferred_element_type=F32, precision=precision
    )


def along_last(left, right, precision=None):
    return lax.dot_general(
        left, right, (((1,), (1,)), ((), ())), preferred_element_type=F32, precision=precision
    )


def matmul(left, right, precision=None):
    return jnp.dot(left, right, preferred_element_type=F32, precision=precision)


def component_rows(feats_ref, degree):
    parts = [feats_ref[:, lanes(m)] for m in range(degree * degree, (degree + 1) * (degree + 1))]
    return parts[0] if degree == 0 else jnp.concatenate(parts, axis=0)


def over_components(gate, degree):
    return jnp.concatenate([gate] * (2 * degree + 1), axis=0)


def kind_rows(species_ref):
    ids = lax.broadcasted_iota(jnp.int32, (KINDS, ATOMS), 0)
    return (ids == species_ref[...]).astype(F32)


def encode_kernel(feats_ref, species_ref, w_deg_ref, w_gate_ref, embed_ref, rows_ref):
    scalar = feats_ref[:, lanes(0)]
    gates = jax.nn.sigmoid(matmul(scalar, w_gate_ref[...]))
    for degree in range(DEGREES):
        low, high = first_rows(degree)
        rows = component_rows(feats_ref, degree)
        mixed = matmul(rows, w_deg_ref[degree])
        if degree == 0:
            added = jax.nn.silu(mixed) + along_first(
                kind_rows(species_ref), embed_ref[...], PRECISE
            )
        else:
            added = mixed * over_components(gates[:, lanes(degree - 1)], degree)
        rows_ref[low:high, :] = (rows.astype(F32) + added).astype(BF16)


def pair_kernel(rows_ref, lists_ref, w_radial_ref, *refs):
    packs = refs[:SOURCES]
    out_refs = refs[SOURCES : 2 * SOURCES]
    spread_ref, sums_ref, radial_ref, basis_ref = refs[2 * SOURCES :]
    sub = lax.broadcasted_iota(jnp.int32, (ATOMS, PROBES), 0).astype(F32)
    dists = []
    for source in range(SOURCES):
        pack = packs[source]
        if source > 0:
            which = source - 1
            ids = lax.broadcasted_iota(jnp.int32, (ATOMS, ATOMS), 0)
            owners = (ids == lists_ref[which : which + 1, :]).astype(BF16)
        for slot in range(SLOTS):
            start = source * SPAN + slot * PROBES
            picked = pack[slot, COMPS + 1 : COMPS + 2, :] - float(source * ATOMS)
            hot = (picked == sub).astype(F32)
            if source > 0:
                hot = matmul(owners, hot.astype(BF16))
            for m in range(COMPS):
                spread_ref[m * ATOMS : (m + 1) * ATOMS, start : start + PROBES] = (
                    hot * pack[slot, m : m + 1, :]
                ).astype(BF16)
            dists.append(pack[slot, COMPS : COMPS + 1, :])
    dist = jnp.concatenate(dists, axis=1)
    orders = lax.broadcasted_iota(jnp.int32, (BASES, PAIRS), 0).astype(F32) + 1.0
    phase = math.pi * dist / CUTOFF
    envelope = 0.5 * (jnp.cos(phase) + 1.0) / dist
    basis = jnp.sin(phase * orders) * envelope
    basis_ref[...] = basis
    total = None
    for degree in range(DEGREES):
        low, high = first_rows(degree)
        radial = along_first(w_radial_ref[:, lanes(degree)], basis, PRECISE)
        radial_ref[lanes(degree), :] = radial
        sums = along_first(rows_ref[low:high, :], spread_ref[low:high, :])
        sums_ref[lanes(degree), :] = sums
        term = radial * sums
        total = term if total is None else total + term
    for source in range(SOURCES):
        start = source * SPAN
        out_refs[source][...] = (
            total[:, start : start + PROBES] + total[:, start + PROBES : start + SPAN]
        )


def silu_slope(values):
    logistic = jax.nn.sigmoid(values)
    return logistic * (1.0 + values * (1.0 - logistic))


def columns_of(row):
    return jnp.broadcast_to(row, (CHANS, CHANS)).T


def readout_kernel(
    scale, weight, gathered_ref, target_ref, w_hidden_ref, b_hidden_ref, w_out_ref,
    density_ref, upstream_ref, head_ref,
):
    summed = gathered_ref[0]
    for shard in range(1, gathered_ref.shape[0]):
        summed = summed + gathered_ref[shard]
    w_hidden = w_hidden_ref[...]
    w_out = columns_of(w_out_ref[...])
    hidden_pre = along_first(w_hidden, summed, PRECISE) + columns_of(b_hidden_ref[...])
    activated = jax.nn.silu(hidden_pre)
    density = jnp.sum(activated * w_out, axis=0, keepdims=True)
    density_ref[...] = density
    error = density - target_ref[...]
    error_grad = error * scale
    pre_grad = w_out * silu_slope(hidden_pre) * error_grad
    upstream_ref[...] = matmul(w_hidden, pre_grad, PRECISE)
    head_ref[0:CHANS, :] = along_last(summed, pre_grad, PRECISE) * weight
    bias = jnp.sum(pre_grad.T, axis=0, keepdims=True) * weight
    out = jnp.sum((activated * error_grad).T, axis=0, keepdims=True) * weight
    loss = error * error * (0.5 * scale * weight)
    head_ref[CHANS : CHANS + 16, :] = jnp.concatenate(
        [bias, out, loss, jnp.zeros((13, CHANS), F32)], axis=0
    )


def backward_kernel(
    feats_ref, species_ref, w_deg_ref, w_gate_ref, spread_ref, sums_ref, radial_ref, basis_ref,
    head_ref, *refs,
):
    upstreams = refs[:SOURCES]
    payload_ref = refs[SOURCES]
    upstream = jnp.concatenate([ref[...] for ref in upstreams for slot in range(SLOTS)], axis=1)
    scalar = feats_ref[:, lanes(0)]
    gates = jax.nn.sigmoid(matmul(scalar, w_gate_ref[...]))
    radial_grads = []
    for degree in range(DEGREES):
        low, high = first_rows(degree)
        inner = (radial_ref[lanes(degree), :] * upstream).astype(BF16)
        grads = along_last(spread_ref[low:high, :], inner)
        radial_grads.append(
            along_last(basis_ref[...], sums_ref[lanes(degree), :] * upstream, PRECISE)
        )
        rows = component_rows(feats_ref, degree)
        mixed = matmul(rows, w_deg_ref[degree])
        if degree == 0:
            mixed_grad = grads * silu_slope(mixed)
            embed_grad = matmul(kind_rows(species_ref), grads, PRECISE)
        else:
            gate = gates[:, lanes(degree - 1)]
            mixed_grad = grads * over_components(gate, degree)
            product = grads * mixed
            total = product[0:ATOMS, :]
            for comp in range(1, 2 * degree + 1):
                total = total + product[comp * ATOMS : (comp + 1) * ATOMS, :]
            pre = (total * gate * (1.0 - gate)).astype(BF16)
            start = (DEGREES + degree - 1) * CHANS
            payload_ref[start : start + CHANS, :] = along_first(scalar, pre).astype(BF16)
        payload_ref[degree * CHANS : (degree + 1) * CHANS, :] = along_first(
            rows, mixed_grad.astype(BF16)
        ).astype(BF16)
    base = (2 * DEGREES - 1) * CHANS
    payload_ref[base : base + CHANS + 16, :] = head_ref[...].astype(BF16)
    base += CHANS + 16
    payload_ref[base : base + 48, :] = jnp.concatenate(
        radial_grads + [embed_grad], axis=0
    ).astype(BF16)
    base += 48
    payload_ref[base:, :] = jnp.zeros((PAYLOAD - base, CHANS), BF16)


def unpack_kernel(
    payload_ref, loss_ref, deg_ref, gate_ref, embed_ref, radial_ref, hidden_ref, bias_ref, out_ref
):
    for degree in range(DEGREES):
        deg_ref[degree] = payload_ref[lanes(degree), :].astype(F32)
    for degree in range(1, DEGREES):
        gate_ref[:, lanes(degree - 1)] = payload_ref[lanes(DEGREES + degree - 1), :].astype(F32)
    base = (2 * DEGREES - 1) * CHANS
    hidden_ref[...] = payload_ref[base : base + CHANS, :].astype(F32)
    base += CHANS
    misc = payload_ref[base : base + 16, :].astype(F32)
    bias_ref[...] = misc[0:1, :]
    out_ref[...] = misc[1:2, :]
    loss_ref[...] = jnp.sum(misc[2:3, :], axis=1, keepdims=True)
    base += 16
    small = payload_ref[base : base + 48, :].astype(F32)
    for degree in range(DEGREES):
        radial_ref[:, lanes(degree)] = small[degree * BASES : (degree + 1) * BASES, :]
    embed_ref[...] = small[DEGREES * BASES :, :]


def shape(dims, dtype=F32):
    return jax.ShapeDtypeStruct(dims, dtype)


def call(kernel, outs, name):
    return pl.pallas_call(
        kernel,
        out_shape=outs,
        name=name,
        compiler_params=pltpu.CompilerParams(vmem_limit_bytes=48 * 1024 * 1024),
    )


def passed_along(block, distance):
    count = lax.axis_size(SLAB)
    route = [(i, (i + distance) % count) for i in range(count)]
    return lax.ppermute(block, SLAB, route)


def to_all(block, axes):
    count = lax.axis_size(axes)
    return lax.all_to_all(jnp.broadcast_to(block[None], (count,) + block.shape), axes, 0, 0)


def sum_parts(parts):
    return jnp.sum(parts.astype(F32), axis=0).astype(BF16)


def reduce_all(payload):
    count = lax.axis_size(PLANE)
    parts = payload.reshape(count, PAYLOAD // count, CHANS)
    part = sum_parts(lax.all_to_all(parts, PLANE, 0, 0))
    part = sum_parts(to_all(part, ("z",)))
    return to_all(part, PLANE).reshape(PAYLOAD, CHANS)


def on_device(
    atom_feats, species, send_rows, neighbours, harmonics, distances, target,
    w_deg, w_gate, embed, w_radial, w_hidden, b_hidden, w_out,
):
    slab_count = lax.axis_size(SLAB)
    shard_count = lax.axis_size(ATOM)
    scale = 1.0 / math.sqrt(PROBES * slab_count)
    species = species.reshape(1, ATOMS)
    lists = send_rows[0, 0]
    with jax.named_scope("pack_pairs"):
        pack = jnp.concatenate(
            [
                harmonics.transpose(1, 0, 2),
                distances[:, None, :],
                neighbours.astype(F32)[:, None, :],
                jnp.zeros((SLOTS, FIELDS - COMPS - 2, PROBES), F32),
            ],
            axis=1,
        )
    with jax.named_scope("exchange_pairs"):
        packs = [pack] + [passed_along(pack, -offset) for offset in OFFSETS]
    rows = call(encode_kernel, shape((COMPS * ATOMS, CHANS), BF16), "encode")(
        atom_feats, species, w_deg, w_gate, embed
    )
    outs = call(
        pair_kernel,
        [shape((CHANS, PROBES))] * SOURCES
        + [
            shape((COMPS * ATOMS, PAIRS), BF16),
            shape((DEGREES * CHANS, PAIRS)),
            shape((DEGREES * CHANS, PAIRS)),
            shape((BASES, PAIRS)),
        ],
        "pair_sums",
    )(rows, lists, w_radial, *packs)
    values = outs[:SOURCES]
    spread, sums, radial, basis = outs[SOURCES:]
    with jax.named_scope("exchange_sums"):
        partial_value = values[0]
        for which, offset in enumerate(OFFSETS):
            partial_value = partial_value + passed_along(values[1 + which], offset)
    with jax.named_scope("gather_shards"):
        gathered = to_all(partial_value, ATOM)
    density, upstream, head = call(
        functools.partial(readout_kernel, scale, 1.0 / shard_count),
        [shape((1, PROBES)), shape((CHANS, PROBES)), shape((CHANS + 16, CHANS))],
        "readout",
    )(
        gathered, target.reshape(1, PROBES), w_hidden, b_hidden.reshape(1, CHANS),
        w_out.reshape(1, CHANS),
    )
    with jax.named_scope("exchange_grads"):
        upstreams = [upstream] + [passed_along(upstream, -offset) for offset in OFFSETS]
    payload = call(backward_kernel, shape((PAYLOAD, CHANS), BF16), "backward")(
        atom_feats, species, w_deg, w_gate, spread, sums, radial, basis, head, *upstreams
    )
    with jax.named_scope("reduce_grads"):
        payload = reduce_all(payload)
    loss, deg, gate, embed_grad, radial_grad, hidden, bias, out = call(
        unpack_kernel,
        [
            shape((1, 1)),
            shape((DEGREES, CHANS, CHANS)),
            shape((CHANS, (DEGREES - 1) * CHANS)),
            shape((KINDS, CHANS)),
            shape((BASES, DEGREES * CHANS)),
            shape((CHANS, CHANS)),
            shape((1, CHANS)),
            shape((1, CHANS)),
        ],
        "unpack",
    )(payload)
    return (
        loss.reshape(()), density.reshape(PROBES), deg, gate, embed_grad, radial_grad, hidden,
        bias.reshape(CHANS), out.reshape(CHANS),
    )


def solution(mesh):
    slabs, shards = mesh.devices.shape
    fine = Mesh(mesh.devices.reshape(slabs // 4, 4, shards // 2, 2), ("z", "y", "x", "c"))
    in_specs = (
        P(SLAB + ATOM, None),
        P(SLAB + ATOM),
        P(SLAB, ATOM, None, None),
        P(ATOM, SLAB),
        P(None, ATOM, SLAB),
        P(ATOM, SLAB),
        P(SLAB),
        P(),
        P(),
        P(),
        P(),
        P(),
        P(),
        P(),
    )
    out_specs = (P(), P(SLAB), P(), P(), P(), P(), P(), P(), P())
    return jax.shard_map(
        on_device, mesh=fine, in_specs=in_specs, out_specs=out_specs, check_vma=False
    )
```

time: 724 us -> 157 us (0.22)
  waiting for transfers between devices: 477 us -> 12.6 us
  blocking collectives: 120 us -> 69.5 us
  other arithmetic: 29.6 us -> 1.64 us
  local copies, waits for them, and re-layouts: 24.3 us -> 6.54 us
  matrix products: 17.1 us -> 0 us
  Pallas kernels: 0 us -> 16.3 us
  between operations: 16.3 us -> 0.92 us
  starting transfers between devices: 37.9 us -> 48.6 us
    psum x2 -> x0, waiting for transfers between devices: 428 us -> none  [the longest x1 359 us: on_device(): lax.psum((grad_deg, grad_gate, grad_embed, grad_radial, head_grads[0], he...]
    psum x1 -> x0, blocking collectives: 120 us -> none  [on_device(): lax.psum((grad_deg, grad_gate, grad_embed, grad_radial, head_grads[0], he...]
    all_to_all x0 -> x4, blocking collectives: none -> 69.5 us  [the longest x3 52.7 us: to_all(): lax.all_to_all(jnp.broadcast_to(block[None], (count,) + block.shape), axe...]
    ppermute x8 -> x12, waiting for transfers between devices: 49.8 us -> 12.6 us  [passed_along(): return lax.ppermute(block, SLAB, route)]
    scatter-add x5 -> x0, other arithmetic: 19.3 us -> none  [the longest x4 10.7 us: on_device(): atom_grad = atom_grad.at[lists[which]].add(back[which])]
    dot_general x21 -> x0, matrix products: 17.1 us -> none  [the longest x9 7.15 us: contract_rows(): lax.dot_general(left, right, (((0,), (0,)), ((), ())), preferred_element_...]
    pallas_call x0 -> x5, Pallas kernels: none -> 16.3 us  [the longest x1 7.75 us: on_device(): call(backward_kernel, shape((PAYLOAD, CHANS), BF16), 'backward')]
    ppermute x8 -> x12, starting transfers between devices: 37.6 us -> 48.6 us  [passed_along(): return lax.ppermute(block, SLAB, route)]
  transfers between devices with their start and end apart: 10 -> 12, of which waited for: 5 -> 5; matrix products, arithmetic and copies ran while one was open for 3% -> 0% of each run, Pallas kernels for 0% -> 0%
where the time goes in v1:
time: 157 us; the launch traced here: 156 us
  blocking collectives  69.5 us (44%)
  starting transfers between devices  48.6 us (31%)
  Pallas kernels  16.3 us (10%)
  waiting for transfers between devices  12.6 us (8%)
  local copies, waits for them, and re-layouts  6.54 us (4%)
  other arithmetic  1.64 us (1%)
    all_to_all x3, blocking collectives, to_all(): lax.all_to_all(jnp.broadcast_to(block[None], (count,) + block.shape), axe...  52.7 us
    ppermute x12, starting transfers between devices, passed_along(): return lax.ppermute(block, SLAB, route)  48.6 us
    all_to_all x1, blocking collectives, reduce_all(): part = sum_parts(lax.all_to_all(parts, PLANE, 0, 0))  16.8 us
    ppermute x12, waiting for transfers between devices, passed_along(): return lax.ppermute(block, SLAB, route)  12.6 us
    pallas_call x1, Pallas kernels, on_device(): call(backward_kernel, shape((PAYLOAD, CHANS), BF16), 'backward')  7.75 us
    pallas_call x1, Pallas kernels, on_device(): call(pair_kernel, [shape((CHANS, PROBES))] * SOURCES + [shape((COMPS * AT...  6.47 us
    unnamed x31, local copies, waits for them, and re-layouts  6.34 us
  transfers between devices with their start and end apart: 12, of which 5 were waited for; matrix products, arithmetic and copies ran while one was open for 0% of the time, Pallas kernels for 0%

profile of v1, /device:TPU:1, one launch (start us, length us, event | category | flops | bytes accessed | tf_op | source)
XLA Modules:
  0.0 156.0 jit_solution(4867910154816394692)
XLA Ops:
  0.7 0.8 convert_element_type.2
  1.5 0.7 copy.26
  2.3 0.8 maximum_maximum_fusion.refs_0_
  3.0 14.6 %collective-permute-start.3 = (f32[2,32,128]{2,1,0:T(8,128)S(1)}, f32[2,32,128]{2,1,0:T(8,128)S(1)}, u32[]{:S(2)}, u32[]{:S(2)}) collective-permute-start(f32[2,32,128]{2,1,0:T(8,128)S(1)} %maximum_maximum_fusion.refs_0_), channel_id=1, source_target_pairs={{0,496},{8,504},{16,0},{24,8},{32,16},{40,24},{48,32},{56,40},{64,... | collective-permute-start | bytes 98312 | tf_op jit(solution)/shard_map/exchange_pairs/ppermute | solution.py:250
  17.6 2.7 %collective-permute-start.2 = (f32[2,32,128]{2,1,0:T(8,128)S(1)}, f32[2,32,128]{2,1,0:T(8,128)S(1)}, u32[]{:S(2)}, u32[]{:S(2)}) collective-permute-start(f32[2,32,128]{2,1,0:T(8,128)S(1)} %maximum_maximum_fusion.refs_0_), channel_id=1, source_target_pairs={{0,504},{8,0},{16,8},{24,16},{32,24},{40,32},{48,40},{56,48},{64,5... | collective-permute-start | bytes 98312 | tf_op jit(solution)/shard_map/exchange_pairs/ppermute | solution.py:250
  20.3 2.6 %collective-permute-start.1 = (f32[2,32,128]{2,1,0:T(8,128)S(1)}, f32[2,32,128]{2,1,0:T(8,128)S(1)}, u32[]{:S(2)}, u32[]{:S(2)}) collective-permute-start(f32[2,32,128]{2,1,0:T(8,128)S(1)} %maximum_maximum_fusion.refs_0_), channel_id=1, source_target_pairs={{0,8},{8,16},{16,24},{24,32},{32,40},{40,48},{48,56},{56,64},{64,7... | collective-permute-start | bytes 98312 | tf_op jit(solution)/shard_map/exchange_pairs/ppermute | solution.py:250
  22.9 2.6 %collective-permute-start = (f32[2,32,128]{2,1,0:T(8,128)S(1)}, f32[2,32,128]{2,1,0:T(8,128)S(1)}, u32[]{:S(2)}, u32[]{:S(2)}) collective-permute-start(f32[2,32,128]{2,1,0:T(8,128)S(1)} %maximum_maximum_fusion.refs_0_), channel_id=1, source_target_pairs={{0,16},{8,24},{16,32},{24,40},{32,48},{40,56},{48,64},{56,72},{64,... | collective-permute-start | bytes 98312 | tf_op jit(solution)/shard_map/exchange_pairs/ppermute | solution.py:250
  25.6 1.0 copy-done
  26.6 0.9 copy-done.2
  27.5 0.9 copy-done.4
  30.1 1.1 collective-permute-done.refs_1_
  31.2 0.7 copy-done.7
  32.6 6.5 %pair_sums.1 = (f32[128,128]{1,0:T(8,128)S(1)}, f32[128,128]{1,0:T(8,128)S(1)}, f32[128,128]{1,0:T(8,128)S(1)}, f32[128,128]{1,0:T(8,128)S(1)}, f32[128,128]{1,0...) custom-call(bf16[1600,128]{1,0:T(8,128)(2,1)S(1)} %encode.1.rows_ref, ...), custom_call_target="tpu_custom_call" | custom-call | tf_op jit(solution)/shard_map/pair_sums/pallas_call | solution.py:294
  39.1 5.2 %collective-permute-start.4 = (f32[128,128]{1,0:T(8,128)S(1)}, f32[128,128]{1,0:T(8,128)S(1)}, u32[]{:S(2)}, u32[]{:S(2)}) collective-permute-start(f32[128,128]{1,0:T(8,128)S(1)} %get-tuple-element.34), channel_id=1, source_target_pairs={{0,496},{8,504},{16,0},{24,8},{32,16},{40,24},{48,32},{56,40},{64,... | collective-permute-start | bytes 196616 | tf_op jit(solution)/shard_map/exchange_sums/ppermute | solution.py:250
  44.3 3.9 %collective-permute-start.5 = (f32[128,128]{1,0:T(8,128)S(1)}, f32[128,128]{1,0:T(8,128)S(1)}, u32[]{:S(2)}, u32[]{:S(2)}) collective-permute-start(f32[128,128]{1,0:T(8,128)S(1)} %get-tuple-element.35), channel_id=1, source_target_pairs={{0,504},{8,0},{16,8},{24,16},{32,24},{40,32},{48,40},{56,48},{64,5... | collective-permute-start | bytes 196616 | tf_op jit(solution)/shard_map/exchange_sums/ppermute | solution.py:250
  48.2 1.9 %collective-permute-start.6 = (f32[128,128]{1,0:T(8,128)S(1)}, f32[128,128]{1,0:T(8,128)S(1)}, u32[]{:S(2)}, u32[]{:S(2)}) collective-permute-start(f32[128,128]{1,0:T(8,128)S(1)} %get-tuple-element.36), channel_id=1, source_target_pairs={{0,8},{8,16},{16,24},{24,32},{32,40},{40,48},{48,56},{56,64},{64,7... | collective-permute-start | bytes 196616 | tf_op jit(solution)/shard_map/exchange_sums/ppermute | solution.py:250
  50.1 2.1 %collective-permute-start.7 = (f32[128,128]{1,0:T(8,128)S(1)}, f32[128,128]{1,0:T(8,128)S(1)}, u32[]{:S(2)}, u32[]{:S(2)}) collective-permute-start(f32[128,128]{1,0:T(8,128)S(1)} %get-tuple-element.37), channel_id=1, source_target_pairs={{0,16},{8,24},{16,32},{24,40},{32,48},{40,56},{48,64},{56,72},{64,... | collective-permute-start | bytes 196616 | tf_op jit(solution)/shard_map/exchange_sums/ppermute | solution.py:250
  52.2 4.3 %collective-permute-done.6 = f32[128,128]{1,0:T(8,128)S(1)} collective-permute-done((f32[128,128]{1,0:T(8,128)S(1)}, f32[128,128]{1,0:T(8,128)S(1)}, u32[]{:S(2)}, u32[]{:S(2)}) %collective-permute-start.6) | collective-permute-done | bytes 65568 | tf_op jit(solution)/shard_map/exchange_sums/ppermute | solution.py:250
  56.5 2.3 %collective-permute-done.7 = f32[128,128]{1,0:T(8,128)S(1)} collective-permute-done((f32[128,128]{1,0:T(8,128)S(1)}, f32[128,128]{1,0:T(8,128)S(1)}, u32[]{:S(2)}, u32[]{:S(2)}) %collective-permute-start.7) | collective-permute-done | bytes 65568 | tf_op jit(solution)/shard_map/exchange_sums/ppermute | solution.py:250
  58.9 16.9 %all_to_all.20.gathered_ref = f32[8,128,128]{2,1,0:T(8,128)S(1)} all-to-all(f32[8,128,128]{2,1,0:T(8,128)S(1)} %broadcast_in_dim.30), channel_id=1, replica_groups=mesh['z'=16,'y'=4,'x'=4,'c'=2] {'x','c'}, dimensions={0} | all-to-all | bytes 1048576 | tf_op jit(solution)/shard_map/gather_shards/all_to_all | solution.py:255
  75.8 0.8 readout.1
  76.6 1.9 %collective-permute-start.11 = (f32[128,128]{1,0:T(8,128)S(1)}, f32[128,128]{1,0:T(8,128)S(1)}, u32[]{:S(2)}, u32[]{:S(2)}) collective-permute-start(f32[128,128]{1,0:T(8,128)S(1)} %get-tuple-element.39.refs_0_), channel_id=1, source_target_pairs={{0,496},{8,504},{16,0},{24,8},{32,16},{40,24},{48,32},{56,40},{64,... | collective-permute-start | bytes 196616 | tf_op jit(solution)/shard_map/exchange_grads/ppermute | solution.py:250
  78.5 4.9 %collective-permute-start.10 = (f32[128,128]{1,0:T(8,128)S(1)}, f32[128,128]{1,0:T(8,128)S(1)}, u32[]{:S(2)}, u32[]{:S(2)}) collective-permute-start(f32[128,128]{1,0:T(8,128)S(1)} %get-tuple-element.39.refs_0_), channel_id=1, source_target_pairs={{0,504},{8,0},{16,8},{24,16},{32,24},{40,32},{48,40},{56,48},{64,5... | collective-permute-start | bytes 196616 | tf_op jit(solution)/shard_map/exchange_grads/ppermute | solution.py:250
  83.4 2.5 %collective-permute-start.9 = (f32[128,128]{1,0:T(8,128)S(1)}, f32[128,128]{1,0:T(8,128)S(1)}, u32[]{:S(2)}, u32[]{:S(2)}) collective-permute-start(f32[128,128]{1,0:T(8,128)S(1)} %get-tuple-element.39.refs_0_), channel_id=1, source_target_pairs={{0,8},{8,16},{16,24},{24,32},{32,40},{40,48},{48,56},{56,64},{64,7... | collective-permute-start | bytes 196616 | tf_op jit(solution)/shard_map/exchange_grads/ppermute | solution.py:250
  85.9 3.7 %collective-permute-start.8 = (f32[128,128]{1,0:T(8,128)S(1)}, f32[128,128]{1,0:T(8,128)S(1)}, u32[]{:S(2)}, u32[]{:S(2)}) collective-permute-start(f32[128,128]{1,0:T(8,128)S(1)} %get-tuple-element.39.refs_0_), channel_id=1, source_target_pairs={{0,16},{8,24},{16,32},{24,40},{32,48},{40,56},{48,64},{56,72},{64,... | collective-permute-start | bytes 196616 | tf_op jit(solution)/shard_map/exchange_grads/ppermute | solution.py:250
  89.6 2.1 %collective-permute-done.9.refs_2_ = f32[128,128]{1,0:T(8,128)S(1)} collective-permute-done((f32[128,128]{1,0:T(8,128)S(1)}, f32[128,128]{1,0:T(8,128)S(1)}, u32[]{:S(2)}, u32[]{:S(2)}) %collective-permute-start.9) | collective-permute-done | bytes 65568 | tf_op jit(solution)/shard_map/exchange_grads/ppermute | solution.py:250
  91.7 2.8 %collective-permute-done.8.refs_1_ = f32[128,128]{1,0:T(8,128)S(1)} collective-permute-done((f32[128,128]{1,0:T(8,128)S(1)}, f32[128,128]{1,0:T(8,128)S(1)}, u32[]{:S(2)}, u32[]{:S(2)}) %collective-permute-start.8) | collective-permute-done | bytes 65568 | tf_op jit(solution)/shard_map/exchange_grads/ppermute | solution.py:250
  94.5 7.7 %backward.1 = bf16[1536,128]{1,0:T(8,128)(2,1)S(1)} custom-call(bf16[64,3200]{1,0:T(8,128)(2,1)S(1)} %copy-done.1, s32[1,64]{1,0:T(1,128)S(1)} %bitcast.20, bf16[5,128,128]{2,1,0:T(8,128)(2,1)S(1)} %copy-done.3, bf16[128,512]{1,0:T(8,128)(2,1)S(1)} %copy-done.5, bf16[1600,1280]{1,0:T(8,128)(2,1)} %get-tuple-element.29.spread_ref, ...), custom_call_target="tpu_custom_call" | custom-call | tf_op jit(solution)/shard_map/backward/pallas_call | solution.py:323
  102.3 16.8 %all_to_all.21 = bf16[32,48,128]{2,1,0:T(8,128)(2,1)S(1)} all-to-all(bf16[32,48,128]{2,1,0:T(8,128)(2,1)S(1)} %bitcast.16), channel_id=1, replica_groups=mesh['z'=16,'y'=4,'x'=4,'c'=2] {'y','x','c'}, dimensions={0} | all-to-all | bytes 786432 | tf_op jit(solution)/shard_map/reduce_grads/all_to_all | solution.py:265
  119.1 18.2 %all_to_all.22 = bf16[16,48,128]{2,1,0:T(8,128)(2,1)S(1)} all-to-all(bf16[16,48,128]{2,1,0:T(8,128)(2,1)S(1)} %broadcast_in_dim.31), channel_id=1, replica_groups=mesh['z'=16,'y'=4,'x'=4,'c'=2] {'z'}, dimensions={0} | all-to-all | bytes 393216 | tf_op jit(solution)/shard_map/reduce_grads/all_to_all | solution.py:255
  137.5 17.6 %all_to_all.23 = bf16[32,48,128]{2,1,0:T(8,128)(2,1)S(1)} all-to-all(bf16[32,48,128]{2,1,0:T(8,128)(2,1)S(1)} %broadcast_in_dim.32), channel_id=1, replica_groups=mesh['z'=16,'y'=4,'x'=4,'c'=2] {'y','x','c'}, dimensions={0} | all-to-all | bytes 786432 | tf_op jit(solution)/shard_map/reduce_grads/all_to_all | solution.py:255
  155.1 0.9 unpack.1
  (42 shorter events, 2.8 us)
Async XLA Ops:
  0.6 93.9 %copy-start.5 = (bf16[128,512]{1,0:T(8,128)(2,1)S(1)}, bf16[128,512]{1,0:T(8,128)(2,1)}, u32[]{:S(2)}) copy-start(bf16[128,512]{1,0:T(8,128)(2,1)} %w_gate_ref.3) | copy-start | bytes 393220
  0.7 93.9 %copy-start.11 = (s32[64]{0:T(128)S(1)}, s32[64]{0:T(128)}, u32[]{:S(2)}) copy-start(s32[64]{0:T(128)} %param.15) | copy-start | bytes 772
  0.7 75.1 %copy-start.14 = (f32[128]{0:T(128)S(1)}, f32[128]{0:T(128)}, u32[]{:S(2)}) copy-start(f32[128]{0:T(128)} %param.27) | copy-start | bytes 1540
  0.7 75.1 %copy-start.13 = (f32[128]{0:T(128)S(1)}, f32[128]{0:T(128)}, u32[]{:S(2)}) copy-start(f32[128]{0:T(128)} %param.26) | copy-start | bytes 1540
  0.7 75.1 %copy-start.12 = (f32[128]{0:T(128)S(1)}, f32[128]{0:T(128)}, u32[]{:S(2)}) copy-start(f32[128]{0:T(128)} %param.20) | copy-start | bytes 1540
  3.0 27.1 %collective-permute-start.3 = (f32[2,32,128]{2,1,0:T(8,128)S(1)}, f32[2,32,128]{2,1,0:T(8,128)S(1)}, u32[]{:S(2)}, u32[]{:S(2)}) collective-permute-start(f32[2,32,128]{2,1,0:T(8,128)S(1)} %maximum_maximum_fusion.refs_0_), channel_id=1, source_target_pairs={{0,496},{8,504},{16,0},{24,8},{32,16},{40,24},{48,32},{56,40},{64,... | collective-permute-start | bytes 98312 | tf_op jit(solution)/shard_map/exchange_pairs/ppermute | solution.py:250
  17.6 12.5 %collective-permute-start.2 = (f32[2,32,128]{2,1,0:T(8,128)S(1)}, f32[2,32,128]{2,1,0:T(8,128)S(1)}, u32[]{:S(2)}, u32[]{:S(2)}) collective-permute-start(f32[2,32,128]{2,1,0:T(8,128)S(1)} %maximum_maximum_fusion.refs_0_), channel_id=1, source_target_pairs={{0,504},{8,0},{16,8},{24,16},{32,24},{40,32},{48,40},{56,48},{64,5... | collective-permute-start | bytes 98312 | tf_op jit(solution)/shard_map/exchange_pairs/ppermute | solution.py:250
  20.3 9.8 %collective-permute-start.1 = (f32[2,32,128]{2,1,0:T(8,128)S(1)}, f32[2,32,128]{2,1,0:T(8,128)S(1)}, u32[]{:S(2)}, u32[]{:S(2)}) collective-permute-start(f32[2,32,128]{2,1,0:T(8,128)S(1)} %maximum_maximum_fusion.refs_0_), channel_id=1, source_target_pairs={{0,8},{8,16},{16,24},{24,32},{32,40},{40,48},{48,56},{56,64},{64,7... | collective-permute-start | bytes 98312 | tf_op jit(solution)/shard_map/exchange_pairs/ppermute | solution.py:250
  22.9 8.3 %collective-permute-start = (f32[2,32,128]{2,1,0:T(8,128)S(1)}, f32[2,32,128]{2,1,0:T(8,128)S(1)}, u32[]{:S(2)}, u32[]{:S(2)}) collective-permute-start(f32[2,32,128]{2,1,0:T(8,128)S(1)} %maximum_maximum_fusion.refs_0_), channel_id=1, source_target_pairs={{0,16},{8,24},{16,32},{24,40},{32,48},{40,56},{48,64},{56,72},{64,... | collective-permute-start | bytes 98312 | tf_op jit(solution)/shard_map/exchange_pairs/ppermute | solution.py:250
  25.6 1.0 copy-start
  26.6 0.9 copy-start.2
  27.5 0.9 copy-start.4
  28.4 0.7 copy-start.8
  29.1 0.7 copy-start.10
  29.7 46.0 %copy-start.6 = (f32[128,128]{1,0:T(8,128)S(1)}, f32[128,128]{1,0:T(8,128)}, u32[]{:S(2)}) copy-start(f32[128,128]{1,0:T(8,128)} %w_hidden_ref.1) | copy-start | bytes 196612
  29.7 64.8 %copy-start.1 = (bf16[64,3200]{1,0:T(8,128)(2,1)S(1)}, bf16[64,3200]{1,0:T(8,128)(2,1)}, u32[]{:S(2)}) copy-start(bf16[64,3200]{1,0:T(8,128)(2,1)} %feats_ref.3) | copy-start | bytes 1228804
  29.7 64.8 %copy-start.3 = (bf16[5,128,128]{2,1,0:T(8,128)(2,1)S(1)}, bf16[5,128,128]{2,1,0:T(8,128)(2,1)}, u32[]{:S(2)}) copy-start(bf16[5,128,128]{2,1,0:T(8,128)(2,1)} %w_deg_ref.3) | copy-start | bytes 491524
  31.2 0.7 copy-start.7
  31.9 0.7 copy-start.9
  39.1 13.2 %collective-permute-start.4 = (f32[128,128]{1,0:T(8,128)S(1)}, f32[128,128]{1,0:T(8,128)S(1)}, u32[]{:S(2)}, u32[]{:S(2)}) collective-permute-start(f32[128,128]{1,0:T(8,128)S(1)} %get-tuple-element.34), channel_id=1, source_target_pairs={{0,496},{8,504},{16,0},{24,8},{32,16},{40,24},{48,32},{56,40},{64,... | collective-permute-start | bytes 196616 | tf_op jit(solution)/shard_map/exchange_sums/ppermute | solution.py:250
  44.3 8.0 %collective-permute-start.5 = (f32[128,128]{1,0:T(8,128)S(1)}, f32[128,128]{1,0:T(8,128)S(1)}, u32[]{:S(2)}, u32[]{:S(2)}) collective-permute-start(f32[128,128]{1,0:T(8,128)S(1)} %get-tuple-element.35), channel_id=1, source_target_pairs={{0,504},{8,0},{16,8},{24,16},{32,24},{40,32},{48,40},{56,48},{64,5... | collective-permute-start | bytes 196616 | tf_op jit(solution)/shard_map/exchange_sums/ppermute | solution.py:250
  48.2 8.3 %collective-permute-start.6 = (f32[128,128]{1,0:T(8,128)S(1)}, f32[128,128]{1,0:T(8,128)S(1)}, u32[]{:S(2)}, u32[]{:S(2)}) collective-permute-start(f32[128,128]{1,0:T(8,128)S(1)} %get-tuple-element.36), channel_id=1, source_target_pairs={{0,8},{8,16},{16,24},{24,32},{32,40},{40,48},{48,56},{56,64},{64,7... | collective-permute-start | bytes 196616 | tf_op jit(solution)/shard_map/exchange_sums/ppermute | solution.py:250
  50.1 8.7 %collective-permute-start.7 = (f32[128,128]{1,0:T(8,128)S(1)}, f32[128,128]{1,0:T(8,128)S(1)}, u32[]{:S(2)}, u32[]{:S(2)}) collective-permute-start(f32[128,128]{1,0:T(8,128)S(1)} %get-tuple-element.37), channel_id=1, source_target_pairs={{0,16},{8,24},{16,32},{24,40},{32,48},{40,56},{48,64},{56,72},{64,... | collective-permute-start | bytes 196616 | tf_op jit(solution)/shard_map/exchange_sums/ppermute | solution.py:250
  76.6 13.0 %collective-permute-start.11 = (f32[128,128]{1,0:T(8,128)S(1)}, f32[128,128]{1,0:T(8,128)S(1)}, u32[]{:S(2)}, u32[]{:S(2)}) collective-permute-start(f32[128,128]{1,0:T(8,128)S(1)} %get-tuple-element.39.refs_0_), channel_id=1, source_target_pairs={{0,496},{8,504},{16,0},{24,8},{32,16},{40,24},{48,32},{56,40},{64,... | collective-permute-start | bytes 196616 | tf_op jit(solution)/shard_map/exchange_grads/ppermute | solution.py:250
  78.5 11.1 %collective-permute-start.10 = (f32[128,128]{1,0:T(8,128)S(1)}, f32[128,128]{1,0:T(8,128)S(1)}, u32[]{:S(2)}, u32[]{:S(2)}) collective-permute-start(f32[128,128]{1,0:T(8,128)S(1)} %get-tuple-element.39.refs_0_), channel_id=1, source_target_pairs={{0,504},{8,0},{16,8},{24,16},{32,24},{40,32},{48,40},{56,48},{64,5... | collective-permute-start | bytes 196616 | tf_op jit(solution)/shard_map/exchange_grads/ppermute | solution.py:250
  83.4 8.3 %collective-permute-start.9 = (f32[128,128]{1,0:T(8,128)S(1)}, f32[128,128]{1,0:T(8,128)S(1)}, u32[]{:S(2)}, u32[]{:S(2)}) collective-permute-start(f32[128,128]{1,0:T(8,128)S(1)} %get-tuple-element.39.refs_0_), channel_id=1, source_target_pairs={{0,8},{8,16},{16,24},{24,32},{32,40},{40,48},{48,56},{56,64},{64,7... | collective-permute-start | bytes 196616 | tf_op jit(solution)/shard_map/exchange_grads/ppermute | solution.py:250
  85.9 8.6 %collective-permute-start.8 = (f32[128,128]{1,0:T(8,128)S(1)}, f32[128,128]{1,0:T(8,128)S(1)}, u32[]{:S(2)}, u32[]{:S(2)}) collective-permute-start(f32[128,128]{1,0:T(8,128)S(1)} %get-tuple-element.39.refs_0_), channel_id=1, source_target_pairs={{0,16},{8,24},{16,32},{24,40},{32,48},{40,56},{48,64},{56,72},{64,... | collective-permute-start | bytes 196616 | tf_op jit(solution)/shard_map/exchange_grads/ppermute | solution.py:250

commit v2 on v1

--- a/solution.py
+++ b/solution.py
@@ -22,7 +22,8 @@
 ATOMS = 64
 SLOTS = 2
 PROBES = 128
-SOURCES = 1 + len(OFFSETS)
+DELTAS = (0,) + OFFSETS
+SOURCES = len(DELTAS)
 SPAN = SLOTS * PROBES
 PAIRS = SOURCES * SPAN
 FIELDS = 32
@@ -69,7 +70,24 @@
     return (ids == species_ref[...]).astype(F32)
 
 
-def encode_kernel(feats_ref, species_ref, w_deg_ref, w_gate_ref, embed_ref, rows_ref):
+def encode_kernel(
+    feats_hbm, species_ref, w_deg_hbm, w_gate_hbm, embed_ref, lists_ref, w_radial_ref,
+    rows_ref, owners_ref, split_ref, feats_ref, w_deg_ref, w_gate_ref, sems,
+):
+    copies = [
+        pltpu.make_async_copy(source, target, sems.at[index])
+        for index, (source, target) in enumerate(
+            ((w_gate_hbm, w_gate_ref), (feats_hbm, feats_ref), (w_deg_hbm, w_deg_ref))
+        )
+    ]
+    for copy in copies:
+        copy.start()
+    ids = lax.broadcasted_iota(jnp.int32, (ATOMS, ATOMS), 0)
+    for which in range(len(OFFSETS)):
+        owners_ref[which] = (ids == lists_ref[which : which + 1, :]).astype(BF16)
+    split_ref[...] = stacked(w_radial_ref[...], (0, 0, 1, 1, 0, 2))
+    for copy in copies:
+        copy.wait()
     scalar = feats_ref[:, lanes(0)]
     gates = jax.nn.sigmoid(matmul(scalar, w_gate_ref[...]))
     for degree in range(DEGREES):
@@ -85,49 +103,81 @@
         rows_ref[low:high, :] = (rows.astype(F32) + added).astype(BF16)
 
 
-def pair_kernel(rows_ref, lists_ref, w_radial_ref, *refs):
-    packs = refs[:SOURCES]
-    out_refs = refs[SOURCES : 2 * SOURCES]
-    spread_ref, sums_ref, radial_ref, basis_ref = refs[2 * SOURCES :]
+def parts_of(values):
+    high = values.astype(BF16)
+    rest = values - high.astype(F32)
+    middle = rest.astype(BF16)
+    low = (rest - middle.astype(F32)).astype(BF16)
+    return high, middle, low
+
+
+def stacked(values, order):
+    parts = [part.astype(F32) for part in parts_of(values)]
+    return jnp.concatenate([parts[index] for index in order], axis=0).astype(BF16)
+
+
+def plane_place(delta):
+    row = lax.axis_index("y") + delta
+    below, above = row < 0, row > 3
+    place = jnp.where(below, row + 2, jnp.where(above, row - 2, row))
+    return place, jnp.where(jnp.logical_or(below, above), 1, 0)
+
+
+def pack_kernel(harm_ref, dist_ref, nbr_ref, target_ref, pack_ref):
+    pack_ref[0:COMPS] = harm_ref[...]
+    pack_ref[COMPS] = dist_ref[...]
+    pack_ref[COMPS + 1] = nbr_ref[...].astype(F32)
+    pack_ref[COMPS + 2] = jnp.broadcast_to(target_ref[...], (SLOTS, PROBES))
+    pack_ref[COMPS + 3 :] = jnp.zeros((FIELDS - COMPS - 3, SLOTS, PROBES), F32)
+
+
+def pair_kernel(
+    packs_ref, rows_ref, owners_ref, split_ref,
+    out_ref, spread_ref, sums_ref, radial_ref, basis_ref,
+):
+    shards, chunk = out_ref.shape[1], out_ref.shape[3]
     sub = lax.broadcasted_iota(jnp.int32, (ATOMS, PROBES), 0).astype(F32)
-    dists = []
+    dists, places = [], []
     for source in range(SOURCES):
-        pack = packs[source]
-        if source > 0:
-            which = source - 1
-            ids = lax.broadcasted_iota(jnp.int32, (ATOMS, ATOMS), 0)
-            owners = (ids == lists_ref[which : which + 1, :]).astype(BF16)
+        place, part = plane_place(DELTAS[source])
+        places.append((place, part))
         for slot in range(SLOTS):
             start = source * SPAN + slot * PROBES
-            picked = pack[slot, COMPS + 1 : COMPS + 2, :] - float(source * ATOMS)
-            hot = (picked == sub).astype(F32)
+
+            def row(field):
+                return packs_ref[place, part, field, slot : slot + 1, :]
+
+            hot = (row(COMPS + 1) - float(source * ATOMS) == sub).astype(F32)
             if source > 0:
-                hot = matmul(owners, hot.astype(BF16))
+                hot = matmul(owners_ref[source - 1], hot.astype(BF16))
             for m in range(COMPS):
                 spread_ref[m * ATOMS : (m + 1) * ATOMS, start : start + PROBES] = (
-                    hot * pack[slot, m : m + 1, :]
+                    hot * row(m)
                 ).astype(BF16)
-            dists.append(pack[slot, COMPS : COMPS + 1, :])
+            dists.append(row(COMPS))
     dist = jnp.concatenate(dists, axis=1)
     orders = lax.broadcasted_iota(jnp.int32, (BASES, PAIRS), 0).astype(F32) + 1.0
     phase = math.pi * dist / CUTOFF
     envelope = 0.5 * (jnp.cos(phase) + 1.0) / dist
     basis = jnp.sin(phase * orders) * envelope
     basis_ref[...] = basis
+    basis_split = stacked(basis, (0, 1, 0, 1, 2, 0))
     total = None
     for degree in range(DEGREES):
         low, high = first_rows(degree)
-        radial = along_first(w_radial_ref[:, lanes(degree)], basis, PRECISE)
+        radial = along_first(split_ref[:, lanes(degree)], basis_split)
         radial_ref[lanes(degree), :] = radial
         sums = along_first(rows_ref[low:high, :], spread_ref[low:high, :])
         sums_ref[lanes(degree), :] = sums
         term = radial * sums
         total = term if total is None else total + term
+    out_ref[...] = jnp.zeros(out_ref.shape, F32)
     for source in range(SOURCES):
         start = source * SPAN
-        out_refs[source][...] = (
-            total[:, start : start + PROBES] + total[:, start + PROBES : start + SPAN]
-        )
+        value = (total[:, start : start + PROBES] + total[:, start + PROBES : start + SPAN]).T
+        place, part = places[source]
+        for shard in range(shards):
+            out_ref[place, shard, part] = value[shard * chunk : (shard + 1) * chunk, :]
 
 
 def silu_slope(values):
@@ -135,31 +185,50 @@
     return logistic * (1.0 + values * (1.0 - logistic))
 
 
-def columns_of(row):
-    return jnp.broadcast_to(row, (CHANS, CHANS)).T
+def sum_kernel(parts_ref, out_ref):
+    total = parts_ref[0].astype(F32)
+    for index in range(1, parts_ref.shape[0]):
+        total = total + parts_ref[index].astype(F32)
+    if len(out_ref.shape) == len(parts_ref.shape):
+        for copy in range(out_ref.shape[0]):
+            out_ref[copy] = total.astype(out_ref.dtype)
+    else:
+        out_ref[...] = total.astype(out_ref.dtype)
 
 
 def readout_kernel(
-    scale, weight, gathered_ref, target_ref, w_hidden_ref, b_hidden_ref, w_out_ref,
-    density_ref, upstream_ref, head_ref,
-):
-    summed = gathered_ref[0]
-    for shard in range(1, gathered_ref.shape[0]):
-        summed = summed + gathered_ref[shard]
+    scale, mine_ref, theirs_ref, pack_ref, their_pack_ref, w_hidden_ref, b_hidden_ref, w_out_ref,
+    up_ref, head_ref, column_ref,
+):
+    chunk = mine_ref.shape[1]
+    shard = lax.axis_index("x") * lax.axis_size("c") + lax.axis_index("c")
+    start = pl.multiple_of(shard * chunk, chunk)
+    summed = jnp.concatenate(
+        [mine_ref[0] + theirs_ref[1], theirs_ref[0] + mine_ref[1]], axis=0
+    )
+    targets = []
+    for ref in (pack_ref, their_pack_ref):
+        column_ref[...] = jnp.broadcast_to(ref[COMPS + 2, 0:1, :], (PROBES, PROBES)).T
+        targets.append(column_ref[pl.ds(start, chunk), :])
+    target = jnp.concatenate(targets, axis=0)
     w_hidden = w_hidden_ref[...]
-    w_out = columns_of(w_out_ref[...])
-    hidden_pre = along_first(w_hidden, summed, PRECISE) + columns_of(b_hidden_ref[...])
+    w_out = w_out_ref[...]
+    hidden_pre = matmul(summed, w_hidden, PRECISE) + b_hidden_ref[...]
     activated = jax.nn.silu(hidden_pre)
-    density = jnp.sum(activated * w_out, axis=0, keepdims=True)
-    density_ref[...] = density
-    error = density - target_ref[...]
+    density = jnp.sum(activated * w_out, axis=1, keepdims=True)
+    error = density - target
     error_grad = error * scale
     pre_grad = w_out * silu_slope(hidden_pre) * error_grad
-    upstream_ref[...] = matmul(w_hidden, pre_grad, PRECISE)
-    head_ref[0:CHANS, :] = along_last(summed, pre_grad, PRECISE) * weight
-    bias = jnp.sum(pre_grad.T, axis=0, keepdims=True) * weight
-    out = jnp.sum((activated * error_grad).T, axis=0, keepdims=True) * weight
-    loss = error * error * (0.5 * scale * weight)
+    spot = lax.broadcasted_iota(jnp.int32, (chunk, PROBES), 0) + start
+    mask = (spot == lax.broadcasted_iota(jnp.int32, (chunk, PROBES), 1)).astype(F32)
+    up_ref[0 : 2 * chunk, :] = along_last(pre_grad, w_hidden, PRECISE)
+    density_row = jnp.sum(mask * density[0:chunk, :], axis=0, keepdims=True)
+    up_ref[2 * chunk :, :] = jnp.broadcast_to(density_row, (8, PROBES))
+    mine, own_error = pre_grad[0:chunk, :], error[0:chunk, :]
+    head_ref[0:CHANS, :] = along_first(summed[0:chunk, :], mine, PRECISE)
+    bias = jnp.sum(mine, axis=0, keepdims=True)
+    out = jnp.sum(activated[0:chunk, :] * error_grad[0:chunk, :], axis=0, keepdims=True)
+    loss = jnp.sum(mask * own_error * own_error * (0.5 * scale), axis=0, keepdims=True)
     head_ref[CHANS : CHANS + 16, :] = jnp.concatenate(
         [bias, out, loss, jnp.zeros((13, CHANS), F32)], axis=0
     )
@@ -167,21 +236,37 @@
 
 def backward_kernel(
     feats_ref, species_ref, w_deg_ref, w_gate_ref, spread_ref, sums_ref, radial_ref, basis_ref,
-    head_ref, *refs,
-):
-    upstreams = refs[:SOURCES]
-    payload_ref = refs[SOURCES]
-    upstream = jnp.concatenate([ref[...] for ref in upstreams for slot in range(SLOTS)], axis=1)
+    head_ref, up_ref, payload_ref, density_ref,
+):
+    shards = up_ref.shape[1]
+    chunk = PROBES // shards
+    blocks = []
+    for delta in DELTAS:
+        place, part = plane_place(delta)
+        begin = pl.multiple_of(part * chunk, chunk)
+        block = jnp.concatenate(
+            [up_ref[place, shard, pl.ds(begin, chunk), :] for shard in range(shards)], axis=0
+        ).T
+        blocks += [block] * SLOTS
+    upstream = jnp.concatenate(blocks, axis=1)
+    density = None
+    for shard in range(shards):
+        row = up_ref[lax.axis_index("y"), shard, 2 * chunk : 2 * chunk + 1, :]
+        density = row if density is None else density + row
+    density_ref[...] = density
     scalar = feats_ref[:, lanes(0)]
     gates = jax.nn.sigmoid(matmul(scalar, w_gate_ref[...]))
+    basis_split = stacked(basis_ref[...], (0, 1))
     radial_grads = []
     for degree in range(DEGREES):
         low, high = first_rows(degree)
         inner = (radial_ref[lanes(degree), :] * upstream).astype(BF16)
         grads = along_last(spread_ref[low:high, :], inner)
-        radial_grads.append(
-            along_last(basis_ref[...], sums_ref[lanes(degree), :] * upstream, PRECISE)
-        )
+        product = sums_ref[lanes(degree), :] * upstream
+        main = product.astype(BF16)
+        rest = (product - main.astype(F32)).astype(BF16)
+        both = along_last(main, basis_split) + along_last(rest, basis_split)
+        radial_grads.append((both[:, 0:BASES] + both[:, BASES : 2 * BASES]).T)
         rows = component_rows(feats_ref, degree)
         mixed = matmul(rows, w_deg_ref[degree])
         if degree == 0:
@@ -235,18 +320,19 @@
     return jax.ShapeDtypeStruct(dims, dtype)
 
 
-def call(kernel, outs, name):
+def call(kernel, outs, name, **options):
     return pl.pallas_call(
         kernel,
         out_shape=outs,
         name=name,
         compiler_params=pltpu.CompilerParams(vmem_limit_bytes=48 * 1024 * 1024),
-    )
-
-
-def passed_along(block, distance):
+        **options,
+    )
+
+
+def to_partner(block):
     count = lax.axis_size(SLAB)
-    route = [(i, (i + distance) % count) for i in range(count)]
+    route = [(i, (i + (2 if i % 4 >= 2 else -2)) % count) for i in range(count)]
     return lax.ppermute(block, SLAB, route)
 
 
@@ -255,16 +341,15 @@
     return lax.all_to_all(jnp.broadcast_to(block[None], (count,) + block.shape), axes, 0, 0)
 
 
-def sum_parts(parts):
-    return jnp.sum(parts.astype(F32), axis=0).astype(BF16)
-
-
 def reduce_all(payload):
     count = lax.axis_size(PLANE)
-    parts = payload.reshape(count, PAYLOAD // count, CHANS)
-    part = sum_parts(lax.all_to_all(parts, PLANE, 0, 0))
-    part = sum_parts(to_all(part, ("z",)))
-    return to_all(part, PLANE).reshape(PAYLOAD, CHANS)
+    depth = lax.axis_size("z")
+    rows = PAYLOAD // count
+    parts = lax.all_to_all(payload.reshape(count, rows, CHANS), PLANE, 0, 0)
+    copies = call(sum_kernel, shape((depth, rows, CHANS), BF16), "sum_plane")(parts)
+    parts = lax.all_to_all(copies, "z", 0, 0)
+    copies = call(sum_kernel, shape((count, rows, CHANS), BF16), "sum_depth")(parts)
+    return lax.all_to_all(copies, PLANE, 0, 0).reshape(PAYLOAD, CHANS)
 
 
 def on_device(
@@ -272,57 +357,65 @@
     w_deg, w_gate, embed, w_radial, w_hidden, b_hidden, w_out,
 ):
     slab_count = lax.axis_size(SLAB)
-    shard_count = lax.axis_size(ATOM)
+    shards = lax.axis_size(ATOM)
+    chunk = PROBES // shards
     scale = 1.0 / math.sqrt(PROBES * slab_count)
     species = species.reshape(1, ATOMS)
-    lists = send_rows[0, 0]
-    with jax.named_scope("pack_pairs"):
-        pack = jnp.concatenate(
-            [
-                harmonics.transpose(1, 0, 2),
-                distances[:, None, :],
-                neighbours.astype(F32)[:, None, :],
-                jnp.zeros((SLOTS, FIELDS - COMPS - 2, PROBES), F32),
-            ],
-            axis=1,
-        )
+    pack = call(pack_kernel, shape((FIELDS, SLOTS, PROBES)), "pack")(
+        harmonics, distances, neighbours, target.reshape(1, PROBES)
+    )
     with jax.named_scope("exchange_pairs"):
-        packs = [pack] + [passed_along(pack, -offset) for offset in OFFSETS]
-    rows = call(encode_kernel, shape((COMPS * ATOMS, CHANS), BF16), "encode")(
-        atom_feats, species, w_deg, w_gate, embed
-    )
-    outs = call(
+        their_pack = to_partner(pack)
+    whole = pl.BlockSpec(memory_space=pltpu.VMEM)
+    apart = pl.BlockSpec(memory_space=pl.ANY)
+    rows, owners, split = call(
+        encode_kernel,
+        [
+            shape((COMPS * ATOMS, CHANS), BF16),
+            shape((len(OFFSETS), ATOMS, ATOMS), BF16),
+            shape((6 * BASES, DEGREES * CHANS), BF16),
+        ],
+        "encode",
+        in_specs=[apart, whole, apart, apart, whole, whole, whole],
+        scratch_shapes=[
+            pltpu.VMEM(atom_feats.shape, BF16),
+            pltpu.VMEM(w_deg.shape, BF16),
+            pltpu.VMEM(w_gate.shape, BF16),
+            pltpu.SemaphoreType.DMA((3,)),
+        ],
+    )(atom_feats, species, w_deg, w_gate, embed, send_rows[0, 0], w_radial)
+    with jax.named_scope("gather_pairs"):
+        packs = to_all(jnp.stack([pack, their_pack]), "y")
+    values, spread, sums, radial, basis = call(
         pair_kernel,
-        [shape((CHANS, PROBES))] * SOURCES
-        + [
+        [
+            shape((4, shards, 2, chunk, CHANS)),
             shape((COMPS * ATOMS, PAIRS), BF16),
             shape((DEGREES * CHANS, PAIRS)),
             shape((DEGREES * CHANS, PAIRS)),
             shape((BASES, PAIRS)),
         ],
         "pair_sums",
-    )(rows, lists, w_radial, *packs)
-    values = outs[:SOURCES]
-    spread, sums, radial, basis = outs[SOURCES:]
+    )(packs, rows, owners, split)
+    with jax.named_scope("scatter_sums"):
+        parts = lax.all_to_all(values.reshape(4 * shards, 2, chunk, CHANS), PLANE, 0, 0)
+    mine = call(sum_kernel, shape((2, chunk, CHANS)), "sum_sources")(parts)
     with jax.named_scope("exchange_sums"):
-        partial_value = values[0]
-        for which, offset in enumerate(OFFSETS):
-            partial_value = partial_value + passed_along(values[1 + which], offset)
-    with jax.named_scope("gather_shards"):
-        gathered = to_all(partial_value, ATOM)
-    density, upstream, head = call(
-        functools.partial(readout_kernel, scale, 1.0 / shard_count),
-        [shape((1, PROBES)), shape((CHANS, PROBES)), shape((CHANS + 16, CHANS))],
+        theirs = to_partner(mine)
+    up, head = call(
+        functools.partial(readout_kernel, scale),
+        [shape((2 * chunk + 8, CHANS)), shape((CHANS + 16, CHANS))],
         "readout",
+        scratch_shapes=[pltpu.VMEM((PROBES, PROBES), F32)],
     )(
-        gathered, target.reshape(1, PROBES), w_hidden, b_hidden.reshape(1, CHANS),
+        mine, theirs, pack, their_pack, w_hidden, b_hidden.reshape(1, CHANS),
         w_out.reshape(1, CHANS),
     )
-    with jax.named_scope("exchange_grads"):
-        upstreams = [upstream] + [passed_along(upstream, -offset) for offset in OFFSETS]
-    payload = call(backward_kernel, shape((PAYLOAD, CHANS), BF16), "backward")(
-        atom_feats, species, w_deg, w_gate, spread, sums, radial, basis, head, *upstreams
-    )
+    with jax.named_scope("gather_grads"):
+        ups = to_all(up, PLANE).reshape(4, shards, 2 * chunk + 8, CHANS)
+    payload, density = call(
+        backward_kernel, [shape((PAYLOAD, CHANS), BF16), shape((1, PROBES))], "backward"
+    )(atom_feats, species, w_deg, w_gate, spread, sums, radial, basis, head, ups)
     with jax.named_scope("reduce_grads"):
         payload = reduce_all(payload)
     loss, deg, gate, embed_grad, radial_grad, hidden, bias, out = call(

time: 157 us -> 143 us (0.911)
  starting transfers between devices: 48.6 us -> 24.7 us
  blocking collectives: 69.5 us -> 90.2 us
  waiting for transfers between devices: 12.6 us -> 2.77 us
  local copies, waits for them, and re-layouts: 6.54 us -> 9.24 us
  Pallas kernels: 16.3 us -> 14.2 us
  other arithmetic: 1.64 us -> 0.03 us
    all_to_all x1 -> x4, blocking collectives: 16.8 us -> 72.9 us  [the longest x1 21.4 us: reduce_all(): parts = lax.all_to_all(copies, 'z', 0, 0)]
    all_to_all x3 -> x1, blocking collectives: 52.7 us -> 17.3 us  [to_all(): lax.all_to_all(jnp.broadcast_to(block[None], (count,) + block.shape), axe...]
    ppermute x12 -> x2, starting transfers between devices: 48.6 us -> 21.3 us  [to_partner(): return lax.ppermute(block, SLAB, route)]
    ppermute x12 -> x2, waiting for transfers between devices: 12.6 us -> 2.76 us  [to_partner(): return lax.ppermute(block, SLAB, route)]
    all_to_all x0 -> x1, starting transfers between devices: none -> 3.41 us  [to_all(): lax.all_to_all(jnp.broadcast_to(block[None], (count,) + block.shape), axe...]
    pallas_call x4 -> x8, Pallas kernels: 15.4 us -> 13.3 us  [the longest x1 7.11 us: on_device(): call(backward_kernel, [shape((PAYLOAD, CHANS), BF16), shape((1, PROBES))]...]
    unnamed x31 -> x36, local copies, waits for them, and re-layouts: 6.34 us -> 8.42 us
  transfers between devices with their start and end apart: 12 -> 3, of which waited for: 5 -> 2; matrix products, arithmetic and copies ran while one was open for 0% -> 0% of each run, Pallas kernels for 0% -> 1%
where the time goes in v2:
time: 143 us; the launch traced here: 142 us
  blocking collectives  90.2 us (63%)
  starting transfers between devices  24.7 us (17%)
  Pallas kernels  14.2 us (10%)
  local copies, waits for them, and re-layouts  9.24 us (6%)
  waiting for transfers between devices  2.77 us (2%)
    all_to_all x1, blocking collectives, reduce_all(): parts = lax.all_to_all(copies, 'z', 0, 0)  21.4 us
    ppermute x2, starting transfers between devices, to_partner(): return lax.ppermute(block, SLAB, route)  21.3 us
    all_to_all x1, blocking collectives, on_device(): lax.all_to_all(values.reshape(4 * shards, 2, chunk, CHANS), PLANE, 0, 0)  20.3 us
    all_to_all x1, blocking collectives, reduce_all(): return lax.all_to_all(copies, PLANE, 0, 0).reshape(PAYLOAD, CHANS)  17.6 us
    all_to_all x1, blocking collectives, to_all(): lax.all_to_all(jnp.broadcast_to(block[None], (count,) + block.shape), axe...  17.3 us
    all_to_all x1, blocking collectives, reduce_all(): parts = lax.all_to_all(payload.reshape(count, rows, CHANS), PLANE, 0, 0)  13.7 us
    unnamed x36, local copies, waits for them, and re-layouts  8.42 us
    pallas_call x1, Pallas kernels, on_device(): call(backward_kernel, [shape((PAYLOAD, CHANS), BF16), shape((1, PROBES))]...  7.11 us
  transfers between devices with their start and end apart: 3, of which 2 were waited for; matrix products, arithmetic and copies ran while one was open for 0% of the time, Pallas kernels for 1%

profile of v2, /device:TPU:1, one launch (start us, length us, event | category | flops | bytes accessed | tf_op | source)
XLA Modules:
  0.0 142.0 jit_solution(15046272440740571042)
XLA Ops:
  0.6 0.0 copy-start.5
  0.7 0.0 copy-start.3
  0.7 0.0 copy-start.1
  0.7 0.8 copy-done.7
  1.5 0.7 copy-done.13
  2.2 0.7 copy-done.14
  2.9 0.7 copy-done.15
  3.5 14.7 %collective-permute-start = (f32[32,2,128]{2,1,0:T(2,128)S(1)}, f32[32,2,128]{2,1,0:T(2,128)S(1)}, u32[]{:S(2)}, u32[]{:S(2)}) collective-permute-start(f32[32,2,128]{2,1,0:T(2,128)S(1)} %pack.1.pack_ref), channel_id=1, source_target_pairs={{0,496},{8,504},{16,32},{24,40},{32,16},{40,24},{48,64},{56,72},{6... | collective-permute-start | bytes 98312 | tf_op jit(solution)/shard_map/exchange_pairs/ppermute | solution.py:336
  18.3 1.3 collective-permute-done.their_pack_ref
  19.6 0.8 broadcast_in_dim.4
  20.4 3.4 %all-to-all-start = ((f32[4,2,32,2,128]{4,3,2,1,0:T(2,128)}), f32[4,2,32,2,128]{4,3,2,1,0:T(2,128)S(1)}, u32[]{:S(2)}, u32[]{:S(2)}) async-start(f32[4,2,32,2,128]{4,3,2,1,0:T(2,128)} %broadcast_in_dim.4), calls=%async_computation | async-start | bytes 524288 | tf_op jit(solution)/shard_map/gather_pairs/all_to_all | solution.py:341
  23.8 1.0 copy-done
  24.8 0.9 copy-done.2
  25.7 0.9 copy-done.4
  26.6 0.7 copy-done.8
  27.3 0.7 copy-done.9
  28.0 0.7 copy-done.10
  28.7 0.7 copy-done.11
  29.4 1.0 encode.1
  30.3 4.5 %pair_sums.1 = (f32[4,8,2,16,128]{4,3,2,1,0:T(8,128)S(1)}, bf16[1600,1280]{1,0:T(8,128)(2,1)}, f32[640,1280]{1,0:T(8,128)S(1)}, f32[640,1280]{1,0:T(8,128)}, f32[8,1280]{1,0:T(8,128)S(1)}) custom-call(f32[4,2,32,2,128]{4,3,2,1,0:T(2,128)S(1)} %all-to-all-done.packs_ref, bf16[1600,128]{1,0:T(8,128)(2,1)S(1)} %get-tuple-element.29.rows_ref, ...), custom_call_target="tpu_custom_call" | custom-call | tf_op jit(solution)/shard_map/pair_sums/pallas_call | solution.py:389
  34.8 20.3 %all_to_all.30.parts_ref = f32[32,2,16,128]{3,2,1,0:T(8,128)S(1)} all-to-all(f32[32,2,16,128]{3,2,1,0:T(8,128)S(1)} %bitcast.17), channel_id=1, replica_groups=mesh['z'=16,'y'=4,'x'=4,'c'=2] {'y','x','c'}, dimensions={0} | all-to-all | bytes 1048576 | tf_op jit(solution)/shard_map/scatter_sums/all_to_all | solution.py:401
  55.1 6.6 %collective-permute-start.1 = (f32[2,16,128]{2,1,0:T(8,128)S(1)}, f32[2,16,128]{2,1,0:T(8,128)S(1)}, u32[]{:S(2)}, u32[]{:S(2)}) collective-permute-start(f32[2,16,128]{2,1,0:T(8,128)S(1)} %sum_sources.1.mine_ref), channel_id=1, source_target_pairs={{0,496},{8,504},{16,32},{24,40},{32,16},{40,24},{48,64},{56,72},{6... | collective-permute-start | bytes 49160 | tf_op jit(solution)/shard_map/exchange_sums/ppermute | solution.py:336
  61.7 1.5 %collective-permute-done.1.theirs_ref = f32[2,16,128]{2,1,0:T(8,128)S(1)} collective-permute-done((f32[2,16,128]{2,1,0:T(8,128)S(1)}, f32[2,16,128]{2,1,0:T(8,128)S(1)}, u32[]{:S(2)}, u32[]{:S(2)}) %collective-permute-start.1) | collective-permute-done | bytes 16416 | tf_op jit(solution)/shard_map/exchange_sums/ppermute | solution.py:336
  63.2 0.6 readout.1
  63.8 0.1 broadcast_in_dim.5
  63.9 17.3 %all_to_all.31 = f32[32,40,128]{2,1,0:T(8,128)S(1)} all-to-all(f32[32,40,128]{2,1,0:T(8,128)S(1)} %broadcast_in_dim.5), channel_id=1, replica_groups=mesh['z'=16,'y'=4,'x'=4,'c'=2] {'y','x','c'}, dimensions={0} | all-to-all | bytes 1310720 | tf_op jit(solution)/shard_map/gather_grads/all_to_all | solution.py:341
  81.2 7.1 %backward.1 = (bf16[1536,128]{1,0:T(8,128)(2,1)S(1)}, f32[1,128]{1,0:T(1,128)}) custom-call(bf16[64,3200]{1,0:T(8,128)(2,1)S(1)} %copy-done.1, s32[1,64]{1,0:T(1,128)S(1)} %bitcast.23, bf16[5,128,128]{2,1,0:T(8,128)(2,1)S(1)} %copy-done.3, bf16[128,512]{1,0:T(8,128)(2,1)S(1)} %copy-done.5, bf16[1600,1280]{1,0:T(8,128)(2,1)} %get-tuple-element.32.spread_ref, ...), custom_call_target="tpu_custom_call" | custom-call | tf_op jit(solution)/shard_map/backward/pallas_call | solution.py:416
  88.3 13.7 %all_to_all.32.parts_ref = bf16[32,48,128]{2,1,0:T(8,128)(2,1)S(1)} all-to-all(bf16[32,48,128]{2,1,0:T(8,128)(2,1)S(1)} %bitcast.18), channel_id=1, replica_groups=mesh['z'=16,'y'=4,'x'=4,'c'=2] {'y','x','c'}, dimensions={0} | all-to-all | bytes 786432 | tf_op jit(solution)/shard_map/reduce_grads/all_to_all | solution.py:348
  102.0 0.1 sum_plane.1
  102.1 21.4 %all_to_all.33.parts_ref = bf16[16,48,128]{2,1,0:T(8,128)(2,1)S(1)} all-to-all(bf16[16,48,128]{2,1,0:T(8,128)(2,1)S(1)} %sum_plane.1), channel_id=1, replica_groups=mesh['z'=16,'y'=4,'x'=4,'c'=2] {'z'}, dimensions={0} | all-to-all | bytes 393216 | tf_op jit(solution)/shard_map/reduce_grads/all_to_all | solution.py:350
  123.5 17.6 %all_to_all.34 = bf16[32,48,128]{2,1,0:T(8,128)(2,1)S(1)} all-to-all(bf16[32,48,128]{2,1,0:T(8,128)(2,1)S(1)} %sum_depth.1), channel_id=1, replica_groups=mesh['z'=16,'y'=4,'x'=4,'c'=2] {'y','x','c'}, dimensions={0} | all-to-all | bytes 786432 | tf_op jit(solution)/shard_map/reduce_grads/all_to_all | solution.py:352
  141.1 0.9 unpack.1
  (27 shorter events, 0.2 us)
Async XLA Ops:
  0.6 80.5 %copy-start.5 = (bf16[128,512]{1,0:T(8,128)(2,1)S(1)}, bf16[128,512]{1,0:T(8,128)(2,1)}, u32[]{:S(2)}) copy-start(bf16[128,512]{1,0:T(8,128)(2,1)} %w_gate_ref.1) | copy-start | bytes 393220
  0.7 80.5 %copy-start.3 = (bf16[5,128,128]{2,1,0:T(8,128)(2,1)S(1)}, bf16[5,128,128]{2,1,0:T(8,128)(2,1)}, u32[]{:S(2)}) copy-start(bf16[5,128,128]{2,1,0:T(8,128)(2,1)} %w_deg_ref.1) | copy-start | bytes 491524
  0.7 80.5 %copy-start.1 = (bf16[64,3200]{1,0:T(8,128)(2,1)S(1)}, bf16[64,3200]{1,0:T(8,128)(2,1)}, u32[]{:S(2)}) copy-start(bf16[64,3200]{1,0:T(8,128)(2,1)} %feats_ref.1) | copy-start | bytes 1228804
  0.7 62.5 %copy-start.6 = (f32[128,128]{1,0:T(8,128)S(1)}, f32[128,128]{1,0:T(8,128)}, u32[]{:S(2)}) copy-start(f32[128,128]{1,0:T(8,128)} %w_hidden_ref.1) | copy-start | bytes 196612
  0.7 0.8 copy-start.7
  1.5 0.7 copy-start.13
  2.2 0.7 copy-start.14
  2.9 0.7 copy-start.15
  3.5 59.7 %copy-start.16 = (f32[128]{0:T(128)S(1)}, f32[128]{0:T(128)}, u32[]{:S(2)}) copy-start(f32[128]{0:T(128)} %param.26) | copy-start | bytes 1540
  3.5 59.7 %copy-start.17 = (f32[128]{0:T(128)S(1)}, f32[128]{0:T(128)}, u32[]{:S(2)}) copy-start(f32[128]{0:T(128)} %param.27) | copy-start | bytes 1540
  3.5 77.6 %copy-start.12 = (s32[64]{0:T(128)S(1)}, s32[64]{0:T(128)}, u32[]{:S(2)}) copy-start(s32[64]{0:T(128)} %param.15) | copy-start | bytes 772
  3.5 16.0 %collective-permute-start = (f32[32,2,128]{2,1,0:T(2,128)S(1)}, f32[32,2,128]{2,1,0:T(2,128)S(1)}, u32[]{:S(2)}, u32[]{:S(2)}) collective-permute-start(f32[32,2,128]{2,1,0:T(2,128)S(1)} %pack.1.pack_ref), channel_id=1, source_target_pairs={{0,496},{8,504},{16,32},{24,40},{32,16},{40,24},{48,64},{56,72},{6... | collective-permute-start | bytes 98312 | tf_op jit(solution)/shard_map/exchange_pairs/ppermute | solution.py:336
  20.4 10.0 %all-to-all-start = ((f32[4,2,32,2,128]{4,3,2,1,0:T(2,128)}), f32[4,2,32,2,128]{4,3,2,1,0:T(2,128)S(1)}, u32[]{:S(2)}, u32[]{:S(2)}) async-start(f32[4,2,32,2,128]{4,3,2,1,0:T(2,128)} %broadcast_in_dim.4), calls=%async_computation | async-start | bytes 524288 | tf_op jit(solution)/shard_map/gather_pairs/all_to_all | solution.py:341
  23.8 1.0 copy-start
  24.8 0.9 copy-start.2
  25.7 0.9 copy-start.4
  26.6 0.7 copy-start.8
  27.3 0.7 copy-start.9
  28.0 0.7 copy-start.10
  28.7 0.7 copy-start.11
  55.1 8.1 %collective-permute-start.1 = (f32[2,16,128]{2,1,0:T(8,128)S(1)}, f32[2,16,128]{2,1,0:T(8,128)S(1)}, u32[]{:S(2)}, u32[]{:S(2)}) collective-permute-start(f32[2,16,128]{2,1,0:T(8,128)S(1)} %sum_sources.1.mine_ref), channel_id=1, source_target_pairs={{0,496},{8,504},{16,32},{24,40},{32,16},{40,24},{48,64},{56,72},{6... | collective-permute-start | bytes 49160 | tf_op jit(solution)/shard_map/exchange_sums/ppermute | solution.py:336

commit v3 on v2

--- a/solution.py
+++ b/solution.py
@@ -30,6 +30,7 @@
 BASES = 8
 KINDS = 8
 PAYLOAD = 1536
+LIMIT = 63
 
 
 def first_rows(degree):
@@ -70,24 +71,39 @@
     return (ids == species_ref[...]).astype(F32)
 
 
-def encode_kernel(
-    feats_hbm, species_ref, w_deg_hbm, w_gate_hbm, embed_ref, lists_ref, w_radial_ref,
-    rows_ref, owners_ref, split_ref, feats_ref, w_deg_ref, w_gate_ref, sems,
-):
+def started(pairs, sems):
     copies = [
         pltpu.make_async_copy(source, target, sems.at[index])
-        for index, (source, target) in enumerate(
-            ((w_gate_hbm, w_gate_ref), (feats_hbm, feats_ref), (w_deg_hbm, w_deg_ref))
-        )
+        for index, (source, target) in enumerate(pairs)
     ]
     for copy in copies:
         copy.start()
+    return copies
+
+
+def encode_kernel(
+    feats_hbm, species_hbm, w_deg_hbm, w_gate_hbm, embed_hbm, lists_hbm, w_radial_hbm,
+    rows_ref, owners_ref, split_ref,
+    feats_ref, species_ref, w_deg_ref, w_gate_ref, embed_ref, lists_ref, w_radial_ref, sems,
+):
+    copies = started(
+        (
+            (feats_hbm, feats_ref),
+            (species_hbm, species_ref),
+            (w_deg_hbm, w_deg_ref),
+            (w_gate_hbm, w_gate_ref),
+            (embed_hbm, embed_ref),
+            (lists_hbm, lists_ref),
+            (w_radial_hbm, w_radial_ref),
+        ),
+        sems,
+    )
+    for copy in copies:
+        copy.wait()
     ids = lax.broadcasted_iota(jnp.int32, (ATOMS, ATOMS), 0)
     for which in range(len(OFFSETS)):
         owners_ref[which] = (ids == lists_ref[which : which + 1, :]).astype(BF16)
     split_ref[...] = stacked(w_radial_ref[...], (0, 0, 1, 1, 0, 2))
-    for copy in copies:
-        copy.wait()
     scalar = feats_ref[:, lanes(0)]
     gates = jax.nn.sigmoid(matmul(scalar, w_gate_ref[...]))
     for degree in range(DEGREES):
@@ -123,24 +139,47 @@
     return place, jnp.where(jnp.logical_or(below, above), 1, 0)
 
 
-def pack_kernel(harm_ref, dist_ref, nbr_ref, target_ref, pack_ref):
-    pack_ref[0:COMPS] = harm_ref[...]
-    pack_ref[COMPS] = dist_ref[...]
+def pack_kernel(harm_hbm, dist_hbm, nbr_hbm, target_hbm, pack_ref, nbr_ref, target_ref, sems):
+    copies = started(
+        (
+            (harm_hbm, pack_ref.at[pl.ds(0, COMPS)]),
+            (dist_hbm, pack_ref.at[COMPS]),
+            (nbr_hbm, nbr_ref),
+            (target_hbm, target_ref),
+        ),
+        sems,
+    )
+    for copy in copies:
+        copy.wait()
     pack_ref[COMPS + 1] = nbr_ref[...].astype(F32)
     pack_ref[COMPS + 2] = jnp.broadcast_to(target_ref[...], (SLOTS, PROBES))
     pack_ref[COMPS + 3 :] = jnp.zeros((FIELDS - COMPS - 3, SLOTS, PROBES), F32)
 
 
 def pair_kernel(
-    packs_ref, rows_ref, owners_ref, split_ref,
-    out_ref, spread_ref, sums_ref, radial_ref, basis_ref,
+    packs_hbm, rows_hbm, owners_hbm, split_hbm, out_hbm, spread_hbm, sums_hbm,
+    packs_ref, rows_ref, owners_ref, split_ref, sems,
+    out_ref, spread_ref, sums_ref, out_sems,
 ):
+    copies = started(
+        (
+            (packs_hbm, packs_ref),
+            (owners_hbm, owners_ref),
+            (split_hbm, split_ref),
+            (rows_hbm, rows_ref),
+        ),
+        sems,
+    )
     shards, chunk = out_ref.shape[1], out_ref.shape[3]
+    out_ref[...] = jnp.zeros(out_ref.shape, F32)
+    copies[0].wait()
     sub = lax.broadcasted_iota(jnp.int32, (ATOMS, PROBES), 0).astype(F32)
     dists, places = [], []
     for source in range(SOURCES):
         place, part = plane_place(DELTAS[source])
         places.append((place, part))
+        if source == 1:
+            copies[1].wait()
         for slot in range(SLOTS):
             start = source * SPAN + slot * PROBES
 
@@ -155,29 +194,36 @@
                     hot * row(m)
                 ).astype(BF16)
             dists.append(row(COMPS))
+    writes = started(((spread_ref, spread_hbm),), out_sems)
     dist = jnp.concatenate(dists, axis=1)
     orders = lax.broadcasted_iota(jnp.int32, (BASES, PAIRS), 0).astype(F32) + 1.0
     phase = math.pi * dist / CUTOFF
     envelope = 0.5 * (jnp.cos(phase) + 1.0) / dist
     basis = jnp.sin(phase * orders) * envelope
-    basis_ref[...] = basis
     basis_split = stacked(basis, (0, 1, 0, 1, 2, 0))
+    sums_ref[DEGREES * CHANS :, :] = basis_split
+    copies[2].wait()
+    copies[3].wait()
     total = None
     for degree in range(DEGREES):
         low, high = first_rows(degree)
         radial = along_first(split_ref[:, lanes(degree)], basis_split)
-        radial_ref[lanes(degree), :] = radial
         sums = along_first(rows_ref[low:high, :], spread_ref[low:high, :])
-        sums_ref[lanes(degree), :] = sums
+        sums_ref[lanes(degree), :] = sums.astype(BF16)
         term = radial * sums
         total = term if total is None else total + term
-    out_ref[...] = jnp.zeros(out_ref.shape, F32)
     for source in range(SOURCES):
         start = source * SPAN
         value = (total[:, start : start + PROBES] + total[:, start + PROBES : start + SPAN]).T
         place, part = places[source]
         for shard in range(shards):
             out_ref[place, shard, part] = value[shard * chunk : (shard + 1) * chunk, :]
+    writes += started(
+        ((out_ref, out_hbm), (sums_ref, sums_hbm)),
+        out_sems.at[pl.ds(1, 2)],
+    )
+    for write in writes:
+        write.wait()
 
 
 def silu_slope(values):
@@ -235,9 +281,15 @@
 
 
 def backward_kernel(
-    feats_ref, species_ref, w_deg_ref, w_gate_ref, spread_ref, sums_ref, radial_ref, basis_ref,
-    head_ref, up_ref, payload_ref, density_ref,
+    feats_ref, species_ref, w_deg_ref, w_gate_ref, split_ref, head_ref, up_ref,
+    spread_hbm, sums_hbm, payload_ref, density_ref, spread_ref, sums_ref, sems,
 ):
+    spreads = [pl.ds(low, high - low) for low, high in map(first_rows, range(DEGREES))]
+    copies = started(
+        [(sums_hbm, sums_ref)]
+        + [(spread_hbm.at[part], spread_ref.at[part]) for part in spreads],
+        sems,
+    )
     shards = up_ref.shape[1]
     chunk = PROBES // shards
     blocks = []
@@ -256,16 +308,17 @@
     density_ref[...] = density
     scalar = feats_ref[:, lanes(0)]
     gates = jax.nn.sigmoid(matmul(scalar, w_gate_ref[...]))
-    basis_split = stacked(basis_ref[...], (0, 1))
+    copies[0].wait()
+    basis_split = sums_ref[DEGREES * CHANS :, :]
     radial_grads = []
     for degree in range(DEGREES):
         low, high = first_rows(degree)
-        inner = (radial_ref[lanes(degree), :] * upstream).astype(BF16)
+        radial = along_first(split_ref[:, lanes(degree)], basis_split)
+        inner = (radial * upstream).astype(BF16)
+        copies[1 + degree].wait()
         grads = along_last(spread_ref[low:high, :], inner)
-        product = sums_ref[lanes(degree), :] * upstream
-        main = product.astype(BF16)
-        rest = (product - main.astype(F32)).astype(BF16)
-        both = along_last(main, basis_split) + along_last(rest, basis_split)
+        product = (sums_ref[lanes(degree), :].astype(F32) * upstream).astype(BF16)
+        both = along_last(product, basis_split[0 : 2 * BASES, :])
         radial_grads.append((both[:, 0:BASES] + both[:, BASES : 2 * BASES]).T)
         rows = component_rows(feats_ref, degree)
         mixed = matmul(rows, w_deg_ref[degree])
@@ -320,14 +373,34 @@
     return jax.ShapeDtypeStruct(dims, dtype)
 
 
-def call(kernel, outs, name, **options):
+def call(kernel, outs, name, limit=48, **options):
     return pl.pallas_call(
         kernel,
         out_shape=outs,
         name=name,
-        compiler_params=pltpu.CompilerParams(vmem_limit_bytes=48 * 1024 * 1024),
+        compiler_params=pltpu.CompilerParams(vmem_limit_bytes=limit * 1024 * 1024),
         **options,
     )
+
+
+def staging(arrays):
+    return [pltpu.VMEM(array.shape, array.dtype) for array in arrays] + [
+        pltpu.SemaphoreType.DMA((len(arrays),))
+    ]
+
+
+def call_apart(kernel, outs, name, *operands, outside=False):
+    far = pl.BlockSpec(memory_space=pltpu.HBM)
+    options = {"out_specs": [far] * len(outs)} if outside else {}
+    return call(
+        kernel,
+        outs,
+        name,
+        limit=LIMIT,
+        in_specs=[far] * len(operands),
+        scratch_shapes=staging(operands) + (staging(outs) if outside else []),
+        **options,
+    )(*operands)
 
 
 def to_partner(block):
@@ -361,14 +434,21 @@
     chunk = PROBES // shards
     scale = 1.0 / math.sqrt(PROBES * slab_count)
     species = species.reshape(1, ATOMS)
-    pack = call(pack_kernel, shape((FIELDS, SLOTS, PROBES)), "pack")(
-        harmonics, distances, neighbours, target.reshape(1, PROBES)
-    )
+    pack = call(
+        pack_kernel,
+        shape((FIELDS, SLOTS, PROBES)),
+        "pack",
+        limit=LIMIT,
+        in_specs=[pl.BlockSpec(memory_space=pltpu.HBM)] * 4,
+        scratch_shapes=[
+            pltpu.VMEM((SLOTS, PROBES), jnp.int32),
+            pltpu.VMEM((1, PROBES), F32),
+            pltpu.SemaphoreType.DMA((4,)),
+        ],
+    )(harmonics, distances, neighbours, target.reshape(1, PROBES))
     with jax.named_scope("exchange_pairs"):
         their_pack = to_partner(pack)
-    whole = pl.BlockSpec(memory_space=pltpu.VMEM)
-    apart = pl.BlockSpec(memory_space=pl.ANY)
-    rows, owners, split = call(
+    rows, owners, split = call_apart(
         encode_kernel,
         [
             shape((COMPS * ATOMS, CHANS), BF16),
@@ -376,27 +456,18 @@
             shape((6 * BASES, DEGREES * CHANS), BF16),
         ],
         "encode",
-        in_specs=[apart, whole, apart, apart, whole, whole, whole],
-        scratch_shapes=[
-            pltpu.VMEM(atom_feats.shape, BF16),
-            pltpu.VMEM(w_deg.shape, BF16),
-            pltpu.VMEM(w_gate.shape, BF16),
-            pltpu.SemaphoreType.DMA((3,)),
-        ],
-    )(atom_feats, species, w_deg, w_gate, embed, send_rows[0, 0], w_radial)
+        atom_feats, species, w_deg, w_gate, embed, send_rows[0, 0], w_radial,
+    )
     with jax.named_scope("gather_pairs"):
         packs = to_all(jnp.stack([pack, their_pack]), "y")
-    values, spread, sums, radial, basis = call(
-        pair_kernel,
-        [
-            shape((4, shards, 2, chunk, CHANS)),
-            shape((COMPS * ATOMS, PAIRS), BF16),
-            shape((DEGREES * CHANS, PAIRS)),
-            shape((DEGREES * CHANS, PAIRS)),
-            shape((BASES, PAIRS)),
-        ],
-        "pair_sums",
-    )(packs, rows, owners, split)
+    held = [
+        shape((4, shards, 2, chunk, CHANS)),
+        shape((COMPS * ATOMS, PAIRS), BF16),
+        shape((DEGREES * CHANS + 6 * BASES, PAIRS), BF16),
+    ]
+    values, spread, sums = call_apart(
+        pair_kernel, held, "pair_sums", packs, rows, owners, split, outside=True
+    )
     with jax.named_scope("scatter_sums"):
         parts = lax.all_to_all(values.reshape(4 * shards, 2, chunk, CHANS), PLANE, 0, 0)
     mine = call(sum_kernel, shape((2, chunk, CHANS)), "sum_sources")(parts)
@@ -413,9 +484,18 @@
     )
     with jax.named_scope("gather_grads"):
         ups = to_all(up, PLANE).reshape(4, shards, 2 * chunk + 8, CHANS)
+    near, far = pl.BlockSpec(memory_space=pltpu.VMEM), pl.BlockSpec(memory_space=pltpu.HBM)
     payload, density = call(
-        backward_kernel, [shape((PAYLOAD, CHANS), BF16), shape((1, PROBES))], "backward"
-    )(atom_feats, species, w_deg, w_gate, spread, sums, radial, basis, head, ups)
+        backward_kernel,
+        [shape((PAYLOAD, CHANS), BF16), shape((1, PROBES))],
+        "backward",
+        in_specs=[near] * 7 + [far] * 2,
+        scratch_shapes=[
+            pltpu.VMEM(spread.shape, BF16),
+            pltpu.VMEM(sums.shape, BF16),
+            pltpu.SemaphoreType.DMA((1 + DEGREES,)),
+        ],
+    )(atom_feats, species, w_deg, w_gate, split, head, ups, spread, sums)
     with jax.named_scope("reduce_grads"):
         payload = reduce_all(payload)
     loss, deg, gate, embed_grad, radial_grad, hidden, bias, out = call(

time: 143 us -> 140 us (0.979)
  local copies, waits for them, and re-layouts: 9.24 us -> 0.87 us
  waiting for transfers between devices: 2.77 us -> 6.85 us
  Pallas kernels: 14.2 us -> 16.4 us
    unnamed x36 -> x20, local copies, waits for them, and re-layouts: 8.42 us -> 0.05 us
    pallas_call x3, Pallas kernels: 5.44 us -> 9.05 us  [the longest x2 7.54 us: call_apart(): call(kernel, outs, name, limit=LIMIT, in_specs=[far] * len(operands), scr...]
    all_to_all x1, waiting for transfers between devices: 0.01 us -> 3.26 us  [to_all(): lax.all_to_all(jnp.broadcast_to(block[None], (count,) + block.shape), axe...]
    pallas_call x1, Pallas kernels: 7.11 us -> 5.67 us  [on_device(): call(backward_kernel, [shape((PAYLOAD, CHANS), BF16), shape((1, PROBES))]...]
  transfers between devices with their start and end apart: 3 -> 3, of which waited for: 2 -> 3; matrix products, arithmetic and copies ran while one was open for 0% -> 0% of each run, Pallas kernels for 1% -> 2%
where the time goes in v3:
time: 140 us
  blocking collectives  89.2 us (64%)
  starting transfers between devices  24.6 us (18%)
  Pallas kernels  16.4 us (12%)
  waiting for transfers between devices  6.85 us (5%)
    all_to_all x1, blocking collectives, reduce_all(): parts = lax.all_to_all(copies, 'z', 0, 0)  21.1 us
    ppermute x2, starting transfers between devices, to_partner(): return lax.ppermute(block, SLAB, route)  20.6 us
    all_to_all x1, blocking collectives, on_device(): lax.all_to_all(values.reshape(4 * shards, 2, chunk, CHANS), PLANE, 0, 0)  19.4 us
    all_to_all x1, blocking collectives, reduce_all(): return lax.all_to_all(copies, PLANE, 0, 0).reshape(PAYLOAD, CHANS)  17.6 us
    all_to_all x1, blocking collectives, to_all(): lax.all_to_all(jnp.broadcast_to(block[None], (count,) + block.shape), axe...  17.3 us
    all_to_all x1, blocking collectives, reduce_all(): parts = lax.all_to_all(payload.reshape(count, rows, CHANS), PLANE, 0, 0)  13.7 us
    pallas_call x2, Pallas kernels, call_apart(): call(kernel, outs, name, limit=LIMIT, in_specs=[far] * len(operands), scr...  7.54 us
    pallas_call x1, Pallas kernels, on_device(): call(backward_kernel, [shape((PAYLOAD, CHANS), BF16), shape((1, PROBES))]...  5.67 us
  transfers between devices with their start and end apart: 3, of which 3 were waited for; matrix products, arithmetic and copies ran while one was open for 0% of the time, Pallas kernels for 2%

profile of v3, /device:TPU:1, one launch (start us, length us, event | category | flops | bytes accessed | tf_op | source)
XLA Modules:
  0.0 139.5 jit_solution(16415404100740367797)
XLA Ops:
  0.6 0.0 copy-start.3
  0.7 0.0 copy-start.2
  0.7 0.0 copy-start.1
  0.7 0.0 copy-start.7
  0.7 0.0 copy-start.9
  0.7 0.0 copy-start.8
  0.7 0.0 copy-start.6
  0.7 1.5 %pack.1.pack_ref = f32[32,2,128]{2,1,0:T(2,128)} custom-call(f32[25,2,128]{2,1,0:T(2,128)} %harm_hbm.1, f32[2,128]{1,0:T(2,128)} %dist_hbm.1, s32[2,128]{1,0:T(2,128)} %nbr_hbm.1, f32[1,128]{1,0:T(1,128)} %bitcast.26), custom_call_target="tpu_custom_call" | custom-call | tf_op jit(solution)/shard_map/pack/pallas_call | solution.py:437
  2.3 14.6 %collective-permute-start = (f32[32,2,128]{2,1,0:T(2,128)}, f32[32,2,128]{2,1,0:T(2,128)S(1)}, u32[]{:S(2)}, u32[]{:S(2)}) collective-permute-start(f32[32,2,128]{2,1,0:T(2,128)} %pack.1.pack_ref), channel_id=1, source_target_pairs={{0,496},{8,504},{16,32},{24,40},{32,16},{40,24},{48,64},{56,72},{6... | collective-permute-start | bytes 98312 | tf_op jit(solution)/shard_map/exchange_pairs/ppermute | solution.py:409
  16.8 1.5 %collective-permute-done.their_pack_ref = f32[32,2,128]{2,1,0:T(2,128)S(1)} collective-permute-done((f32[32,2,128]{2,1,0:T(2,128)}, f32[32,2,128]{2,1,0:T(2,128)S(1)}, u32[]{:S(2)}, u32[]{:S(2)}) %collective-permute-start) | collective-permute-done | bytes 32800 | tf_op jit(solution)/shard_map/exchange_pairs/ppermute | solution.py:409
  18.3 0.8 pad_maximum_fusion
  19.1 0.8 broadcast_in_dim.4
  19.9 4.0 %all-to-all-start = ((f32[4,2,32,2,128]{4,3,2,1,0:T(2,128)}), f32[4,2,32,2,128]{4,3,2,1,0:T(2,128)}, u32[]{:S(2)}, u32[]{:S(2)}) async-start(f32[4,2,32,2,128]{4,3,2,1,0:T(2,128)} %broadcast_in_dim.4), calls=%async_computation | async-start | bytes 524288 | tf_op jit(solution)/shard_map/gather_pairs/all_to_all | solution.py:414
  24.0 2.3 %encode.1 = (bf16[1600,128]{1,0:T(8,128)(2,1)}, bf16[4,64,64]{2,1,0:T(8,128)(2,1)}, bf16[48,640]{1,0:T(8,128)(2,1)}) custom-call(bf16[64,3200]{1,0:T(8,128)(2,1)} %feats_ref.1, s32[1,64]{1,0:T(1,128)} %bitcast.20, bf16[5,128,128]{2,1,0:T(8,128)(2,1)} %w_deg_ref.1, bf16[128,512]{1,0:T(8,128)(2,1)} %w_gate_ref.1, f32[8,128]{1,0:T(8,128)} %embed_hbm.1, ...), custom_call_target="tpu_custom_call" | custom-call | tf_op jit(solution)/shard_map/encode/pallas_call | solution.py:395
  26.3 0.0 copy-start.5
  26.3 3.3 %all-to-all-done.packs_hbm = f32[4,2,32,2,128]{4,3,2,1,0:T(2,128)} async-done(((f32[4,2,32,2,128]{4,3,2,1,0:T(2,128)}), f32[4,2,32,2,128]{4,3,2,1,0:T(2,128)}, u32[]{:S(2)}, u32[]{:S(2)}) %all-to-all-start) | async-done | bytes 262176 | tf_op jit(solution)/shard_map/gather_pairs/all_to_all | solution.py:414
  29.5 5.2 %pair_sums.1 = (f32[4,8,2,16,128]{4,3,2,1,0:T(8,128)}, bf16[1600,1280]{1,0:T(8,128)(2,1)}, bf16[688,1280]{1,0:T(8,128)(2,1)}) custom-call(f32[4,2,32,2,128]{4,3,2,1,0:T(2,128)} %all-to-all-done.packs_hbm, bf16[1600,128]{1,0:T(8,128)(2,1)} %get-tuple-element.28.rows_hbm, bf16[4,64,64]{2,1,0:T(8,128)(2,1)} %get-tuple-element.29.owners_hbm, ...), custom_call_target="tpu_custom_call" | custom-call | tf_op jit(solution)/shard_map/pair_sums/pallas_call | solution.py:395
  34.8 19.4 %all_to_all.30.parts_ref = f32[32,2,16,128]{3,2,1,0:T(8,128)S(1)} all-to-all(f32[32,2,16,128]{3,2,1,0:T(8,128)} %bitcast.24), channel_id=1, replica_groups=mesh['z'=16,'y'=4,'x'=4,'c'=2] {'y','x','c'}, dimensions={0} | all-to-all | bytes 1048576 | tf_op jit(solution)/shard_map/scatter_sums/all_to_all | solution.py:472
  54.3 6.0 %collective-permute-start.1 = (f32[2,16,128]{2,1,0:T(8,128)S(1)}, f32[2,16,128]{2,1,0:T(8,128)S(1)}, u32[]{:S(2)}, u32[]{:S(2)}) collective-permute-start(f32[2,16,128]{2,1,0:T(8,128)S(1)} %sum_sources.1.mine_ref), channel_id=1, source_target_pairs={{0,496},{8,504},{16,32},{24,40},{32,16},{40,24},{48,64},{56,72},{6... | collective-permute-start | bytes 49160 | tf_op jit(solution)/shard_map/exchange_sums/ppermute | solution.py:409
  60.3 2.1 %collective-permute-done.1.theirs_ref = f32[2,16,128]{2,1,0:T(8,128)S(1)} collective-permute-done((f32[2,16,128]{2,1,0:T(8,128)S(1)}, f32[2,16,128]{2,1,0:T(8,128)S(1)}, u32[]{:S(2)}, u32[]{:S(2)}) %collective-permute-start.1) | collective-permute-done | bytes 16416 | tf_op jit(solution)/shard_map/exchange_sums/ppermute | solution.py:409
  62.4 0.0 copy-done.6
  62.4 0.0 copy-done.4
  62.4 0.6 readout.1
  63.0 0.1 broadcast_in_dim.5
  63.1 17.3 %all_to_all.31 = f32[32,40,128]{2,1,0:T(8,128)S(1)} all-to-all(f32[32,40,128]{2,1,0:T(8,128)S(1)} %broadcast_in_dim.5), channel_id=1, replica_groups=mesh['z'=16,'y'=4,'x'=4,'c'=2] {'y','x','c'}, dimensions={0} | all-to-all | bytes 1310720 | tf_op jit(solution)/shard_map/gather_grads/all_to_all | solution.py:414
  80.3 0.0 copy-done.3
  80.4 5.7 %backward.1 = (bf16[1536,128]{1,0:T(8,128)(2,1)S(1)}, f32[1,128]{1,0:T(1,128)}) custom-call(bf16[64,3200]{1,0:T(8,128)(2,1)S(1)} %copy-done.1, s32[1,64]{1,0:T(1,128)S(1)} %bitcast.21, bf16[5,128,128]{2,1,0:T(8,128)(2,1)S(1)} %copy-done.2, bf16[128,512]{1,0:T(8,128)(2,1)S(1)} %copy-done.3, bf16[48,640]{1,0:T(8,128)(2,1)S(1)} %copy-done.5, ...), custom_call_target="tpu_custom_call" | custom-call | tf_op jit(solution)/shard_map/backward/pallas_call | solution.py:488
  86.1 13.7 %all_to_all.32.parts_ref = bf16[32,48,128]{2,1,0:T(8,128)(2,1)S(1)} all-to-all(bf16[32,48,128]{2,1,0:T(8,128)(2,1)S(1)} %bitcast.17), channel_id=1, replica_groups=mesh['z'=16,'y'=4,'x'=4,'c'=2] {'y','x','c'}, dimensions={0} | all-to-all | bytes 786432 | tf_op jit(solution)/shard_map/reduce_grads/all_to_all | solution.py:421
  99.8 0.1 sum_plane.1
  99.8 21.1 %all_to_all.33.parts_ref = bf16[16,48,128]{2,1,0:T(8,128)(2,1)S(1)} all-to-all(bf16[16,48,128]{2,1,0:T(8,128)(2,1)S(1)} %sum_plane.1), channel_id=1, replica_groups=mesh['z'=16,'y'=4,'x'=4,'c'=2] {'z'}, dimensions={0} | all-to-all | bytes 393216 | tf_op jit(solution)/shard_map/reduce_grads/all_to_all | solution.py:423
  121.0 17.6 %all_to_all.34 = bf16[32,48,128]{2,1,0:T(8,128)(2,1)S(1)} all-to-all(bf16[32,48,128]{2,1,0:T(8,128)(2,1)S(1)} %sum_depth.1), channel_id=1, replica_groups=mesh['z'=16,'y'=4,'x'=4,'c'=2] {'y','x','c'}, dimensions={0} | all-to-all | bytes 786432 | tf_op jit(solution)/shard_map/reduce_grads/all_to_all | solution.py:425
  138.6 0.9 unpack.1
  (11 shorter events, 0.1 us)
Async XLA Ops:
  0.6 79.7 %copy-start.3 = (bf16[128,512]{1,0:T(8,128)(2,1)S(1)}, bf16[128,512]{1,0:T(8,128)(2,1)}, u32[]{:S(2)}) copy-start(bf16[128,512]{1,0:T(8,128)(2,1)} %w_gate_ref.1) | copy-start | bytes 393220
  0.7 79.7 %copy-start.2 = (bf16[5,128,128]{2,1,0:T(8,128)(2,1)S(1)}, bf16[5,128,128]{2,1,0:T(8,128)(2,1)}, u32[]{:S(2)}) copy-start(bf16[5,128,128]{2,1,0:T(8,128)(2,1)} %w_deg_ref.1) | copy-start | bytes 491524
  0.7 79.7 %copy-start.1 = (bf16[64,3200]{1,0:T(8,128)(2,1)S(1)}, bf16[64,3200]{1,0:T(8,128)(2,1)}, u32[]{:S(2)}) copy-start(bf16[64,3200]{1,0:T(8,128)(2,1)} %feats_ref.1) | copy-start | bytes 1228804
  0.7 79.7 %copy-start.7 = (s32[64]{0:T(128)S(1)}, s32[64]{0:T(128)}, u32[]{:S(2)}) copy-start(s32[64]{0:T(128)} %param.15) | copy-start | bytes 772
  0.7 61.7 %copy-start.9 = (f32[128]{0:T(128)S(1)}, f32[128]{0:T(128)}, u32[]{:S(2)}) copy-start(f32[128]{0:T(128)} %param.27) | copy-start | bytes 1540
  0.7 61.7 %copy-start.8 = (f32[128]{0:T(128)S(1)}, f32[128]{0:T(128)}, u32[]{:S(2)}) copy-start(f32[128]{0:T(128)} %param.26) | copy-start | bytes 1540
  0.7 61.7 %copy-start.6 = (f32[128,128]{1,0:T(8,128)S(1)}, f32[128,128]{1,0:T(8,128)}, u32[]{:S(2)}) copy-start(f32[128,128]{1,0:T(8,128)} %w_hidden_ref.1) | copy-start | bytes 196612
  2.2 60.1 %copy-start.4 = (f32[32,2,128]{2,1,0:T(2,128)S(1)}, f32[32,2,128]{2,1,0:T(2,128)}, u32[]{:S(2)}) copy-start(f32[32,2,128]{2,1,0:T(2,128)} %pack.1.pack_ref) | copy-start | bytes 98308
  2.3 16.1 %collective-permute-start = (f32[32,2,128]{2,1,0:T(2,128)}, f32[32,2,128]{2,1,0:T(2,128)S(1)}, u32[]{:S(2)}, u32[]{:S(2)}) collective-permute-start(f32[32,2,128]{2,1,0:T(2,128)} %pack.1.pack_ref), channel_id=1, source_target_pairs={{0,496},{8,504},{16,32},{24,40},{32,16},{40,24},{48,64},{56,72},{6... | collective-permute-start | bytes 98312 | tf_op jit(solution)/shard_map/exchange_pairs/ppermute | solution.py:409
  19.9 9.6 %all-to-all-start = ((f32[4,2,32,2,128]{4,3,2,1,0:T(2,128)}), f32[4,2,32,2,128]{4,3,2,1,0:T(2,128)}, u32[]{:S(2)}, u32[]{:S(2)}) async-start(f32[4,2,32,2,128]{4,3,2,1,0:T(2,128)} %broadcast_in_dim.4), calls=%async_computation | async-start | bytes 524288 | tf_op jit(solution)/shard_map/gather_pairs/all_to_all | solution.py:414
  26.3 54.1 %copy-start.5 = (bf16[48,640]{1,0:T(8,128)(2,1)S(1)}, bf16[48,640]{1,0:T(8,128)(2,1)}, u32[]{:S(2)}) copy-start(bf16[48,640]{1,0:T(8,128)(2,1)} %get-tuple-element.27.split_hbm.split_ref) | copy-start | bytes 184324
  34.8 45.6 %copy-start = (bf16[688,1280]{1,0:T(8,128)(2,1)S(1)}, bf16[688,1280]{1,0:T(8,128)(2,1)}, u32[]{:S(2)}) copy-start(bf16[688,1280]{1,0:T(8,128)(2,1)} %get-tuple-element.34.sums_hbm) | copy-start | bytes 5283844
  54.3 8.1 %collective-permute-start.1 = (f32[2,16,128]{2,1,0:T(8,128)S(1)}, f32[2,16,128]{2,1,0:T(8,128)S(1)}, u32[]{:S(2)}, u32[]{:S(2)}) collective-permute-start(f32[2,16,128]{2,1,0:T(8,128)S(1)} %sum_sources.1.mine_ref), channel_id=1, source_target_pairs={{0,496},{8,504},{16,32},{24,40},{32,16},{40,24},{48,64},{56,72},{6... | collective-permute-start | bytes 49160 | tf_op jit(solution)/shard_map/exchange_sums/ppermute | solution.py:409

commit v4 on v3

--- a/solution.py
+++ b/solution.py
@@ -139,7 +139,15 @@
     return place, jnp.where(jnp.logical_or(below, above), 1, 0)
 
 
-def pack_kernel(harm_hbm, dist_hbm, nbr_hbm, target_hbm, pack_ref, nbr_ref, target_ref, sems):
+def pack_place(delta):
+    row = lax.axis_index("y") + delta
+    return jnp.where(jnp.logical_or(row < 0, row > 3), 4 if abs(delta) == 2 else 5, row)
+
+
+def pack_kernel(
+    harm_hbm, dist_hbm, nbr_hbm, target_hbm, pack_hbm, copies_hbm,
+    pack_ref, nbr_ref, target_ref, sems, out_sems,
+):
     copies = started(
         (
             (harm_hbm, pack_ref.at[pl.ds(0, COMPS)]),
@@ -154,16 +162,21 @@
     pack_ref[COMPS + 1] = nbr_ref[...].astype(F32)
     pack_ref[COMPS + 2] = jnp.broadcast_to(target_ref[...], (SLOTS, PROBES))
     pack_ref[COMPS + 3 :] = jnp.zeros((FIELDS - COMPS - 3, SLOTS, PROBES), F32)
+    targets = [pack_hbm] + [copies_hbm.at[row] for row in range(copies_hbm.shape[0])]
+    for write in started([(pack_ref, target) for target in targets], out_sems):
+        write.wait()
 
 
 def pair_kernel(
-    packs_hbm, rows_hbm, owners_hbm, split_hbm, out_hbm, spread_hbm, sums_hbm,
-    packs_ref, rows_ref, owners_ref, split_ref, sems,
+    plane_hbm, second_hbm, first_hbm, rows_hbm, owners_hbm, split_hbm,
+    out_hbm, spread_hbm, sums_hbm, packs_ref, rows_ref, owners_ref, split_ref, sems,
     out_ref, spread_ref, sums_ref, out_sems,
 ):
     copies = started(
         (
-            (packs_hbm, packs_ref),
+            (plane_hbm, packs_ref.at[pl.ds(0, 4)]),
+            (second_hbm, packs_ref.at[4]),
+            (first_hbm, packs_ref.at[5]),
             (owners_hbm, owners_ref),
             (split_hbm, split_ref),
             (rows_hbm, rows_ref),
@@ -172,19 +185,19 @@
     )
     shards, chunk = out_ref.shape[1], out_ref.shape[3]
     out_ref[...] = jnp.zeros(out_ref.shape, F32)
-    copies[0].wait()
+    for copy in copies[:3]:
+        copy.wait()
     sub = lax.broadcasted_iota(jnp.int32, (ATOMS, PROBES), 0).astype(F32)
-    dists, places = [], []
+    dists = []
     for source in range(SOURCES):
-        place, part = plane_place(DELTAS[source])
-        places.append((place, part))
+        where = pack_place(DELTAS[source])
         if source == 1:
-            copies[1].wait()
+            copies[3].wait()
         for slot in range(SLOTS):
             start = source * SPAN + slot * PROBES
 
             def row(field):
-                return packs_ref[place, part, field, slot : slot + 1, :]
+                return packs_ref[where, field, slot : slot + 1, :]
 
             hot = (row(COMPS + 1) - float(source * ATOMS) == sub).astype(F32)
             if source > 0:
@@ -202,8 +215,8 @@
     basis = jnp.sin(phase * orders) * envelope
     basis_split = stacked(basis, (0, 1, 0, 1, 2, 0))
     sums_ref[DEGREES * CHANS :, :] = basis_split
-    copies[2].wait()
-    copies[3].wait()
+    copies[4].wait()
+    copies[5].wait()
     total = None
     for degree in range(DEGREES):
         low, high = first_rows(degree)
@@ -215,7 +228,7 @@
     for source in range(SOURCES):
         start = source * SPAN
         value = (total[:, start : start + PROBES] + total[:, start + PROBES : start + SPAN]).T
-        place, part = places[source]
+        place, part = plane_place(DELTAS[source])
         for shard in range(shards):
             out_ref[place, shard, part] = value[shard * chunk : (shard + 1) * chunk, :]
     writes += started(
@@ -243,9 +256,24 @@
 
 
 def readout_kernel(
-    scale, mine_ref, theirs_ref, pack_ref, their_pack_ref, w_hidden_ref, b_hidden_ref, w_out_ref,
-    up_ref, head_ref, column_ref,
+    scale, mine_hbm, theirs_hbm, pack_hbm, their_pack_hbm, w_hidden_hbm, b_hidden_hbm, w_out_hbm,
+    up_ref, head_ref, density_ref, column_ref,
+    mine_ref, theirs_ref, target_ref, w_hidden_ref, b_hidden_ref, w_out_ref, sems,
 ):
+    copies = started(
+        (
+            (mine_hbm, mine_ref),
+            (theirs_hbm, theirs_ref),
+            (pack_hbm.at[COMPS + 2], target_ref.at[0]),
+            (their_pack_hbm.at[COMPS + 2], target_ref.at[1]),
+            (w_hidden_hbm, w_hidden_ref),
+            (b_hidden_hbm, b_hidden_ref),
+            (w_out_hbm, w_out_ref),
+        ),
+        sems,
+    )
+    for copy in copies:
+        copy.wait()
     chunk = mine_ref.shape[1]
     shard = lax.axis_index("x") * lax.axis_size("c") + lax.axis_index("c")
     start = pl.multiple_of(shard * chunk, chunk)
@@ -253,8 +281,8 @@
         [mine_ref[0] + theirs_ref[1], theirs_ref[0] + mine_ref[1]], axis=0
     )
     targets = []
-    for ref in (pack_ref, their_pack_ref):
-        column_ref[...] = jnp.broadcast_to(ref[COMPS + 2, 0:1, :], (PROBES, PROBES)).T
+    for side in range(2):
+        column_ref[...] = jnp.broadcast_to(target_ref[side, 0:1, :], (PROBES, PROBES)).T
         targets.append(column_ref[pl.ds(start, chunk), :])
     target = jnp.concatenate(targets, axis=0)
     w_hidden = w_hidden_ref[...]
@@ -267,9 +295,11 @@
     pre_grad = w_out * silu_slope(hidden_pre) * error_grad
     spot = lax.broadcasted_iota(jnp.int32, (chunk, PROBES), 0) + start
     mask = (spot == lax.broadcasted_iota(jnp.int32, (chunk, PROBES), 1)).astype(F32)
-    up_ref[0 : 2 * chunk, :] = along_last(pre_grad, w_hidden, PRECISE)
+    upstream = along_last(pre_grad, w_hidden, PRECISE)
+    for copy in range(up_ref.shape[0]):
+        up_ref[copy] = upstream
     density_row = jnp.sum(mask * density[0:chunk, :], axis=0, keepdims=True)
-    up_ref[2 * chunk :, :] = jnp.broadcast_to(density_row, (8, PROBES))
+    density_ref[...] = density_row
     mine, own_error = pre_grad[0:chunk, :], error[0:chunk, :]
     head_ref[0:CHANS, :] = along_first(summed[0:chunk, :], mine, PRECISE)
     bias = jnp.sum(mine, axis=0, keepdims=True)
@@ -280,16 +310,33 @@
     )
 
 
+def own_slab():
+    return lax.axis_index("z") * 4 + lax.axis_index("y")
+
+
 def backward_kernel(
-    feats_ref, species_ref, w_deg_ref, w_gate_ref, split_ref, head_ref, up_ref,
-    spread_hbm, sums_hbm, payload_ref, density_ref, spread_ref, sums_ref, sems,
+    up_hbm, split_hbm, sums_hbm, feats_hbm, w_deg_hbm, w_gate_hbm, species_hbm, head_hbm,
+    density_hbm, spread_hbm, payload_ref,
+    up_ref, split_ref, sums_ref, feats_ref, w_deg_ref, w_gate_ref, species_ref, head_ref,
+    density_ref, spread_ref, sems,
 ):
     spreads = [pl.ds(low, high - low) for low, high in map(first_rows, range(DEGREES))]
     copies = started(
-        [(sums_hbm, sums_ref)]
+        [
+            (up_hbm, up_ref),
+            (split_hbm, split_ref),
+            (sums_hbm, sums_ref),
+            (feats_hbm, feats_ref),
+            (w_deg_hbm, w_deg_ref),
+            (w_gate_hbm, w_gate_ref),
+            (species_hbm, species_ref),
+            (head_hbm, head_ref),
+            (density_hbm, density_ref),
+        ]
         + [(spread_hbm.at[part], spread_ref.at[part]) for part in spreads],
         sems,
     )
+    copies[0].wait()
     shards = up_ref.shape[1]
     chunk = PROBES // shards
     blocks = []
@@ -301,21 +348,17 @@
         ).T
         blocks += [block] * SLOTS
     upstream = jnp.concatenate(blocks, axis=1)
-    density = None
-    for shard in range(shards):
-        row = up_ref[lax.axis_index("y"), shard, 2 * chunk : 2 * chunk + 1, :]
-        density = row if density is None else density + row
-    density_ref[...] = density
+    for copy in copies[1:9]:
+        copy.wait()
     scalar = feats_ref[:, lanes(0)]
     gates = jax.nn.sigmoid(matmul(scalar, w_gate_ref[...]))
-    copies[0].wait()
     basis_split = sums_ref[DEGREES * CHANS :, :]
     radial_grads = []
     for degree in range(DEGREES):
         low, high = first_rows(degree)
         radial = along_first(split_ref[:, lanes(degree)], basis_split)
         inner = (radial * upstream).astype(BF16)
-        copies[1 + degree].wait()
+        copies[9 + degree].wait()
         grads = along_last(spread_ref[low:high, :], inner)
         product = (sums_ref[lanes(degree), :].astype(F32) * upstream).astype(BF16)
         both = along_last(product, basis_split[0 : 2 * BASES, :])
@@ -345,11 +388,16 @@
         radial_grads + [embed_grad], axis=0
     ).astype(BF16)
     base += 48
-    payload_ref[base:, :] = jnp.zeros((PAYLOAD - base, CHANS), BF16)
+    slabs = (PAYLOAD - base) // 3
+    here = lax.broadcasted_iota(jnp.int32, (slabs, PROBES), 0) == own_slab()
+    for part in parts_of(jnp.where(here, density_ref[...], 0.0)):
+        payload_ref[base : base + slabs, :] = part
+        base += slabs
 
 
 def unpack_kernel(
-    payload_ref, loss_ref, deg_ref, gate_ref, embed_ref, radial_ref, hidden_ref, bias_ref, out_ref
+    payload_ref, loss_ref, density_ref, deg_ref, gate_ref, embed_ref, radial_ref, hidden_ref,
+    bias_ref, out_ref,
 ):
     for degree in range(DEGREES):
         deg_ref[degree] = payload_ref[lanes(degree), :].astype(F32)
@@ -367,6 +415,15 @@
     for degree in range(DEGREES):
         radial_ref[:, lanes(degree)] = small[degree * BASES : (degree + 1) * BASES, :]
     embed_ref[...] = small[DEGREES * BASES :, :]
+    base += 48
+    slabs = (PAYLOAD - base) // 3
+    total = None
+    for _ in range(3):
+        part = payload_ref[base : base + slabs, :].astype(F32)
+        total = part if total is None else total + part
+        base += slabs
+    here = lax.broadcasted_iota(jnp.int32, (slabs, PROBES), 0) == own_slab()
+    density_ref[...] = jnp.sum(jnp.where(here, total, 0.0), axis=0, keepdims=True)
 
 
 def shape(dims, dtype=F32):
@@ -389,29 +446,22 @@
     ]
 
 
-def call_apart(kernel, outs, name, *operands, outside=False):
-    far = pl.BlockSpec(memory_space=pltpu.HBM)
-    options = {"out_specs": [far] * len(outs)} if outside else {}
+def call_apart(kernel, outs, name, *operands):
     return call(
         kernel,
         outs,
         name,
         limit=LIMIT,
-        in_specs=[far] * len(operands),
-        scratch_shapes=staging(operands) + (staging(outs) if outside else []),
-        **options,
+        in_specs=[pl.BlockSpec(memory_space=pl.ANY)] * len(operands),
+        scratch_shapes=staging(operands),
     )(*operands)
 
 
-def to_partner(block):
+def to_partner(block, distance=2):
     count = lax.axis_size(SLAB)
-    route = [(i, (i + (2 if i % 4 >= 2 else -2)) % count) for i in range(count)]
+    steps = (-2, -2, 2, 2) if distance == 2 else (-1, 1, -1, 1)
+    route = [(i, (i + steps[i % 4]) % count) for i in range(count)]
     return lax.ppermute(block, SLAB, route)
-
-
-def to_all(block, axes):
-    count = lax.axis_size(axes)
-    return lax.all_to_all(jnp.broadcast_to(block[None], (count,) + block.shape), axes, 0, 0)
 
 
 def reduce_all(payload):
@@ -434,20 +484,28 @@
     chunk = PROBES // shards
     scale = 1.0 / math.sqrt(PROBES * slab_count)
     species = species.reshape(1, ATOMS)
-    pack = call(
+    far = pl.BlockSpec(memory_space=pl.ANY)
+    field_shape = (FIELDS, SLOTS, PROBES)
+    pack, copies = call(
         pack_kernel,
-        shape((FIELDS, SLOTS, PROBES)),
+        [shape(field_shape), shape((4,) + field_shape)],
         "pack",
         limit=LIMIT,
-        in_specs=[pl.BlockSpec(memory_space=pltpu.HBM)] * 4,
+        in_specs=[far] * 4,
+        out_specs=[far] * 2,
         scratch_shapes=[
+            pltpu.VMEM(field_shape, F32),
             pltpu.VMEM((SLOTS, PROBES), jnp.int32),
             pltpu.VMEM((1, PROBES), F32),
             pltpu.SemaphoreType.DMA((4,)),
+            pltpu.SemaphoreType.DMA((5,)),
         ],
     )(harmonics, distances, neighbours, target.reshape(1, PROBES))
+    with jax.named_scope("gather_pairs"):
+        packs = lax.all_to_all(copies, "y", 0, 0)
     with jax.named_scope("exchange_pairs"):
-        their_pack = to_partner(pack)
+        their_pack = to_partner(pack, 2)
+        next_pack = to_partner(pack, 1)
     rows, owners, split = call_apart(
         encode_kernel,
         [
@@ -458,50 +516,75 @@
         "encode",
         atom_feats, species, w_deg, w_gate, embed, send_rows[0, 0], w_radial,
     )
-    with jax.named_scope("gather_pairs"):
-        packs = to_all(jnp.stack([pack, their_pack]), "y")
     held = [
         shape((4, shards, 2, chunk, CHANS)),
         shape((COMPS * ATOMS, PAIRS), BF16),
         shape((DEGREES * CHANS + 6 * BASES, PAIRS), BF16),
     ]
-    values, spread, sums = call_apart(
-        pair_kernel, held, "pair_sums", packs, rows, owners, split, outside=True
-    )
+    operands = (packs, their_pack, next_pack, rows, owners, split)
+    values, spread, sums = call(
+        pair_kernel,
+        held,
+        "pair_sums",
+        limit=LIMIT,
+        in_specs=[far] * len(operands),
+        out_specs=[far] * len(held),
+        scratch_shapes=[pltpu.VMEM((6,) + field_shape, F32)]
+        + [pltpu.VMEM(operand.shape, operand.dtype) for operand in (rows, owners, split)]
+        + [pltpu.SemaphoreType.DMA((len(operands),))]
+        + staging(held),
+    )(*operands)
     with jax.named_scope("scatter_sums"):
         parts = lax.all_to_all(values.reshape(4 * shards, 2, chunk, CHANS), PLANE, 0, 0)
     mine = call(sum_kernel, shape((2, chunk, CHANS)), "sum_sources")(parts)
     with jax.named_scope("exchange_sums"):
         theirs = to_partner(mine)
-    up, head = call(
-        functools.partial(readout_kernel, scale),
-        [shape((2 * chunk + 8, CHANS)), shape((CHANS + 16, CHANS))],
-        "readout",
-        scratch_shapes=[pltpu.VMEM((PROBES, PROBES), F32)],
-    )(
+    operands = (
         mine, theirs, pack, their_pack, w_hidden, b_hidden.reshape(1, CHANS),
         w_out.reshape(1, CHANS),
     )
+    up, head, density_row = call(
+        functools.partial(readout_kernel, scale),
+        [
+            shape((4 * shards, 2 * chunk, CHANS)),
+            shape((CHANS + 16, CHANS)),
+            shape((1, PROBES)),
+        ],
+        "readout",
+        limit=LIMIT,
+        in_specs=[far] * len(operands),
+        scratch_shapes=[
+            pltpu.VMEM((PROBES, PROBES), F32),
+            pltpu.VMEM(mine.shape, F32),
+            pltpu.VMEM(theirs.shape, F32),
+            pltpu.VMEM((2, SLOTS, PROBES), F32),
+            pltpu.VMEM((CHANS, CHANS), F32),
+            pltpu.VMEM((1, CHANS), F32),
+            pltpu.VMEM((1, CHANS), F32),
+            pltpu.SemaphoreType.DMA((len(operands),)),
+        ],
+    )(*operands)
     with jax.named_scope("gather_grads"):
-        ups = to_all(up, PLANE).reshape(4, shards, 2 * chunk + 8, CHANS)
-    near, far = pl.BlockSpec(memory_space=pltpu.VMEM), pl.BlockSpec(memory_space=pltpu.HBM)
-    payload, density = call(
+        ups = lax.all_to_all(up, PLANE, 0, 0).reshape(4, shards, 2 * chunk, CHANS)
+    operands = (
+        ups, split, sums, atom_feats, w_deg, w_gate, species, head, density_row, spread
+    )
+    payload = call(
         backward_kernel,
-        [shape((PAYLOAD, CHANS), BF16), shape((1, PROBES))],
+        shape((PAYLOAD, CHANS), BF16),
         "backward",
-        in_specs=[near] * 7 + [far] * 2,
-        scratch_shapes=[
-            pltpu.VMEM(spread.shape, BF16),
-            pltpu.VMEM(sums.shape, BF16),
-            pltpu.SemaphoreType.DMA((1 + DEGREES,)),
-        ],
-    )(atom_feats, species, w_deg, w_gate, split, head, ups, spread, sums)
+        limit=LIMIT,
+        in_specs=[far] * len(operands),
+        scratch_shapes=[pltpu.VMEM(operand.shape, operand.dtype) for operand in operands]
+        + [pltpu.SemaphoreType.DMA((len(operands) - 1 + DEGREES,))],
+    )(*operands)
     with jax.named_scope("reduce_grads"):
         payload = reduce_all(payload)
-    loss, deg, gate, embed_grad, radial_grad, hidden, bias, out = call(
+    loss, density, deg, gate, embed_grad, radial_grad, hidden, bias, out = call(
         unpack_kernel,
         [
             shape((1, 1)),
+            shape((1, PROBES)),
             shape((DEGREES, CHANS, CHANS)),
             shape((CHANS, (DEGREES - 1) * CHANS)),
             shape((KINDS, CHANS)),

time: 140 us -> 142 us (1.014)
  Pallas kernels: 16.4 us -> 19.7 us
  blocking collectives: 89.2 us -> 86.4 us
  waiting for transfers between devices: 6.85 us -> 8.35 us
    ppermute x2 -> x3, waiting for transfers between devices: 3.59 us -> 8.35 us  [to_partner(): return lax.ppermute(block, SLAB, route)]
    pallas_call x6, Pallas kernels: 16.2 us -> 19.6 us  [the longest x1 7.27 us: on_device(): call(backward_kernel, shape((PAYLOAD, CHANS), BF16), 'backward', limit=LI...]
    all_to_all x1, waiting for transfers between devices: 3.26 us -> 0.01 us  [on_device(): packs = lax.all_to_all(copies, 'y', 0, 0)]
    all_to_all x1, blocking collectives: 21.1 us -> 18.4 us  [reduce_all(): parts = lax.all_to_all(copies, 'z', 0, 0)]
    ppermute x2 -> x3, starting transfers between devices: 20.6 us -> 19.4 us  [to_partner(): return lax.ppermute(block, SLAB, route)]
  transfers between devices with their start and end apart: 3 -> 4, of which waited for: 3 -> 2; matrix products, arithmetic and copies ran while one was open for 0% -> 0% of each run, Pallas kernels for 2% -> 2%
where the time goes in v4:
time: 142 us; the launch traced here: 141 us
  blocking collectives  86.4 us (61%)
  starting transfers between devices  24.4 us (17%)
  Pallas kernels  19.7 us (14%)
  waiting for transfers between devices  8.35 us (6%)
    ppermute x3, starting transfers between devices, to_partner(): return lax.ppermute(block, SLAB, route)  19.4 us
    all_to_all x1, blocking collectives, on_device(): lax.all_to_all(values.reshape(4 * shards, 2, chunk, CHANS), PLANE, 0, 0)  18.7 us
    all_to_all x1, blocking collectives, reduce_all(): parts = lax.all_to_all(copies, 'z', 0, 0)  18.4 us
    all_to_all x1, blocking collectives, reduce_all(): return lax.all_to_all(copies, PLANE, 0, 0).reshape(PAYLOAD, CHANS)  17.6 us
    all_to_all x1, blocking collectives, on_device(): ups = lax.all_to_all(up, PLANE, 0, 0).reshape(4, shards, 2 * chunk, CHANS)  17.5 us
    all_to_all x1, blocking collectives, reduce_all(): parts = lax.all_to_all(payload.reshape(count, rows, CHANS), PLANE, 0, 0)  14.3 us
    ppermute x3, waiting for transfers between devices, to_partner(): return lax.ppermute(block, SLAB, route)  8.35 us
    pallas_call x1, Pallas kernels, on_device(): call(backward_kernel, shape((PAYLOAD, CHANS), BF16), 'backward', limit=LI...  7.27 us
  transfers between devices with their start and end apart: 4, of which 2 were waited for; matrix products, arithmetic and copies ran while one was open for 0% of the time, Pallas kernels for 2%

profile of v4, /device:TPU:1, one launch (start us, length us, event | category | flops | bytes accessed | tf_op | source)
XLA Modules:
  0.0 140.9 jit_solution(5978783754107436320)
XLA Ops:
  0.6 1.5 %pack.1 = (f32[32,2,128]{2,1,0:T(2,128)}, f32[4,32,2,128]{3,2,1,0:T(2,128)}) custom-call(f32[25,2,128]{2,1,0:T(2,128)} %harm_hbm.1, f32[2,128]{1,0:T(2,128)} %dist_hbm.1, s32[2,128]{1,0:T(2,128)} %nbr_hbm.1, f32[1,128]{1,0:T(1,128)} %bitcast.20), custom_call_target="tpu_custom_call" | custom-call | tf_op jit(solution)/shard_map/pack/pallas_call | solution.py:489
  2.1 5.0 %all-to-all-start = ((f32[4,32,2,128]{3,2,1,0:T(2,128)}), f32[4,32,2,128]{3,2,1,0:T(2,128)S(1)}, u32[]{:S(2)}, u32[]{:S(2)}) async-start(f32[4,32,2,128]{3,2,1,0:T(2,128)} %get-tuple-element.29), calls=%async_computation | async-start | bytes 262144 | tf_op jit(solution)/shard_map/gather_pairs/all_to_all | solution.py:505
  7.2 13.5 %collective-permute-start.1 = (f32[32,2,128]{2,1,0:T(2,128)}, f32[32,2,128]{2,1,0:T(2,128)S(1)}, u32[]{:S(2)}, u32[]{:S(2)}) collective-permute-start(f32[32,2,128]{2,1,0:T(2,128)} %get-tuple-element.30.pack_hbm), channel_id=1, source_target_pairs={{0,504},{8,16},{16,8},{24,32},{32,24},{40,48},{48,40},{56,64},{64,... | collective-permute-start | bytes 98312 | tf_op jit(solution)/shard_map/exchange_pairs/ppermute | solution.py:464
  20.7 2.5 %collective-permute-start = (f32[32,2,128]{2,1,0:T(2,128)}, f32[32,2,128]{2,1,0:T(2,128)S(1)}, u32[]{:S(2)}, u32[]{:S(2)}) collective-permute-start(f32[32,2,128]{2,1,0:T(2,128)} %get-tuple-element.30.pack_hbm), channel_id=1, source_target_pairs={{0,496},{8,504},{16,32},{24,40},{32,16},{40,24},{48,64},{56,72},{6... | collective-permute-start | bytes 98312 | tf_op jit(solution)/shard_map/exchange_pairs/ppermute | solution.py:464
  23.2 2.3 %encode.1 = (bf16[1600,128]{1,0:T(8,128)(2,1)}, bf16[4,64,64]{2,1,0:T(8,128)(2,1)}, bf16[48,640]{1,0:T(8,128)(2,1)}) custom-call(bf16[64,3200]{1,0:T(8,128)(2,1)} %feats_hbm.3, s32[1,64]{1,0:T(1,128)} %bitcast.18, bf16[5,128,128]{2,1,0:T(8,128)(2,1)} %w_deg_hbm.3, bf16[128,512]{1,0:T(8,128)(2,1)} %w_gate_hbm.3, f32[8,128]{1,0:T(8,128)} %embed_hbm.1, ...), custom_call_target="tpu_custom_call" | custom-call | tf_op jit(solution)/shard_map/encode/pallas_call | solution.py:450
  25.5 0.0 collective-permute-done.1.first_hbm
  25.5 0.0 copy-start.3
  25.5 3.7 %collective-permute-done.second_hbm.their_pack_hbm = f32[32,2,128]{2,1,0:T(2,128)S(1)} collective-permute-done((f32[32,2,128]{2,1,0:T(2,128)}, f32[32,2,128]{2,1,0:T(2,128)S(1)}, u32[]{:S(2)}, u32[]{:S(2)}) %collective-permute-start) | collective-permute-done | bytes 32800 | tf_op jit(solution)/shard_map/exchange_pairs/ppermute | solution.py:464
  29.1 0.0 copy-start.2
  29.2 0.0 all-to-all-done.plane_hbm
  29.2 0.0 copy-start.1
  29.2 0.0 copy-done.3
  29.2 0.6 copy-done.2
  29.8 0.1 copy-done.1
  29.8 5.2 %pair_sums.1 = (f32[4,8,2,16,128]{4,3,2,1,0:T(8,128)}, bf16[1600,1280]{1,0:T(8,128)(2,1)}, bf16[688,1280]{1,0:T(8,128)(2,1)}) custom-call(f32[4,32,2,128]{3,2,1,0:T(2,128)} %copy-done.1, f32[32,2,128]{2,1,0:T(2,128)} %copy-done.2, f32[32,2,128]{2,1,0:T(2,128)} %copy-done.3, bf16[1600,128]{1,0:T(8,128)(2,1)} %get-tuple-element.31.rows_hbm, ...), custom_call_target="tpu_custom_call" | custom-call | tf_op jit(solution)/shard_map/pair_sums/pallas_call | solution.py:525
  35.0 18.7 %all_to_all.30.parts_ref = f32[32,2,16,128]{3,2,1,0:T(8,128)S(1)} all-to-all(f32[32,2,16,128]{3,2,1,0:T(8,128)} %bitcast.16), channel_id=1, replica_groups=mesh['z'=16,'y'=4,'x'=4,'c'=2] {'y','x','c'}, dimensions={0} | all-to-all | bytes 1048576 | tf_op jit(solution)/shard_map/scatter_sums/all_to_all | solution.py:538
  53.8 0.0 copy-start
  53.8 3.4 %collective-permute-start.2 = (f32[2,16,128]{2,1,0:T(8,128)S(1)}, f32[2,16,128]{2,1,0:T(8,128)S(1)}, u32[]{:S(2)}, u32[]{:S(2)}) collective-permute-start(f32[2,16,128]{2,1,0:T(8,128)S(1)} %sum_sources.1.mine_hbm), channel_id=1, source_target_pairs={{0,496},{8,504},{16,32},{24,40},{32,16},{40,24},{48,64},{56,72},{6... | collective-permute-start | bytes 49160 | tf_op jit(solution)/shard_map/exchange_sums/ppermute | solution.py:464
  57.2 4.7 %collective-permute-done.2.theirs_hbm = f32[2,16,128]{2,1,0:T(8,128)S(1)} collective-permute-done((f32[2,16,128]{2,1,0:T(8,128)S(1)}, f32[2,16,128]{2,1,0:T(8,128)S(1)}, u32[]{:S(2)}, u32[]{:S(2)}) %collective-permute-start.2) | collective-permute-done | bytes 16416 | tf_op jit(solution)/shard_map/exchange_sums/ppermute | solution.py:464
  61.9 0.0 copy-start.4
  61.9 0.0 copy-done
  61.9 0.6 copy-done.4
  62.5 2.4 %readout.1 = (f32[32,32,128]{2,1,0:T(8,128)}, f32[144,128]{1,0:T(8,128)}, f32[1,128]{1,0:T(1,128)}) custom-call(f32[2,16,128]{2,1,0:T(8,128)} %copy-done, f32[2,16,128]{2,1,0:T(8,128)} %copy-done.4, f32[32,2,128]{2,1,0:T(2,128)} %get-tuple-element.30.pack_hbm, f32[32,2,128]{2,1,0:T(2,128)} %copy-done.2, f32[128,128]{1,0:T(8,128)} %w_hidden_hbm.1, ...), custom_call_target="tpu_custom_call" | custom-call | tf_op jit(solution)/shard_map/readout/pallas_call | solution.py:546
  64.9 17.5 %all_to_all.31 = f32[32,32,128]{2,1,0:T(8,128)} all-to-all(f32[32,32,128]{2,1,0:T(8,128)} %get-tuple-element.35), channel_id=1, replica_groups=mesh['z'=16,'y'=4,'x'=4,'c'=2] {'y','x','c'}, dimensions={0} | all-to-all | bytes 1048576 | tf_op jit(solution)/shard_map/gather_grads/all_to_all | solution.py:568
  82.4 7.3 %backward.1 = bf16[1536,128]{1,0:T(8,128)(2,1)} custom-call(f32[4,8,32,128]{3,2,1,0:T(8,128)} %bitcast.14, bf16[48,640]{1,0:T(8,128)(2,1)} %get-tuple-element.33.split_hbm, bf16[688,1280]{1,0:T(8,128)(2,1)} %get-tuple-element.36.sums_hbm, bf16[64,3200]{1,0:T(8,128)(2,1)} %feats_hbm.3, bf16[5,128,128]{2,1,0:T(8,128)(2,1)} %w_deg_hbm.3, ...), custom_call_target="tpu_custom_call" | custom-call | tf_op jit(solution)/shard_map/backward/pallas_call | solution.py:572
  89.7 14.3 %all_to_all.32.parts_ref = bf16[32,48,128]{2,1,0:T(8,128)(2,1)S(1)} all-to-all(bf16[32,48,128]{2,1,0:T(8,128)(2,1)} %bitcast.15), channel_id=1, replica_groups=mesh['z'=16,'y'=4,'x'=4,'c'=2] {'y','x','c'}, dimensions={0} | all-to-all | bytes 786432 | tf_op jit(solution)/shard_map/reduce_grads/all_to_all | solution.py:471
  104.0 0.1 sum_plane.1
  104.0 18.4 %all_to_all.33.parts_ref = bf16[16,48,128]{2,1,0:T(8,128)(2,1)S(1)} all-to-all(bf16[16,48,128]{2,1,0:T(8,128)(2,1)S(1)} %sum_plane.1), channel_id=1, replica_groups=mesh['z'=16,'y'=4,'x'=4,'c'=2] {'z'}, dimensions={0} | all-to-all | bytes 393216 | tf_op jit(solution)/shard_map/reduce_grads/all_to_all | solution.py:473
  122.4 17.6 %all_to_all.34 = bf16[32,48,128]{2,1,0:T(8,128)(2,1)S(1)} all-to-all(bf16[32,48,128]{2,1,0:T(8,128)(2,1)S(1)} %sum_depth.1), channel_id=1, replica_groups=mesh['z'=16,'y'=4,'x'=4,'c'=2] {'y','x','c'}, dimensions={0} | all-to-all | bytes 786432 | tf_op jit(solution)/shard_map/reduce_grads/all_to_all | solution.py:475
  140.1 0.9 unpack.1
  (2 shorter events, 0.1 us)
Async XLA Ops:
  2.1 27.0 %all-to-all-start = ((f32[4,32,2,128]{3,2,1,0:T(2,128)}), f32[4,32,2,128]{3,2,1,0:T(2,128)S(1)}, u32[]{:S(2)}, u32[]{:S(2)}) async-start(f32[4,32,2,128]{3,2,1,0:T(2,128)} %get-tuple-element.29), calls=%async_computation | async-start | bytes 262144 | tf_op jit(solution)/shard_map/gather_pairs/all_to_all | solution.py:505
  7.2 18.3 %collective-permute-start.1 = (f32[32,2,128]{2,1,0:T(2,128)}, f32[32,2,128]{2,1,0:T(2,128)S(1)}, u32[]{:S(2)}, u32[]{:S(2)}) collective-permute-start(f32[32,2,128]{2,1,0:T(2,128)} %get-tuple-element.30.pack_hbm), channel_id=1, source_target_pairs={{0,504},{8,16},{16,8},{24,32},{32,24},{40,48},{48,40},{56,64},{64,... | collective-permute-start | bytes 98312 | tf_op jit(solution)/shard_map/exchange_pairs/ppermute | solution.py:464
  20.7 8.5 %collective-permute-start = (f32[32,2,128]{2,1,0:T(2,128)}, f32[32,2,128]{2,1,0:T(2,128)S(1)}, u32[]{:S(2)}, u32[]{:S(2)}) collective-permute-start(f32[32,2,128]{2,1,0:T(2,128)} %get-tuple-element.30.pack_hbm), channel_id=1, source_target_pairs={{0,496},{8,504},{16,32},{24,40},{32,16},{40,24},{48,64},{56,72},{6... | collective-permute-start | bytes 98312 | tf_op jit(solution)/shard_map/exchange_pairs/ppermute | solution.py:464
  25.5 3.7 %copy-start.3 = (f32[32,2,128]{2,1,0:T(2,128)}, f32[32,2,128]{2,1,0:T(2,128)S(1)}, u32[]{:S(2)}) copy-start(f32[32,2,128]{2,1,0:T(2,128)S(1)} %collective-permute-done.1.first_hbm) | copy-start | bytes 98308
  29.1 0.6 copy-start.2
  29.2 0.7 copy-start.1
  53.8 8.1 %copy-start = (f32[2,16,128]{2,1,0:T(8,128)}, f32[2,16,128]{2,1,0:T(8,128)S(1)}, u32[]{:S(2)}) copy-start(f32[2,16,128]{2,1,0:T(8,128)S(1)} %sum_sources.1.mine_hbm) | copy-start | bytes 49156
  53.8 8.1 %collective-permute-start.2 = (f32[2,16,128]{2,1,0:T(8,128)S(1)}, f32[2,16,128]{2,1,0:T(8,128)S(1)}, u32[]{:S(2)}, u32[]{:S(2)}) collective-permute-start(f32[2,16,128]{2,1,0:T(8,128)S(1)} %sum_sources.1.mine_hbm), channel_id=1, source_target_pairs={{0,496},{8,504},{16,32},{24,40},{32,16},{40,24},{48,64},{56,72},{6... | collective-permute-start | bytes 49160 | tf_op jit(solution)/shard_map/exchange_sums/ppermute | solution.py:464
  61.9 0.6 copy-start.4

commit v5 on v2

v5 whole, which is shorter than its diff:
```python
import functools
import math

import jax
import jax.numpy as jnp
from jax import lax
from jax.experimental import pallas as pl
from jax.experimental.pallas import tpu as pltpu
from jax.sharding import Mesh, PartitionSpec as P

OFFSETS = (-2, -1, 1, 2)
CUTOFF = 4.0
PRECISE = lax.Precision.HIGHEST
F32 = jnp.float32
BF16 = jnp.bfloat16
SLAB = ("z", "y")
ATOM = ("x", "c")
PLANE = ("y", "x", "c")
DEGREES = 5
COMPS = DEGREES * DEGREES
CHANS = 128
ATOMS = 64
SLOTS = 2
PROBES = 128
SPAN = SLOTS * PROBES
ROWS = 4
HALO = 2
OWN_PAIRS = ROWS * SPAN
HALO_PAIRS = HALO * SPAN
PAIRS = OWN_PAIRS + HALO_PAIRS
FIELDS = 32
BASES = 8
KINDS = 8
PAYLOAD = 1536
LIMIT = 63


def first_rows(degree):
    return degree * degree * ATOMS, (degree + 1) * (degree + 1) * ATOMS


def lanes(block):
    return slice(block * CHANS, (block + 1) * CHANS)


def along_first(left, right, precision=None):
    return lax.dot_general(
        left, right, (((0,), (0,)), ((), ())), preferred_element_type=F32, precision=precision
    )


def along_last(left, right, precision=None):
    return lax.dot_general(
        left, right, (((1,), (1,)), ((), ())), preferred_element_type=F32, precision=precision
    )


def matmul(left, right, precision=None):
    return jnp.dot(left, right, preferred_element_type=F32, precision=precision)


def component_rows(feats_ref, degree):
    parts = [feats_ref[:, lanes(m)] for m in range(degree * degree, (degree + 1) * (degree + 1))]
    return parts[0] if degree == 0 else jnp.concatenate(parts, axis=0)


def over_components(gate, degree):
    return jnp.concatenate([gate] * (2 * degree + 1), axis=0)


def kind_rows(species):
    ids = lax.broadcasted_iota(jnp.int32, (KINDS, ATOMS), 0).astype(F32)
    return (ids == species).astype(F32)


def owner_tables(lists, owners_ref):
    ids = lax.broadcasted_iota(jnp.int32, (ATOMS, ATOMS), 0).astype(F32)
    same = lax.broadcasted_iota(jnp.int32, (ATOMS, ATOMS), 1).astype(F32)
    for index in range(1 + len(OFFSETS)):
        row = same if index == 2 else lists[index - (index > 2)]
        owners_ref[index] = (ids == row).astype(BF16)


def started(pairs, sems):
    copies = [
        pltpu.make_async_copy(source, target, sems.at[index])
        for index, (source, target) in enumerate(pairs)
    ]
    for copy in copies:
        copy.start()
    return copies


def encode_rows(feats_ref, species, w_deg_ref, w_gate_ref, embed_ref, rows_ref):
    scalar = feats_ref[:, lanes(0)]
    gates = jax.nn.sigmoid(matmul(scalar, w_gate_ref[...]))
    for degree in range(DEGREES):
        low, high = first_rows(degree)
        rows = component_rows(feats_ref, degree)
        mixed = matmul(rows, w_deg_ref[degree])
        if degree == 0:
            added = jax.nn.silu(mixed) + along_first(
                kind_rows(species), embed_ref[...], PRECISE
            )
        else:
            added = mixed * over_components(gates[:, lanes(degree - 1)], degree)
        rows_ref[low:high, :] = (rows.astype(F32) + added).astype(BF16)


def encode_kernel(
    feats_ref, species_ref, w_deg_ref, w_gate_ref, embed_ref, lists_ref, w_radial_ref,
    rows_ref, owners_ref, split_ref, w_deg_out_ref, w_gate_out_ref,
):
    w_deg_out_ref[...] = w_deg_ref[...]
    w_gate_out_ref[...] = w_gate_ref[...]
    lists = [lists_ref[which : which + 1, :].astype(F32) for which in range(len(OFFSETS))]
    owner_tables(lists, owners_ref)
    split_ref[...] = stacked(w_radial_ref[...], (0, 0, 1, 1, 0, 2))
    encode_rows(
        feats_ref, species_ref[...].astype(F32), w_deg_ref, w_gate_ref, embed_ref, rows_ref
    )


def parts_of(values):
    high = values.astype(BF16)
    rest = values - high.astype(F32)
    middle = rest.astype(BF16)
    low = (rest - middle.astype(F32)).astype(BF16)
    return high, middle, low


def stacked(values, order):
    parts = [part.astype(F32) for part in parts_of(values)]
    return jnp.concatenate([parts[index] for index in order], axis=0).astype(BF16)


def pack_kernel(
    harm_hbm, dist_hbm, nbr_hbm, feats_hbm, lists_hbm, species_hbm, copies_hbm, atoms_hbm,
    pack_ref, nbr_ref, lists_ref, species_ref, extra_ref, sems, out_sems,
):
    far = atoms_hbm.at[:, pl.ds(0, COMPS * CHANS)]
    copies = started(
        (
            (harm_hbm, pack_ref.at[pl.ds(0, COMPS)]),
            (dist_hbm, pack_ref.at[COMPS]),
            (nbr_hbm, nbr_ref),
            (lists_hbm, lists_ref),
            (species_hbm, species_ref),
            (feats_hbm, far),
        ),
        sems,
    )
    for copy in copies[:5]:
        copy.wait()
    extra = jnp.concatenate(
        [
            lists_ref[...].astype(F32),
            species_ref[...].astype(F32),
            jnp.zeros((CHANS - 1 - len(OFFSETS), ATOMS), F32),
        ],
        axis=0,
    )
    extra_ref[...] = extra.T.astype(BF16)
    pack_ref[COMPS + 1] = nbr_ref[...].astype(F32)
    pack_ref[COMPS + 2 :] = jnp.zeros((FIELDS - COMPS - 2, SLOTS, PROBES), F32)
    writes = started(
        [(extra_ref, atoms_hbm.at[:, pl.ds(COMPS * CHANS, CHANS)])]
        + [(pack_ref, copies_hbm.at[row]) for row in range(ROWS)],
        out_sems,
    )
    for copy in copies[5:] + writes:
        copy.wait()


def plane_halves():
    row = lax.axis_index("y")
    upper = jnp.where(row > 1, 1, 0)
    partner = row + 4 * upper - 2
    return row, 2 * upper, partner


def pair_kernel(
    packs_ref, theirs_ref, rows_ref, owners_ref, split_ref, w_deg_ref, w_gate_ref, embed_ref,
    out_ref, spread_ref, halo_ref, sums_ref, their_rows_ref, their_owners_ref,
):
    shards, chunk = out_ref.shape[1], out_ref.shape[2]
    own_row, first, partner_row = plane_halves()
    sub = lax.broadcasted_iota(jnp.int32, (ATOMS, PROBES), 0).astype(F32)

    def spread_pairs(target_ref, tables_ref, begin, probe_row, atom_row):
        delta = probe_row - atom_row
        valid = jnp.logical_and(delta >= -2, delta <= 2)
        table = jnp.clip(delta + 2, 0, 4)
        block = jnp.where(delta < 0, delta + 3, jnp.where(delta > 0, delta + 2, 0))
        base = jnp.where(valid, block * ATOMS, 1 << 20).astype(F32)
        for slot in range(SLOTS):
            start = begin + slot * PROBES

            def row(field):
                return packs_ref[probe_row, field, slot : slot + 1, :]

            hot = (row(COMPS + 1) - base == sub).astype(BF16)
            hot = matmul(tables_ref[table], hot)
            for m in range(COMPS):
                target_ref[m * ATOMS : (m + 1) * ATOMS, start : start + PROBES] = (
                    hot * row(m)
                ).astype(BF16)

    for row in range(ROWS):
        spread_pairs(spread_ref, owners_ref, row * SPAN, row, own_row)
    extra = theirs_ref[:, lanes(COMPS)].astype(F32).T
    count = len(OFFSETS)
    owner_tables([extra[which : which + 1, :] for which in range(count)], their_owners_ref)
    encode_rows(
        theirs_ref, extra[count : count + 1, :], w_deg_ref, w_gate_ref, embed_ref, their_rows_ref
    )
    for row in range(HALO):
        spread_pairs(halo_ref, their_owners_ref, row * SPAN, first + row, partner_row)
    dists = [packs_ref[row, COMPS, slot : slot + 1, :] for row in range(ROWS) for slot in range(SLOTS)]
    dists += [
        packs_ref[first + row, COMPS, slot : slot + 1, :]
        for row in range(HALO)
        for slot in range(SLOTS)
    ]
    dist = jnp.concatenate(dists, axis=1)
    orders = lax.broadcasted_iota(jnp.int32, (BASES, PAIRS), 0).astype(F32) + 1.0
    phase = math.pi * dist / CUTOFF
    envelope = 0.5 * (jnp.cos(phase) + 1.0) / dist
    basis_split = stacked(jnp.sin(phase * orders) * envelope, (0, 1, 0, 1, 2, 0))
    sums_ref[DEGREES * CHANS :, :] = basis_split
    total = None
    for degree in range(DEGREES):
        low, high = first_rows(degree)
        radial = along_first(split_ref[:, lanes(degree)], basis_split)
        sums = jnp.concatenate(
            [
                along_first(rows_ref[low:high, :], spread_ref[low:high, :]),
                along_first(their_rows_ref[low:high, :], halo_ref[low:high, :]),
            ],
            axis=1,
        )
        sums_ref[lanes(degree), :] = sums.astype(BF16)
        term = radial * sums
        total = term if total is None else total + term

    def value_of(block):
        start = block * SPAN
        both = total[:, start : start + PROBES] + total[:, start + PROBES : start + SPAN]
        return both.T

    for row in range(ROWS):
        value = value_of(row)
        for shard in range(shards):
            out_ref[row, shard] = value[shard * chunk : (shard + 1) * chunk, :]
    for row in range(HALO):
        value = value_of(ROWS + row)
        for shard in range(shards):
            out_ref[first + row, shard] += value[shard * chunk : (shard + 1) * chunk, :]


def silu_slope(values):
    logistic = jax.nn.sigmoid(values)
    return logistic * (1.0 + values * (1.0 - logistic))


def sum_kernel(parts_ref, out_ref):
    total = parts_ref[0].astype(F32)
    for index in range(1, parts_ref.shape[0]):
        total = total + parts_ref[index].astype(F32)
    if len(out_ref.shape) == len(parts_ref.shape):
        for copy in range(out_ref.shape[0]):
            out_ref[copy] = total.astype(out_ref.dtype)
    else:
        out_ref[...] = total.astype(out_ref.dtype)


def readout_kernel(
    scale, parts_ref, target_ref, w_hidden_ref, b_hidden_ref, w_out_ref,
    up_ref, head_ref, density_ref, column_ref,
):
    chunk = parts_ref.shape[1]
    shard = lax.axis_index("x") * lax.axis_size("c") + lax.axis_index("c")
    start = pl.multiple_of(shard * chunk, chunk)
    column_ref[...] = jnp.broadcast_to(target_ref[...], (PROBES, PROBES)).T
    target = column_ref[pl.ds(start, chunk), :]
    summed = parts_ref[0]
    for index in range(1, parts_ref.shape[0]):
        summed = summed + parts_ref[index]
    w_hidden = w_hidden_ref[...]
    w_out = w_out_ref[...]
    hidden_pre = matmul(summed, w_hidden, PRECISE) + b_hidden_ref[...]
    activated = jax.nn.silu(hidden_pre)
    density = jnp.sum(activated * w_out, axis=1, keepdims=True)
    error = density - target
    error_grad = error * scale
    pre_grad = w_out * silu_slope(hidden_pre) * error_grad
    spot = lax.broadcasted_iota(jnp.int32, (chunk, PROBES), 0) + start
    mask = (spot == lax.broadcasted_iota(jnp.int32, (chunk, PROBES), 1)).astype(F32)
    upstream = along_last(pre_grad, w_hidden, PRECISE)
    for copy in range(up_ref.shape[0]):
        up_ref[copy] = upstream
    density_ref[...] = jnp.sum(mask * density, axis=0, keepdims=True)
    head_ref[0:CHANS, :] = along_first(summed, pre_grad, PRECISE)
    bias = jnp.sum(pre_grad, axis=0, keepdims=True)
    out = jnp.sum(activated * error_grad, axis=0, keepdims=True)
    loss = jnp.sum(mask * error * error * (0.5 * scale), axis=0, keepdims=True)
    head_ref[CHANS : CHANS + 16, :] = jnp.concatenate(
        [bias, out, loss, jnp.zeros((13, CHANS), F32)], axis=0
    )


def own_slab():
    return lax.axis_index("z") * ROWS + lax.axis_index("y")


def backward_kernel(
    feats_ref, theirs_ref, species_ref, w_deg_ref, w_gate_ref, split_ref, head_ref, density_ref,
    up_ref, sums_ref, spread_ref, halo_ref, payload_ref,
):
    shards = up_ref.shape[1]
    first = plane_halves()[1]

    def block_of(row):
        parts = [up_ref[row, shard] for shard in range(shards)]
        return [jnp.concatenate(parts, axis=0).T] * SLOTS

    blocks = []
    for row in list(range(ROWS)) + [first + row for row in range(HALO)]:
        blocks += block_of(row)
    upstream = jnp.concatenate(blocks, axis=1)
    scalar = jnp.concatenate([feats_ref[:, lanes(0)], theirs_ref[:, lanes(0)]], axis=0)
    gates = jax.nn.sigmoid(matmul(scalar, w_gate_ref[...]))
    their_species = theirs_ref[:, lanes(COMPS)].astype(F32).T[len(OFFSETS) : len(OFFSETS) + 1, :]
    kinds = jnp.concatenate(
        [kind_rows(species_ref[...].astype(F32)), kind_rows(their_species)], axis=1
    )
    basis_split = sums_ref[DEGREES * CHANS :, :]
    radial_grads = []
    for degree in range(DEGREES):
        low, high = first_rows(degree)
        size = high - low
        radial = along_first(split_ref[:, lanes(degree)], basis_split)
        inner = (radial * upstream).astype(BF16)
        grads = jnp.concatenate(
            [
                along_last(spread_ref[low:high, :], inner[:, 0:OWN_PAIRS]),
                along_last(halo_ref[low:high, :], inner[:, OWN_PAIRS:]),
            ],
            axis=0,
        )
        product = (sums_ref[lanes(degree), :].astype(F32) * upstream).astype(BF16)
        both = along_last(product, basis_split[0 : 2 * BASES, :])
        radial_grads.append((both[:, 0:BASES] + both[:, BASES : 2 * BASES]).T)
        rows = jnp.concatenate(
            [component_rows(feats_ref, degree), component_rows(theirs_ref, degree)], axis=0
        )
        mixed = matmul(rows, w_deg_ref[degree])
        if degree == 0:
            mixed_grad = grads * silu_slope(mixed)
            embed_grad = matmul(kinds, grads, PRECISE)
        else:
            gate = gates[:, lanes(degree - 1)]
            spread_gate = jnp.concatenate(
                [over_components(gate[0:ATOMS, :], degree), over_components(gate[ATOMS:, :], degree)],
                axis=0,
            )
            mixed_grad = grads * spread_gate
            product = grads * mixed
            totals = []
            for side in range(2):
                total = product[side * size : side * size + ATOMS, :]
                for comp in range(1, 2 * degree + 1):
                    begin = side * size + comp * ATOMS
                    total = total + product[begin : begin + ATOMS, :]
                totals.append(total)
            total = jnp.concatenate(totals, axis=0)
            pre = (total * gate * (1.0 - gate)).astype(BF16)
            start = (DEGREES + degree - 1) * CHANS
            payload_ref[start : start + CHANS, :] = along_first(scalar, pre).astype(BF16)
        payload_ref[degree * CHANS : (degree + 1) * CHANS, :] = along_first(
            rows, mixed_grad.astype(BF16)
        ).astype(BF16)
    base = (2 * DEGREES - 1) * CHANS
    payload_ref[base : base + CHANS + 16, :] = head_ref[...].astype(BF16)
    base += CHANS + 16
    payload_ref[base : base + 48, :] = jnp.concatenate(
        radial_grads + [embed_grad], axis=0
    ).astype(BF16)
    base += 48
    slabs = (PAYLOAD - base) // 3
    here = lax.broadcasted_iota(jnp.int32, (slabs, PROBES), 0) == own_slab()
    for part in parts_of(jnp.where(here, density_ref[...], 0.0)):
        payload_ref[base : base + slabs, :] = part
        base += slabs


def unpack_kernel(
    payload_ref, loss_ref, density_ref, deg_ref, gate_ref, embed_ref, radial_ref, hidden_ref,
    bias_ref, out_ref,
):
    for degree in range(DEGREES):
        deg_ref[degree] = payload_ref[lanes(degree), :].astype(F32)
    for degree in range(1, DEGREES):
        gate_ref[:, lanes(degree - 1)] = payload_ref[lanes(DEGREES + degree - 1), :].astype(F32)
    base = (2 * DEGREES - 1) * CHANS
    hidden_ref[...] = payload_ref[base : base + CHANS, :].astype(F32)
    base += CHANS
    misc = payload_ref[base : base + 16, :].astype(F32)
    bias_ref[...] = misc[0:1, :]
    out_ref[...] = misc[1:2, :]
    loss_ref[...] = jnp.sum(misc[2:3, :], axis=1, keepdims=True)
    base += 16
    small = payload_ref[base : base + 48, :].astype(F32)
    for degree in range(DEGREES):
        radial_ref[:, lanes(degree)] = small[degree * BASES : (degree + 1) * BASES, :]
    embed_ref[...] = small[DEGREES * BASES :, :]
    base += 48
    slabs = (PAYLOAD - base) // 3
    total = None
    for _ in range(3):
        part = payload_ref[base : base + slabs, :].astype(F32)
        total = part if total is None else total + part
        base += slabs
    here = lax.broadcasted_iota(jnp.int32, (slabs, PROBES), 0) == own_slab()
    density_ref[...] = jnp.sum(jnp.where(here, total, 0.0), axis=0, keepdims=True)


def shape(dims, dtype=F32):
    return jax.ShapeDtypeStruct(dims, dtype)


def call(kernel, outs, name, limit=32, **options):
    return pl.pallas_call(
        kernel,
        out_shape=outs,
        name=name,
        compiler_params=pltpu.CompilerParams(vmem_limit_bytes=limit * 1024 * 1024),
        **options,
    )


def to_partner(block):
    count = lax.axis_size(SLAB)
    route = [(i, (i + (2 if i % 4 >= 2 else -2)) % count) for i in range(count)]
    return lax.ppermute(block, SLAB, route)


def reduce_all(payload):
    count = lax.axis_size(PLANE)
    depth = lax.axis_size("z")
    rows = PAYLOAD // count
    parts = lax.all_to_all(payload.reshape(count, rows, CHANS), PLANE, 0, 0)
    copies = call(sum_kernel, shape((depth, rows, CHANS), BF16), "sum_plane")(parts)
    parts = lax.all_to_all(copies, "z", 0, 0)
    copies = call(sum_kernel, shape((count, rows, CHANS), BF16), "sum_depth")(parts)
    return lax.all_to_all(copies, PLANE, 0, 0).reshape(PAYLOAD, CHANS)


def on_device(
    atom_feats, species, send_rows, neighbours, harmonics, distances, target,
    w_deg, w_gate, embed, w_radial, w_hidden, b_hidden, w_out,
):
    slab_count = lax.axis_size(SLAB)
    shards = lax.axis_size(ATOM)
    chunk = PROBES // shards
    scale = 1.0 / math.sqrt(PROBES * slab_count)
    species = species.reshape(1, ATOMS)
    lists = send_rows[0, 0]
    far = pl.BlockSpec(memory_space=pl.ANY)
    field_shape = (FIELDS, SLOTS, PROBES)
    operands = (harmonics, distances, neighbours, atom_feats, lists, species)
    copies, atoms = call(
        pack_kernel,
        [shape((ROWS,) + field_shape), shape((ATOMS, (COMPS + 1) * CHANS), BF16)],
        "pack",
        limit=LIMIT,
        in_specs=[far] * len(operands),
        out_specs=[far] * 2,
        scratch_shapes=[
            pltpu.VMEM(field_shape, F32),
            pltpu.VMEM((SLOTS, PROBES), jnp.int32),
            pltpu.VMEM(lists.shape, jnp.int32),
            pltpu.VMEM(species.shape, jnp.int32),
            pltpu.VMEM((ATOMS, CHANS), BF16),
            pltpu.SemaphoreType.DMA((len(operands),)),
            pltpu.SemaphoreType.DMA((1 + ROWS,)),
        ],
    )(*operands)
    with jax.named_scope("exchange_atoms"):
        theirs = to_partner(atoms)
    with jax.named_scope("gather_pairs"):
        packs = lax.all_to_all(copies, "y", 0, 0)
    rows, owners, split, w_deg_near, w_gate_near = call(
        encode_kernel,
        [
            shape((COMPS * ATOMS, CHANS), BF16),
            shape((1 + len(OFFSETS), ATOMS, ATOMS), BF16),
            shape((6 * BASES, DEGREES * CHANS), BF16),
            shape(w_deg.shape, BF16),
            shape(w_gate.shape, BF16),
        ],
        "encode",
    )(atom_feats, species, w_deg, w_gate, embed, lists, w_radial)
    values, spread, halo, sums = call(
        pair_kernel,
        [
            shape((ROWS, shards, chunk, CHANS)),
            shape((COMPS * ATOMS, OWN_PAIRS), BF16),
            shape((COMPS * ATOMS, HALO_PAIRS), BF16),
            shape((DEGREES * CHANS + 6 * BASES, PAIRS), BF16),
        ],
        "pair_sums",
        scratch_shapes=[pltpu.VMEM(rows.shape, BF16), pltpu.VMEM(owners.shape, BF16)],
    )(packs, theirs, rows, owners, split, w_deg_near, w_gate_near, embed)
    with jax.named_scope("scatter_sums"):
        parts = lax.all_to_all(values.reshape(ROWS * shards, chunk, CHANS), PLANE, 0, 0)
    up, head, density_row = call(
        functools.partial(readout_kernel, scale),
        [
            shape((ROWS * shards, chunk, CHANS)),
            shape((CHANS + 16, CHANS)),
            shape((1, PROBES)),
        ],
        "readout",
        scratch_shapes=[pltpu.VMEM((PROBES, PROBES), F32)],
    )(
        parts, target.reshape(1, PROBES), w_hidden, b_hidden.reshape(1, CHANS),
        w_out.reshape(1, CHANS),
    )
    with jax.named_scope("gather_grads"):
        ups = lax.all_to_all(up, PLANE, 0, 0).reshape(ROWS, shards, chunk, CHANS)
    operands = (
        atom_feats, theirs, species, w_deg_near, w_gate_near, split, head, density_row, ups, sums,
        spread, halo,
    )
    payload = call(backward_kernel, shape((PAYLOAD, CHANS), BF16), "backward")(*operands)
    with jax.named_scope("reduce_grads"):
        payload = reduce_all(payload)
    loss, density, deg, gate, embed_grad, radial_grad, hidden, bias, out = call(
        unpack_kernel,
        [
            shape((1, 1)),
            shape((1, PROBES)),
            shape((DEGREES, CHANS, CHANS)),
            shape((CHANS, (DEGREES - 1) * CHANS)),
            shape((KINDS, CHANS)),
            shape((BASES, DEGREES * CHANS)),
            shape((CHANS, CHANS)),
            shape((1, CHANS)),
            shape((1, CHANS)),
        ],
        "unpack",
    )(payload)
    return (
        loss.reshape(()), density.reshape(PROBES), deg, gate, embed_grad, radial_grad, hidden,
        bias.reshape(CHANS), out.reshape(CHANS),
    )


def solution(mesh):
    slabs, shards = mesh.devices.shape
    fine = Mesh(mesh.devices.reshape(slabs // 4, 4, shards // 2, 2), ("z", "y", "x", "c"))
    in_specs = (
        P(SLAB + ATOM, None),
        P(SLAB + ATOM),
        P(SLAB, ATOM, None, None),
        P(ATOM, SLAB),
        P(None, ATOM, SLAB),
        P(ATOM, SLAB),
        P(SLAB),
        P(),
        P(),
        P(),
        P(),
        P(),
        P(),
        P(),
    )
    out_specs = (P(), P(SLAB), P(), P(), P(), P(), P(), P(), P())
    return jax.shard_map(
        on_device, mesh=fine, in_specs=in_specs, out_specs=out_specs, check_vma=False
    )
```

time: 143 us -> 131 us (0.916)
  blocking collectives: 90.2 us -> 79.7 us
  Pallas kernels: 14.2 us -> 22.6 us
  starting transfers between devices: 24.7 us -> 17.9 us
  local copies, waits for them, and re-layouts: 9.24 us -> 6.28 us
    all_to_all x2, blocking collectives: 37.5 us -> 27 us  [the longest x1 14.5 us: on_device(): lax.all_to_all(values.reshape(ROWS * shards, chunk, CHANS), PLANE, 0, 0)]
    pallas_call x7 -> x6, Pallas kernels: 14.1 us -> 22.5 us  [the longest x1 13.6 us: on_device(): call(pack_kernel, [shape((ROWS,) + field_shape), shape((ATOMS, (COMPS + 1...]
    ppermute x2 -> x1, starting transfers between devices: 21.3 us -> 14.6 us  [to_partner(): return lax.ppermute(block, SLAB, route)]
    ppermute x2 -> x1, waiting for transfers between devices: 2.76 us -> 0.01 us  [to_partner(): return lax.ppermute(block, SLAB, route)]
    all_to_all x1, waiting for transfers between devices: 0.01 us -> 2.55 us  [on_device(): packs = lax.all_to_all(copies, 'y', 0, 0)]
    unnamed x36 -> x28, local copies, waits for them, and re-layouts: 8.42 us -> 6.28 us
  transfers between devices with their start and end apart: 3 -> 2, of which waited for: 2 -> 1; matrix products, arithmetic and copies ran while one was open for 0% -> 0% of each run, Pallas kernels for 1% -> 0%
where the time goes in v5:
time: 131 us; the launch traced here: 130 us
  blocking collectives  79.7 us (61%)
  Pallas kernels  22.6 us (17%)
  starting transfers between devices  17.9 us (14%)
  local copies, waits for them, and re-layouts  6.28 us (5%)
  waiting for transfers between devices  2.55 us (2%)
    all_to_all x1, blocking collectives, reduce_all(): parts = lax.all_to_all(copies, 'z', 0, 0)  21.4 us
    all_to_all x1, blocking collectives, reduce_all(): return lax.all_to_all(copies, PLANE, 0, 0).reshape(PAYLOAD, CHANS)  17.6 us
    ppermute x1, starting transfers between devices, to_partner(): return lax.ppermute(block, SLAB, route)  14.6 us
    all_to_all x1, blocking collectives, on_device(): lax.all_to_all(values.reshape(ROWS * shards, chunk, CHANS), PLANE, 0, 0)  14.5 us
    all_to_all x1, blocking collectives, reduce_all(): parts = lax.all_to_all(payload.reshape(count, rows, CHANS), PLANE, 0, 0)  13.7 us
    pallas_call x1, Pallas kernels, on_device(): call(pack_kernel, [shape((ROWS,) + field_shape), shape((ATOMS, (COMPS + 1...  13.6 us
    all_to_all x1, blocking collectives, on_device(): ups = lax.all_to_all(up, PLANE, 0, 0).reshape(ROWS, shards, chunk, CHANS)  12.5 us
    unnamed x28, local copies, waits for them, and re-layouts  6.28 us
  transfers between devices with their start and end apart: 2, of which 1 were waited for; matrix products, arithmetic and copies ran while one was open for 0% of the time, Pallas kernels for 0%

profile of v5, /device:TPU:1, one launch (start us, length us, event | category | flops | bytes accessed | tf_op | source)
XLA Modules:
  0.0 129.9 jit_solution(13755089023306708943)
XLA Ops:
  0.6 0.0 copy-start.13
  0.7 0.0 copy-start.12
  0.7 0.0 copy-start.4
  0.7 0.0 copy-start.1
  0.7 0.0 copy-start.10
  0.7 13.6 %pack.1 = (f32[4,32,2,128]{3,2,1,0:T(2,128)}, bf16[64,3328]{1,0:T(8,128)(2,1)}) custom-call(f32[25,2,128]{2,1,0:T(2,128)} %harm_hbm.1, f32[2,128]{1,0:T(2,128)} %dist_hbm.1, s32[2,128]{1,0:T(2,128)} %nbr_hbm.1, bf16[64,3200]{1,0:T(8,128)(2,1)} %feats_ref.3, s32[4,64]{1,0:T(4,128)} %bitcast.17, s32[1,64]{1,0:T(1,128)} %bitcast.19), custom_call_target="tpu_custom_call" | custom-call | tf_op jit(solution)/shard_map/pack/pallas_call | solution.py:472
  14.3 14.6 %collective-permute-start = (bf16[64,3328]{1,0:T(8,128)(2,1)}, bf16[64,3328]{1,0:T(8,128)(2,1)S(1)}, u32[]{:S(2)}, u32[]{:S(2)}) collective-permute-start(bf16[64,3328]{1,0:T(8,128)(2,1)} %get-tuple-element.32), channel_id=1, source_target_pairs={{0,496},{8,504},{16,32},{24,40},{32,16},{40,24},{48,64},{56,72},{6... | collective-permute-start | bytes 1277960 | tf_op jit(solution)/shard_map/exchange_atoms/ppermute | solution.py:445
  28.9 3.3 %all-to-all-start = ((f32[4,32,2,128]{3,2,1,0:T(2,128)}), f32[4,32,2,128]{3,2,1,0:T(2,128)S(1)}, u32[]{:S(2)}, u32[]{:S(2)}) async-start(f32[4,32,2,128]{3,2,1,0:T(2,128)} %get-tuple-element.36), calls=%async_computation | async-start | bytes 262144 | tf_op jit(solution)/shard_map/gather_pairs/all_to_all | solution.py:492
  32.3 0.0 copy-start
  32.3 1.0 copy-done
  33.3 0.9 copy-done.2
  34.2 0.9 copy-done.3
  35.1 0.7 copy-done.5
  35.8 0.7 copy-done.6
  36.5 0.7 copy-done.8
  37.2 0.7 copy-done.9
  37.9 0.4 encode.1
  38.3 2.5 %all-to-all-done.packs_ref = f32[4,32,2,128]{3,2,1,0:T(2,128)S(1)} async-done(((f32[4,32,2,128]{3,2,1,0:T(2,128)}), f32[4,32,2,128]{3,2,1,0:T(2,128)S(1)}, u32[]{:S(2)}, u32[]{:S(2)}) %all-to-all-start) | async-done | bytes 131104 | tf_op jit(solution)/shard_map/gather_pairs/all_to_all | solution.py:492
  40.8 0.0 collective-permute-done.theirs_ref
  40.8 0.7 copy-done.7
  41.5 2.8 %pair_sums.1 = (f32[4,8,16,128]{3,2,1,0:T(8,128)S(1)}, bf16[1600,1024]{1,0:T(8,128)(2,1)S(1)}, bf16[1600,512]{1,0:T(8,128)(2,1)S(1)}, bf16[688,1536]{1,0:T(8,128)(2,1)S(1)}) custom-call(f32[4,32,2,128]{3,2,1,0:T(2,128)S(1)} %all-to-all-done.packs_ref, bf16[64,3328]{1,0:T(8,128)(2,1)S(1)} %collective-permute-done.theirs_ref, ...), custom_call_target="tpu_custom_call" | custom-call | tf_op jit(solution)/shard_map/pair_sums/pallas_call | solution.py:504
  44.3 14.5 %all_to_all.30.parts_ref = f32[32,16,128]{2,1,0:T(8,128)S(1)} all-to-all(f32[32,16,128]{2,1,0:T(8,128)S(1)} %bitcast.16), channel_id=1, replica_groups=mesh['z'=16,'y'=4,'x'=4,'c'=2] {'y','x','c'}, dimensions={0} | all-to-all | bytes 524288 | tf_op jit(solution)/shard_map/scatter_sums/all_to_all | solution.py:516
  58.8 0.0 copy-done.12
  58.8 0.6 readout.1
  59.5 12.5 %all_to_all.31 = f32[32,16,128]{2,1,0:T(8,128)S(1)} all-to-all(f32[32,16,128]{2,1,0:T(8,128)S(1)} %get-tuple-element.42), channel_id=1, replica_groups=mesh['z'=16,'y'=4,'x'=4,'c'=2] {'y','x','c'}, dimensions={0} | all-to-all | bytes 524288 | tf_op jit(solution)/shard_map/gather_grads/all_to_all | solution.py:531
  71.9 0.0 copy-done.1
  71.9 4.1 %backward.1 = bf16[1536,128]{1,0:T(8,128)(2,1)S(1)} custom-call(bf16[64,3200]{1,0:T(8,128)(2,1)S(1)} %copy-done.1, bf16[64,3328]{1,0:T(8,128)(2,1)S(1)} %collective-permute-done.theirs_ref, s32[1,64]{1,0:T(1,128)S(1)} %bitcast.21, bf16[5,128,128]{2,1,0:T(8,128)(2,1)S(1)} %get-tuple-element.33.w_deg_ref, bf16[128,512]{1,0:T(8,128)(2,1)S(1)} %get-tuple-element.34.w_gate_ref, ...), custom_call_target="tpu_custom_call" | custom-call | tf_op jit(solution)/shard_map/backward/pallas_call | solution.py:536
  76.1 13.7 %all_to_all.32.parts_ref = bf16[32,48,128]{2,1,0:T(8,128)(2,1)S(1)} all-to-all(bf16[32,48,128]{2,1,0:T(8,128)(2,1)S(1)} %bitcast.13), channel_id=1, replica_groups=mesh['z'=16,'y'=4,'x'=4,'c'=2] {'y','x','c'}, dimensions={0} | all-to-all | bytes 786432 | tf_op jit(solution)/shard_map/reduce_grads/all_to_all | solution.py:452
  89.8 0.1 sum_plane.1
  89.9 21.4 %all_to_all.33.parts_ref = bf16[16,48,128]{2,1,0:T(8,128)(2,1)S(1)} all-to-all(bf16[16,48,128]{2,1,0:T(8,128)(2,1)S(1)} %sum_plane.1), channel_id=1, replica_groups=mesh['z'=16,'y'=4,'x'=4,'c'=2] {'z'}, dimensions={0} | all-to-all | bytes 393216 | tf_op jit(solution)/shard_map/reduce_grads/all_to_all | solution.py:454
  111.4 17.6 %all_to_all.34 = bf16[32,48,128]{2,1,0:T(8,128)(2,1)S(1)} all-to-all(bf16[32,48,128]{2,1,0:T(8,128)(2,1)S(1)} %sum_depth.1), channel_id=1, replica_groups=mesh['z'=16,'y'=4,'x'=4,'c'=2] {'y','x','c'}, dimensions={0} | all-to-all | bytes 786432 | tf_op jit(solution)/shard_map/reduce_grads/all_to_all | solution.py:456
  129.0 0.9 unpack.1
  (13 shorter events, 0.1 us)
Async XLA Ops:
  0.6 58.2 %copy-start.13 = (f32[128]{0:T(128)S(1)}, f32[128]{0:T(128)}, u32[]{:S(2)}) copy-start(f32[128]{0:T(128)} %param.27) | copy-start | bytes 1540
  0.7 58.2 %copy-start.12 = (f32[128]{0:T(128)S(1)}, f32[128]{0:T(128)}, u32[]{:S(2)}) copy-start(f32[128]{0:T(128)} %param.26) | copy-start | bytes 1540
  0.7 58.1 %copy-start.4 = (f32[128,128]{1,0:T(8,128)S(1)}, f32[128,128]{1,0:T(8,128)}, u32[]{:S(2)}) copy-start(f32[128,128]{1,0:T(8,128)} %w_hidden_ref.1) | copy-start | bytes 196612
  0.7 58.1 %copy-start.11 = (f32[128]{0:T(128)S(1)}, f32[128]{0:T(128)}, u32[]{:S(2)}) copy-start(f32[128]{0:T(128)} %param.20) | copy-start | bytes 1540
  0.7 71.2 %copy-start.1 = (bf16[64,3200]{1,0:T(8,128)(2,1)S(1)}, bf16[64,3200]{1,0:T(8,128)(2,1)}, u32[]{:S(2)}) copy-start(bf16[64,3200]{1,0:T(8,128)(2,1)} %feats_ref.3) | copy-start | bytes 1228804
  0.7 71.2 %copy-start.10 = (s32[64]{0:T(128)S(1)}, s32[64]{0:T(128)}, u32[]{:S(2)}) copy-start(s32[64]{0:T(128)} %param.15) | copy-start | bytes 772
  14.3 26.5 %collective-permute-start = (bf16[64,3328]{1,0:T(8,128)(2,1)}, bf16[64,3328]{1,0:T(8,128)(2,1)S(1)}, u32[]{:S(2)}, u32[]{:S(2)}) collective-permute-start(bf16[64,3328]{1,0:T(8,128)(2,1)} %get-tuple-element.32), channel_id=1, source_target_pairs={{0,496},{8,504},{16,32},{24,40},{32,16},{40,24},{48,64},{56,72},{6... | collective-permute-start | bytes 1277960 | tf_op jit(solution)/shard_map/exchange_atoms/ppermute | solution.py:445
  28.9 11.9 %all-to-all-start = ((f32[4,32,2,128]{3,2,1,0:T(2,128)}), f32[4,32,2,128]{3,2,1,0:T(2,128)S(1)}, u32[]{:S(2)}, u32[]{:S(2)}) async-start(f32[4,32,2,128]{3,2,1,0:T(2,128)} %get-tuple-element.36), calls=%async_computation | async-start | bytes 262144 | tf_op jit(solution)/shard_map/gather_pairs/all_to_all | solution.py:492
  32.3 1.0 copy-start
  33.3 0.9 copy-start.2
  34.2 0.9 copy-start.3
  35.1 0.7 copy-start.5
  35.8 0.7 copy-start.6
  36.5 0.7 copy-start.8
  37.2 0.7 copy-start.9
  40.8 0.7 copy-start.7

commit v6 on v5

--- a/solution.py
+++ b/solution.py
@@ -32,7 +32,6 @@
 BASES = 8
 KINDS = 8
 PAYLOAD = 1536
-LIMIT = 63
 
 
 def first_rows(degree):
@@ -107,18 +106,23 @@
         rows_ref[low:high, :] = (rows.astype(F32) + added).astype(BF16)
 
 
+def lists_of(atoms_ref):
+    extra = atoms_ref[:, lanes(COMPS)].astype(F32).T
+    count = len(OFFSETS)
+    return [extra[which : which + 1, :] for which in range(count)], extra[count : count + 1, :]
+
+
 def encode_kernel(
-    feats_ref, species_ref, w_deg_ref, w_gate_ref, embed_ref, lists_ref, w_radial_ref,
-    rows_ref, owners_ref, split_ref, w_deg_out_ref, w_gate_out_ref,
+    atoms_ref, w_deg_ref, w_gate_ref, small_ref,
+    rows_ref, owners_ref, split_ref, w_deg_out_ref, w_gate_out_ref, embed_ref,
 ):
     w_deg_out_ref[...] = w_deg_ref[...]
     w_gate_out_ref[...] = w_gate_ref[...]
-    lists = [lists_ref[which : which + 1, :].astype(F32) for which in range(len(OFFSETS))]
+    embed_ref[...] = small_ref[BASES:, lanes(0)]
+    lists, species = lists_of(atoms_ref)
     owner_tables(lists, owners_ref)
-    split_ref[...] = stacked(w_radial_ref[...], (0, 0, 1, 1, 0, 2))
-    encode_rows(
-        feats_ref, species_ref[...].astype(F32), w_deg_ref, w_gate_ref, embed_ref, rows_ref
-    )
+    split_ref[...] = stacked(small_ref[0:BASES, :], (0, 0, 1, 1, 0, 2))
+    encode_rows(atoms_ref, species, w_deg_ref, w_gate_ref, embed_ref, rows_ref)
 
 
 def parts_of(values):
@@ -135,22 +139,25 @@
 
 
 def pack_kernel(
-    harm_hbm, dist_hbm, nbr_hbm, feats_hbm, lists_hbm, species_hbm, copies_hbm, atoms_hbm,
-    pack_ref, nbr_ref, lists_ref, species_ref, extra_ref, sems, out_sems,
-):
-    far = atoms_hbm.at[:, pl.ds(0, COMPS * CHANS)]
+    harm_hbm, dist_hbm, nbr_hbm, feats_hbm, lists_hbm, species_hbm, w_radial_hbm, embed_hbm,
+    copies_hbm, atoms_hbm, small_hbm,
+    pack_ref, atoms_ref, small_ref, nbr_ref, lists_ref, species_ref, sems, out_sems,
+):
+    small_ref[...] = jnp.zeros(small_ref.shape, F32)
     copies = started(
         (
+            (feats_hbm, atoms_ref.at[:, pl.ds(0, COMPS * CHANS)]),
             (harm_hbm, pack_ref.at[pl.ds(0, COMPS)]),
             (dist_hbm, pack_ref.at[COMPS]),
             (nbr_hbm, nbr_ref),
             (lists_hbm, lists_ref),
             (species_hbm, species_ref),
-            (feats_hbm, far),
+            (w_radial_hbm, small_ref.at[pl.ds(0, BASES)]),
+            (embed_hbm, small_ref.at[pl.ds(BASES, KINDS), pl.ds(0, CHANS)]),
         ),
         sems,
     )
-    for copy in copies[:5]:
+    for copy in copies[1:]:
         copy.wait()
     extra = jnp.concatenate(
         [
@@ -160,23 +167,23 @@
         ],
         axis=0,
     )
-    extra_ref[...] = extra.T.astype(BF16)
+    atoms_ref[:, lanes(COMPS)] = extra.T.astype(BF16)
     pack_ref[COMPS + 1] = nbr_ref[...].astype(F32)
     pack_ref[COMPS + 2 :] = jnp.zeros((FIELDS - COMPS - 2, SLOTS, PROBES), F32)
+    copies[0].wait()
     writes = started(
-        [(extra_ref, atoms_hbm.at[:, pl.ds(COMPS * CHANS, CHANS)])]
+        [(atoms_ref, atoms_hbm), (small_ref, small_hbm)]
         + [(pack_ref, copies_hbm.at[row]) for row in range(ROWS)],
         out_sems,
     )
-    for copy in copies[5:] + writes:
-        copy.wait()
+    for write in writes:
+        write.wait()
 
 
 def plane_halves():
     row = lax.axis_index("y")
     upper = jnp.where(row > 1, 1, 0)
-    partner = row + 4 * upper - 2
-    return row, 2 * upper, partner
+    return row, HALO - HALO * upper, row + ROWS - 2 * ROWS * upper
 
 
 def pair_kernel(
@@ -208,11 +215,10 @@
 
     for row in range(ROWS):
         spread_pairs(spread_ref, owners_ref, row * SPAN, row, own_row)
-    extra = theirs_ref[:, lanes(COMPS)].astype(F32).T
-    count = len(OFFSETS)
-    owner_tables([extra[which : which + 1, :] for which in range(count)], their_owners_ref)
+    their_lists, their_species = lists_of(theirs_ref)
+    owner_tables(their_lists, their_owners_ref)
     encode_rows(
-        theirs_ref, extra[count : count + 1, :], w_deg_ref, w_gate_ref, embed_ref, their_rows_ref
+        theirs_ref, their_species, w_deg_ref, w_gate_ref, embed_ref, their_rows_ref
     )
     for row in range(HALO):
         spread_pairs(halo_ref, their_owners_ref, row * SPAN, first + row, partner_row)
@@ -314,8 +320,8 @@
 
 
 def backward_kernel(
-    feats_ref, theirs_ref, species_ref, w_deg_ref, w_gate_ref, split_ref, head_ref, density_ref,
-    up_ref, sums_ref, spread_ref, halo_ref, payload_ref,
+    atoms_ref, theirs_ref, w_deg_ref, w_gate_ref, split_ref, head_ref, density_ref, up_ref,
+    sums_ref, spread_ref, halo_ref, payload_ref,
 ):
     shards = up_ref.shape[1]
     first = plane_halves()[1]
@@ -328,11 +334,10 @@
     for row in list(range(ROWS)) + [first + row for row in range(HALO)]:
         blocks += block_of(row)
     upstream = jnp.concatenate(blocks, axis=1)
-    scalar = jnp.concatenate([feats_ref[:, lanes(0)], theirs_ref[:, lanes(0)]], axis=0)
+    scalar = jnp.concatenate([atoms_ref[:, lanes(0)], theirs_ref[:, lanes(0)]], axis=0)
     gates = jax.nn.sigmoid(matmul(scalar, w_gate_ref[...]))
-    their_species = theirs_ref[:, lanes(COMPS)].astype(F32).T[len(OFFSETS) : len(OFFSETS) + 1, :]
     kinds = jnp.concatenate(
-        [kind_rows(species_ref[...].astype(F32)), kind_rows(their_species)], axis=1
+        [kind_rows(lists_of(ref)[1]) for ref in (atoms_ref, theirs_ref)], axis=1
     )
     basis_split = sums_ref[DEGREES * CHANS :, :]
     radial_grads = []
@@ -352,7 +357,7 @@
         both = along_last(product, basis_split[0 : 2 * BASES, :])
         radial_grads.append((both[:, 0:BASES] + both[:, BASES : 2 * BASES]).T)
         rows = jnp.concatenate(
-            [component_rows(feats_ref, degree), component_rows(theirs_ref, degree)], axis=0
+            [component_rows(atoms_ref, degree), component_rows(theirs_ref, degree)], axis=0
         )
         mixed = matmul(rows, w_deg_ref[degree])
         if degree == 0:
@@ -441,7 +446,7 @@
 
 def to_partner(block):
     count = lax.axis_size(SLAB)
-    route = [(i, (i + (2 if i % 4 >= 2 else -2)) % count) for i in range(count)]
+    route = [(i, (i + (ROWS if i % ROWS >= HALO else -ROWS)) % count) for i in range(count)]
     return lax.ppermute(block, SLAB, route)
 
 
@@ -468,29 +473,37 @@
     lists = send_rows[0, 0]
     far = pl.BlockSpec(memory_space=pl.ANY)
     field_shape = (FIELDS, SLOTS, PROBES)
-    operands = (harmonics, distances, neighbours, atom_feats, lists, species)
-    copies, atoms = call(
+    operands = (
+        harmonics, distances, neighbours, atom_feats, lists, species, w_radial, embed
+    )
+    held = [
+        shape((ROWS,) + field_shape),
+        shape((ATOMS, (COMPS + 1) * CHANS), BF16),
+        shape((BASES + KINDS, DEGREES * CHANS)),
+    ]
+    copies, atoms, small = call(
         pack_kernel,
-        [shape((ROWS,) + field_shape), shape((ATOMS, (COMPS + 1) * CHANS), BF16)],
+        held,
         "pack",
-        limit=LIMIT,
+        limit=63,
         in_specs=[far] * len(operands),
-        out_specs=[far] * 2,
+        out_specs=[far] * len(held),
         scratch_shapes=[
             pltpu.VMEM(field_shape, F32),
+            pltpu.VMEM(held[1].shape, BF16),
+            pltpu.VMEM(held[2].shape, F32),
             pltpu.VMEM((SLOTS, PROBES), jnp.int32),
             pltpu.VMEM(lists.shape, jnp.int32),
             pltpu.VMEM(species.shape, jnp.int32),
-            pltpu.VMEM((ATOMS, CHANS), BF16),
             pltpu.SemaphoreType.DMA((len(operands),)),
-            pltpu.SemaphoreType.DMA((1 + ROWS,)),
+            pltpu.SemaphoreType.DMA((2 + ROWS,)),
         ],
     )(*operands)
     with jax.named_scope("exchange_atoms"):
         theirs = to_partner(atoms)
     with jax.named_scope("gather_pairs"):
         packs = lax.all_to_all(copies, "y", 0, 0)
-    rows, owners, split, w_deg_near, w_gate_near = call(
+    rows, owners, split, w_deg_near, w_gate_near, embed_near = call(
         encode_kernel,
         [
             shape((COMPS * ATOMS, CHANS), BF16),
@@ -498,9 +511,10 @@
             shape((6 * BASES, DEGREES * CHANS), BF16),
             shape(w_deg.shape, BF16),
             shape(w_gate.shape, BF16),
+            shape(embed.shape),
         ],
         "encode",
-    )(atom_feats, species, w_deg, w_gate, embed, lists, w_radial)
+    )(atoms, w_deg, w_gate, small)
     values, spread, halo, sums = call(
         pair_kernel,
         [
@@ -511,7 +525,7 @@
         ],
         "pair_sums",
         scratch_shapes=[pltpu.VMEM(rows.shape, BF16), pltpu.VMEM(owners.shape, BF16)],
-    )(packs, theirs, rows, owners, split, w_deg_near, w_gate_near, embed)
+    )(packs, theirs, rows, owners, split, w_deg_near, w_gate_near, embed_near)
     with jax.named_scope("scatter_sums"):
         parts = lax.all_to_all(values.reshape(ROWS * shards, chunk, CHANS), PLANE, 0, 0)
     up, head, density_row = call(
@@ -530,7 +544,7 @@
     with jax.named_scope("gather_grads"):
         ups = lax.all_to_all(up, PLANE, 0, 0).reshape(ROWS, shards, chunk, CHANS)
     operands = (
-        atom_feats, theirs, species, w_deg_near, w_gate_near, split, head, density_row, ups, sums,
+        atoms, theirs, w_deg_near, w_gate_near, split, head, density_row, ups, sums,
         spread, halo,
     )
     payload = call(backward_kernel, shape((PAYLOAD, CHANS), BF16), "backward")(*operands)

time: 131 us -> 115 us (0.88)
  Pallas kernels: 22.6 us -> 10.9 us
  blocking collectives: 79.7 us -> 82.9 us
  local copies, waits for them, and re-layouts: 6.28 us -> 3.62 us
  starting transfers between devices: 17.9 us -> 15.3 us
    pallas_call x1, Pallas kernels: 13.6 us -> 1.98 us  [on_device(): call(pack_kernel, held, 'pack', limit=63, in_specs=[far] * len(operands),...]
    all_to_all x1, blocking collectives: 14.5 us -> 18 us  [on_device(): lax.all_to_all(values.reshape(ROWS * shards, chunk, CHANS), PLANE, 0, 0)]
    unnamed x28 -> x18, local copies, waits for them, and re-layouts: 6.28 us -> 3.62 us
    ppermute x1, starting transfers between devices: 14.6 us -> 12 us  [to_partner(): return lax.ppermute(block, SLAB, route)]
    all_to_all x1, waiting for transfers between devices: 2.55 us -> 0.72 us  [on_device(): packs = lax.all_to_all(copies, 'y', 0, 0)]
  transfers between devices with their start and end apart: 2 -> 2, of which waited for: 1 -> 2; matrix products, arithmetic and copies ran while one was open for 0% -> 0% of each run, Pallas kernels for 0% -> 0%
where the time goes in v6:
time: 115 us
  blocking collectives  82.9 us (72%)
  starting transfers between devices  15.3 us (13%)
  Pallas kernels  10.9 us (9%)
  local copies, waits for them, and re-layouts  3.62 us (3%)
  waiting for transfers between devices  1.36 us (1%)
    all_to_all x1, blocking collectives, reduce_all(): parts = lax.all_to_all(copies, 'z', 0, 0)  21.1 us
    all_to_all x1, blocking collectives, on_device(): lax.all_to_all(values.reshape(ROWS * shards, chunk, CHANS), PLANE, 0, 0)  18 us
    all_to_all x1, blocking collectives, reduce_all(): return lax.all_to_all(copies, PLANE, 0, 0).reshape(PAYLOAD, CHANS)  17.6 us
    all_to_all x1, blocking collectives, reduce_all(): parts = lax.all_to_all(payload.reshape(count, rows, CHANS), PLANE, 0, 0)  13.7 us
    all_to_all x1, blocking collectives, on_device(): ups = lax.all_to_all(up, PLANE, 0, 0).reshape(ROWS, shards, chunk, CHANS)  12.5 us
    ppermute x1, starting transfers between devices, to_partner(): return lax.ppermute(block, SLAB, route)  12 us
    pallas_call x1, Pallas kernels, on_device(): call(backward_kernel, shape((PAYLOAD, CHANS), BF16), 'backward')(*operands)  4.12 us
    unnamed x18, local copies, waits for them, and re-layouts  3.62 us
  transfers between devices with their start and end apart: 2, of which 2 were waited for; matrix products, arithmetic and copies ran while one was open for 0% of the time, Pallas kernels for 0%

profile of v6, /device:TPU:1, one launch (start us, length us, event | category | flops | bytes accessed | tf_op | source)
XLA Modules:
  0.0 114.8 jit_solution(11850160169258081353)
XLA Ops:
  0.6 0.0 copy-start.8
  0.7 0.0 copy-start.7
  0.7 0.0 copy-start.4
  0.7 0.0 copy-start.6
  0.7 2.0 %pack.1 = (f32[4,32,2,128]{3,2,1,0:T(2,128)}, bf16[64,3328]{1,0:T(8,128)(2,1)}, f32[16,640]{1,0:T(8,128)}) custom-call(f32[25,2,128]{2,1,0:T(2,128)} %harm_hbm.1, f32[2,128]{1,0:T(2,128)} %dist_hbm.1, s32[2,128]{1,0:T(2,128)} %nbr_hbm.1, bf16[64,3200]{1,0:T(8,128)(2,1)} %feats_hbm.1, s32[4,64]{1,0:T(4,128)} %bitcast.20, s32[1,64]{1,0:T(1,128)} %bitcast.21, ...), custom_call_target="tpu_custom_call" | custom-call | tf_op jit(solution)/shard_map/pack/pallas_call | solution.py:484
  2.7 12.0 %collective-permute-start = (bf16[64,3328]{1,0:T(8,128)(2,1)}, bf16[64,3328]{1,0:T(8,128)(2,1)S(1)}, u32[]{:S(2)}, u32[]{:S(2)}) collective-permute-start(bf16[64,3328]{1,0:T(8,128)(2,1)} %get-tuple-element.34.atoms_ref), channel_id=1, source_target_pairs={{0,480},{8,488},{16,48},{24,56},{32,0},{40,8},{48,80},{56,88},{64,... | collective-permute-start | bytes 1277960 | tf_op jit(solution)/shard_map/exchange_atoms/ppermute | solution.py:450
  14.6 3.3 %all-to-all-start = ((f32[4,32,2,128]{3,2,1,0:T(2,128)}), f32[4,32,2,128]{3,2,1,0:T(2,128)S(1)}, u32[]{:S(2)}, u32[]{:S(2)}) async-start(f32[4,32,2,128]{3,2,1,0:T(2,128)} %get-tuple-element.39), calls=%async_computation | async-start | bytes 262144 | tf_op jit(solution)/shard_map/gather_pairs/all_to_all | solution.py:505
  18.0 0.0 copy-start
  18.0 1.0 copy-done
  19.0 0.0 copy-start.2
  19.0 0.9 copy-done.2
  19.9 0.0 copy-start.3
  19.9 0.9 copy-done.3
  20.8 0.8 copy-done.5
  21.6 0.5 encode.1
  22.1 0.7 all-to-all-done.packs_ref
  22.8 0.6 collective-permute-done.theirs_ref
  23.4 2.8 %pair_sums.1 = (f32[4,8,16,128]{3,2,1,0:T(8,128)S(1)}, bf16[1600,1024]{1,0:T(8,128)(2,1)S(1)}, bf16[1600,512]{1,0:T(8,128)(2,1)S(1)}, bf16[688,1536]{1,0:T(8,128)(2,1)S(1)}) custom-call(f32[4,32,2,128]{3,2,1,0:T(2,128)S(1)} %all-to-all-done.packs_ref, bf16[64,3328]{1,0:T(8,128)(2,1)S(1)} %collective-permute-done.theirs_ref, ...), custom_call_target="tpu_custom_call" | custom-call | tf_op jit(solution)/shard_map/pair_sums/pallas_call | solution.py:518
  26.2 18.0 %all_to_all.30.parts_ref = f32[32,16,128]{2,1,0:T(8,128)S(1)} all-to-all(f32[32,16,128]{2,1,0:T(8,128)S(1)} %bitcast.16), channel_id=1, replica_groups=mesh['z'=16,'y'=4,'x'=4,'c'=2] {'y','x','c'}, dimensions={0} | all-to-all | bytes 524288 | tf_op jit(solution)/shard_map/scatter_sums/all_to_all | solution.py:530
  44.2 0.0 copy-done.8
  44.2 0.0 copy-done.7
  44.2 0.0 copy-done.4
  44.2 0.0 copy-done.6
  44.2 0.6 readout.1
  44.8 12.5 %all_to_all.31 = f32[32,16,128]{2,1,0:T(8,128)S(1)} all-to-all(f32[32,16,128]{2,1,0:T(8,128)S(1)} %get-tuple-element.46), channel_id=1, replica_groups=mesh['z'=16,'y'=4,'x'=4,'c'=2] {'y','x','c'}, dimensions={0} | all-to-all | bytes 524288 | tf_op jit(solution)/shard_map/gather_grads/all_to_all | solution.py:545
  57.3 0.0 copy-done.1
  57.3 4.1 %backward.1 = bf16[1536,128]{1,0:T(8,128)(2,1)S(1)} custom-call(bf16[64,3328]{1,0:T(8,128)(2,1)S(1)} %copy-done.1, bf16[64,3328]{1,0:T(8,128)(2,1)S(1)} %collective-permute-done.theirs_ref, bf16[5,128,128]{2,1,0:T(8,128)(2,1)S(1)} %get-tuple-element.36.w_deg_ref, bf16[128,512]{1,0:T(8,128)(2,1)S(1)} %get-tuple-element.37.w_gate_ref, ...), custom_call_target="tpu_custom_call" | custom-call | tf_op jit(solution)/shard_map/backward/pallas_call | solution.py:550
  61.4 13.7 %all_to_all.32.parts_ref = bf16[32,48,128]{2,1,0:T(8,128)(2,1)S(1)} all-to-all(bf16[32,48,128]{2,1,0:T(8,128)(2,1)S(1)} %bitcast.13), channel_id=1, replica_groups=mesh['z'=16,'y'=4,'x'=4,'c'=2] {'y','x','c'}, dimensions={0} | all-to-all | bytes 786432 | tf_op jit(solution)/shard_map/reduce_grads/all_to_all | solution.py:457
  75.1 0.1 sum_plane.1
  75.2 21.1 %all_to_all.33.parts_ref = bf16[16,48,128]{2,1,0:T(8,128)(2,1)S(1)} all-to-all(bf16[16,48,128]{2,1,0:T(8,128)(2,1)S(1)} %sum_plane.1), channel_id=1, replica_groups=mesh['z'=16,'y'=4,'x'=4,'c'=2] {'z'}, dimensions={0} | all-to-all | bytes 393216 | tf_op jit(solution)/shard_map/reduce_grads/all_to_all | solution.py:459
  96.3 17.6 %all_to_all.34 = bf16[32,48,128]{2,1,0:T(8,128)(2,1)S(1)} all-to-all(bf16[32,48,128]{2,1,0:T(8,128)(2,1)S(1)} %sum_depth.1), channel_id=1, replica_groups=mesh['z'=16,'y'=4,'x'=4,'c'=2] {'y','x','c'}, dimensions={0} | all-to-all | bytes 786432 | tf_op jit(solution)/shard_map/reduce_grads/all_to_all | solution.py:461
  114.0 0.9 unpack.1
  (3 shorter events, 0.0 us)
Async XLA Ops:
  0.6 43.5 %copy-start.8 = (f32[128]{0:T(128)S(1)}, f32[128]{0:T(128)}, u32[]{:S(2)}) copy-start(f32[128]{0:T(128)} %param.27) | copy-start | bytes 1540
  0.7 43.5 %copy-start.7 = (f32[128]{0:T(128)S(1)}, f32[128]{0:T(128)}, u32[]{:S(2)}) copy-start(f32[128]{0:T(128)} %param.26) | copy-start | bytes 1540
  0.7 43.5 %copy-start.4 = (f32[128,128]{1,0:T(8,128)S(1)}, f32[128,128]{1,0:T(8,128)}, u32[]{:S(2)}) copy-start(f32[128,128]{1,0:T(8,128)} %w_hidden_ref.1) | copy-start | bytes 196612
  0.7 43.5 %copy-start.6 = (f32[128]{0:T(128)S(1)}, f32[128]{0:T(128)}, u32[]{:S(2)}) copy-start(f32[128]{0:T(128)} %param.20) | copy-start | bytes 1540
  2.7 20.7 %collective-permute-start = (bf16[64,3328]{1,0:T(8,128)(2,1)}, bf16[64,3328]{1,0:T(8,128)(2,1)S(1)}, u32[]{:S(2)}, u32[]{:S(2)}) collective-permute-start(bf16[64,3328]{1,0:T(8,128)(2,1)} %get-tuple-element.34.atoms_ref), channel_id=1, source_target_pairs={{0,480},{8,488},{16,48},{24,56},{32,0},{40,8},{48,80},{56,88},{64,... | collective-permute-start | bytes 1277960 | tf_op jit(solution)/shard_map/exchange_atoms/ppermute | solution.py:450
  14.6 8.1 %all-to-all-start = ((f32[4,32,2,128]{3,2,1,0:T(2,128)}), f32[4,32,2,128]{3,2,1,0:T(2,128)S(1)}, u32[]{:S(2)}, u32[]{:S(2)}) async-start(f32[4,32,2,128]{3,2,1,0:T(2,128)} %get-tuple-element.39), calls=%async_computation | async-start | bytes 262144 | tf_op jit(solution)/shard_map/gather_pairs/all_to_all | solution.py:505
  18.0 1.0 copy-start
  19.0 0.9 copy-start.2
  19.9 0.9 copy-start.3
  20.8 0.8 copy-start.5
  21.6 35.7 %copy-start.1 = (bf16[64,3328]{1,0:T(8,128)(2,1)S(1)}, bf16[64,3328]{1,0:T(8,128)(2,1)}, u32[]{:S(2)}) copy-start(bf16[64,3328]{1,0:T(8,128)(2,1)} %get-tuple-element.34.atoms_ref) | copy-start | bytes 1277956

commit v7 on v6

--- a/solution.py
+++ b/solution.py
@@ -13,9 +13,10 @@
 PRECISE = lax.Precision.HIGHEST
 F32 = jnp.float32
 BF16 = jnp.bfloat16
-SLAB = ("z", "y")
+SLAB = ("zh", "zl", "y")
 ATOM = ("x", "c")
 PLANE = ("y", "x", "c")
+NEAR = ("zl", "y", "x", "c")
 DEGREES = 5
 COMPS = DEGREES * DEGREES
 CHANS = 128
@@ -90,13 +91,17 @@
     return copies
 
 
-def encode_rows(feats_ref, species, w_deg_ref, w_gate_ref, embed_ref, rows_ref):
+def encode_rows(
+    feats_ref, species, w_deg_ref, w_gate_ref, embed_ref, rows_ref, mixed_ref, gates_ref
+):
     scalar = feats_ref[:, lanes(0)]
     gates = jax.nn.sigmoid(matmul(scalar, w_gate_ref[...]))
+    gates_ref[...] = gates
     for degree in range(DEGREES):
         low, high = first_rows(degree)
         rows = component_rows(feats_ref, degree)
         mixed = matmul(rows, w_deg_ref[degree])
+        mixed_ref[low:high, :] = mixed
         if degree == 0:
             added = jax.nn.silu(mixed) + along_first(
                 kind_rows(species), embed_ref[...], PRECISE
@@ -114,7 +119,8 @@
 
 def encode_kernel(
     atoms_ref, w_deg_ref, w_gate_ref, small_ref,
-    rows_ref, owners_ref, split_ref, w_deg_out_ref, w_gate_out_ref, embed_ref,
+    rows_ref, owners_ref, split_ref, w_deg_out_ref, w_gate_out_ref, embed_ref, mixed_ref,
+    gates_ref,
 ):
     w_deg_out_ref[...] = w_deg_ref[...]
     w_gate_out_ref[...] = w_gate_ref[...]
@@ -122,7 +128,9 @@
     lists, species = lists_of(atoms_ref)
     owner_tables(lists, owners_ref)
     split_ref[...] = stacked(small_ref[0:BASES, :], (0, 0, 1, 1, 0, 2))
-    encode_rows(atoms_ref, species, w_deg_ref, w_gate_ref, embed_ref, rows_ref)
+    encode_rows(
+        atoms_ref, species, w_deg_ref, w_gate_ref, embed_ref, rows_ref, mixed_ref, gates_ref
+    )
 
 
 def parts_of(values):
@@ -188,7 +196,8 @@
 
 def pair_kernel(
     packs_ref, theirs_ref, rows_ref, owners_ref, split_ref, w_deg_ref, w_gate_ref, embed_ref,
-    out_ref, spread_ref, halo_ref, sums_ref, their_rows_ref, their_owners_ref,
+    out_ref, spread_ref, halo_ref, sums_ref, radial_ref, their_mixed_ref, their_gates_ref,
+    their_rows_ref, their_owners_ref,
 ):
     shards, chunk = out_ref.shape[1], out_ref.shape[2]
     own_row, first, partner_row = plane_halves()
@@ -218,7 +227,8 @@
     their_lists, their_species = lists_of(theirs_ref)
     owner_tables(their_lists, their_owners_ref)
     encode_rows(
-        theirs_ref, their_species, w_deg_ref, w_gate_ref, embed_ref, their_rows_ref
+        theirs_ref, their_species, w_deg_ref, w_gate_ref, embed_ref, their_rows_ref,
+        their_mixed_ref, their_gates_ref,
     )
     for row in range(HALO):
         spread_pairs(halo_ref, their_owners_ref, row * SPAN, first + row, partner_row)
@@ -233,11 +243,12 @@
     phase = math.pi * dist / CUTOFF
     envelope = 0.5 * (jnp.cos(phase) + 1.0) / dist
     basis_split = stacked(jnp.sin(phase * orders) * envelope, (0, 1, 0, 1, 2, 0))
-    sums_ref[DEGREES * CHANS :, :] = basis_split
+    sums_ref[DEGREES * CHANS :, :] = basis_split[0 : 2 * BASES, :]
     total = None
     for degree in range(DEGREES):
         low, high = first_rows(degree)
         radial = along_first(split_ref[:, lanes(degree)], basis_split)
+        radial_ref[lanes(degree), :] = radial
         sums = jnp.concatenate(
             [
                 along_first(rows_ref[low:high, :], spread_ref[low:high, :]),
@@ -316,12 +327,13 @@
 
 
 def own_slab():
-    return lax.axis_index("z") * ROWS + lax.axis_index("y")
+    depth = lax.axis_index("zh") * lax.axis_size("zl") + lax.axis_index("zl")
+    return depth * ROWS + lax.axis_index("y")
 
 
 def backward_kernel(
-    atoms_ref, theirs_ref, w_deg_ref, w_gate_ref, split_ref, head_ref, density_ref, up_ref,
-    sums_ref, spread_ref, halo_ref, payload_ref,
+    atoms_ref, theirs_ref, mixed_ref, their_mixed_ref, gates_ref, their_gates_ref, radial_ref,
+    head_ref, density_ref, up_ref, sums_ref, spread_ref, halo_ref, payload_ref,
 ):
     shards = up_ref.shape[1]
     first = plane_halves()[1]
@@ -335,7 +347,7 @@
         blocks += block_of(row)
     upstream = jnp.concatenate(blocks, axis=1)
     scalar = jnp.concatenate([atoms_ref[:, lanes(0)], theirs_ref[:, lanes(0)]], axis=0)
-    gates = jax.nn.sigmoid(matmul(scalar, w_gate_ref[...]))
+    gates = jnp.concatenate([gates_ref[...], their_gates_ref[...]], axis=0)
     kinds = jnp.concatenate(
         [kind_rows(lists_of(ref)[1]) for ref in (atoms_ref, theirs_ref)], axis=1
     )
@@ -344,8 +356,7 @@
     for degree in range(DEGREES):
         low, high = first_rows(degree)
         size = high - low
-        radial = along_first(split_ref[:, lanes(degree)], basis_split)
-        inner = (radial * upstream).astype(BF16)
+        inner = (radial_ref[lanes(degree), :] * upstream).astype(BF16)
         grads = jnp.concatenate(
             [
                 along_last(spread_ref[low:high, :], inner[:, 0:OWN_PAIRS]),
@@ -354,12 +365,12 @@
             axis=0,
         )
         product = (sums_ref[lanes(degree), :].astype(F32) * upstream).astype(BF16)
-        both = along_last(product, basis_split[0 : 2 * BASES, :])
+        both = along_last(product, basis_split)
         radial_grads.append((both[:, 0:BASES] + both[:, BASES : 2 * BASES]).T)
         rows = jnp.concatenate(
             [component_rows(atoms_ref, degree), component_rows(theirs_ref, degree)], axis=0
         )
-        mixed = matmul(rows, w_deg_ref[degree])
+        mixed = jnp.concatenate([mixed_ref[low:high, :], their_mixed_ref[low:high, :]], axis=0)
         if degree == 0:
             mixed_grad = grads * silu_slope(mixed)
             embed_grad = matmul(kinds, grads, PRECISE)
@@ -451,14 +462,13 @@
 
 
 def reduce_all(payload):
-    count = lax.axis_size(PLANE)
-    depth = lax.axis_size("z")
+    count, depth = lax.axis_size(NEAR), lax.axis_size("zh")
     rows = PAYLOAD // count
-    parts = lax.all_to_all(payload.reshape(count, rows, CHANS), PLANE, 0, 0)
-    copies = call(sum_kernel, shape((depth, rows, CHANS), BF16), "sum_plane")(parts)
-    parts = lax.all_to_all(copies, "z", 0, 0)
+    parts = lax.all_to_all(payload.reshape(count, rows, CHANS), NEAR, 0, 0)
+    copies = call(sum_kernel, shape((depth, rows, CHANS), BF16), "sum_near")(parts)
+    parts = lax.all_to_all(copies, "zh", 0, 0)
     copies = call(sum_kernel, shape((count, rows, CHANS), BF16), "sum_depth")(parts)
-    return lax.all_to_all(copies, PLANE, 0, 0).reshape(PAYLOAD, CHANS)
+    return lax.all_to_all(copies, NEAR, 0, 0).reshape(PAYLOAD, CHANS)
 
 
 def on_device(
@@ -503,7 +513,8 @@
         theirs = to_partner(atoms)
     with jax.named_scope("gather_pairs"):
         packs = lax.all_to_all(copies, "y", 0, 0)
-    rows, owners, split, w_deg_near, w_gate_near, embed_near = call(
+    mixed_shapes = [shape((COMPS * ATOMS, CHANS)), shape((ATOMS, (DEGREES - 1) * CHANS))]
+    rows, owners, split, w_deg_near, w_gate_near, embed_near, mixed, gates = call(
         encode_kernel,
         [
             shape((COMPS * ATOMS, CHANS), BF16),
@@ -512,17 +523,20 @@
             shape(w_deg.shape, BF16),
             shape(w_gate.shape, BF16),
             shape(embed.shape),
-        ],
+        ]
+        + mixed_shapes,
         "encode",
     )(atoms, w_deg, w_gate, small)
-    values, spread, halo, sums = call(
+    values, spread, halo, sums, radial, their_mixed, their_gates = call(
         pair_kernel,
         [
             shape((ROWS, shards, chunk, CHANS)),
             shape((COMPS * ATOMS, OWN_PAIRS), BF16),
             shape((COMPS * ATOMS, HALO_PAIRS), BF16),
-            shape((DEGREES * CHANS + 6 * BASES, PAIRS), BF16),
-        ],
+            shape((DEGREES * CHANS + 2 * BASES, PAIRS), BF16),
+            shape((DEGREES * CHANS, PAIRS)),
+        ]
+        + mixed_shapes,
         "pair_sums",
         scratch_shapes=[pltpu.VMEM(rows.shape, BF16), pltpu.VMEM(owners.shape, BF16)],
     )(packs, theirs, rows, owners, split, w_deg_near, w_gate_near, embed_near)
@@ -544,8 +558,8 @@
     with jax.named_scope("gather_grads"):
         ups = lax.all_to_all(up, PLANE, 0, 0).reshape(ROWS, shards, chunk, CHANS)
     operands = (
-        atoms, theirs, w_deg_near, w_gate_near, split, head, density_row, ups, sums,
-        spread, halo,
+        atoms, theirs, mixed, their_mixed, gates, their_gates, radial, head, density_row, ups,
+        sums, spread, halo,
     )
     payload = call(backward_kernel, shape((PAYLOAD, CHANS), BF16), "backward")(*operands)
     with jax.named_scope("reduce_grads"):
@@ -573,7 +587,8 @@
 
 def solution(mesh):
     slabs, shards = mesh.devices.shape
-    fine = Mesh(mesh.devices.reshape(slabs // 4, 4, shards // 2, 2), ("z", "y", "x", "c"))
+    fine = mesh.devices.reshape(slabs // 8, 2, 4, shards // 2, 2)
+    fine = Mesh(fine, ("zh", "zl", "y", "x", "c"))
     in_specs = (
         P(SLAB + ATOM, None),
         P(SLAB + ATOM),

time: 115 us -> 114 us (level)
  no operation moved by 1% of the time
where the time goes in v7:
time: 114 us; the launch traced here: 113 us
  blocking collectives  82.2 us (72%)
  starting transfers between devices  15.3 us (13%)
  Pallas kernels  10.1 us (9%)
  local copies, waits for them, and re-layouts  3.62 us (3%)
  waiting for transfers between devices  1.36 us (1%)
    all_to_all x1, blocking collectives, reduce_all(): parts = lax.all_to_all(copies, 'zh', 0, 0)  19.9 us
    all_to_all x1, blocking collectives, on_device(): lax.all_to_all(values.reshape(ROWS * shards, chunk, CHANS), PLANE, 0, 0)  18 us
    all_to_all x1, blocking collectives, reduce_all(): return lax.all_to_all(copies, NEAR, 0, 0).reshape(PAYLOAD, CHANS)  16.9 us
    all_to_all x1, blocking collectives, reduce_all(): parts = lax.all_to_all(payload.reshape(count, rows, CHANS), NEAR, 0, 0)  14.9 us
    all_to_all x1, blocking collectives, on_device(): ups = lax.all_to_all(up, PLANE, 0, 0).reshape(ROWS, shards, chunk, CHANS)  12.5 us
    ppermute x1, starting transfers between devices, to_partner(): return lax.ppermute(block, SLAB, route)  12 us
    unnamed x18, local copies, waits for them, and re-layouts  3.62 us
    all_to_all x1, starting transfers between devices, on_device(): packs = lax.all_to_all(copies, 'y', 0, 0)  3.34 us
  transfers between devices with their start and end apart: 2, of which 2 were waited for; matrix products, arithmetic and copies ran while one was open for 0% of the time, Pallas kernels for 0%

profile of v7, /device:TPU:1, one launch (start us, length us, event | category | flops | bytes accessed | tf_op | source)
XLA Modules:
  0.0 113.3 jit_solution(3126190106613681289)
XLA Ops:
  0.6 0.0 copy-start.8
  0.7 0.0 copy-start.7
  0.7 0.0 copy-start.4
  0.7 0.0 copy-start.6
  0.7 2.0 %pack.1 = (f32[4,32,2,128]{3,2,1,0:T(2,128)}, bf16[64,3328]{1,0:T(8,128)(2,1)}, f32[16,640]{1,0:T(8,128)}) custom-call(f32[25,2,128]{2,1,0:T(2,128)} %harm_hbm.1, f32[2,128]{1,0:T(2,128)} %dist_hbm.1, s32[2,128]{1,0:T(2,128)} %nbr_hbm.1, bf16[64,3200]{1,0:T(8,128)(2,1)} %feats_hbm.1, s32[4,64]{1,0:T(4,128)} %bitcast.20, s32[1,64]{1,0:T(1,128)} %bitcast.21, ...), custom_call_target="tpu_custom_call" | custom-call | tf_op jit(solution)/shard_map/pack/pallas_call | solution.py:494
  2.7 12.0 %collective-permute-start = (bf16[64,3328]{1,0:T(8,128)(2,1)}, bf16[64,3328]{1,0:T(8,128)(2,1)S(1)}, u32[]{:S(2)}, u32[]{:S(2)}) collective-permute-start(bf16[64,3328]{1,0:T(8,128)(2,1)} %get-tuple-element.39.atoms_ref), channel_id=1, source_target_pairs={{0,480},{8,488},{16,48},{24,56},{32,0},{40,8},{48,80},{56,88},{64,... | collective-permute-start | bytes 1277960 | tf_op jit(solution)/shard_map/exchange_atoms/ppermute | solution.py:461
  14.6 3.3 %all-to-all-start = ((f32[4,32,2,128]{3,2,1,0:T(2,128)}), f32[4,32,2,128]{3,2,1,0:T(2,128)S(1)}, u32[]{:S(2)}, u32[]{:S(2)}) async-start(f32[4,32,2,128]{3,2,1,0:T(2,128)} %get-tuple-element.42), calls=%async_computation | async-start | bytes 262144 | tf_op jit(solution)/shard_map/gather_pairs/all_to_all | solution.py:515
  18.0 0.0 copy-start
  18.0 1.0 copy-done
  19.0 0.0 copy-start.2
  19.0 0.9 copy-done.2
  19.9 0.0 copy-start.3
  19.9 0.9 copy-done.3
  20.8 0.8 copy-done.5
  21.6 0.5 encode.1
  22.1 0.7 all-to-all-done.packs_ref
  22.8 0.6 collective-permute-done.theirs_ref
  23.4 2.8 %pair_sums.1 = (f32[4,8,16,128]{3,2,1,0:T(8,128)S(1)}, bf16[1600,1024]{1,0:T(8,128)(2,1)S(1)}, bf16[1600,512]{1,0:T(8,128)(2,1)S(1)}, bf16[656,1536]{1,0:T(8,128...) custom-call(f32[4,32,2,128]{3,2,1,0:T(2,128)S(1)} %all-to-all-done.packs_ref, ...), custom_call_target="tpu_custom_call" | custom-call | tf_op jit(solution)/shard_map/pair_sums/pallas_call | solution.py:530
  26.2 18.0 %all_to_all.30.parts_ref = f32[32,16,128]{2,1,0:T(8,128)S(1)} all-to-all(f32[32,16,128]{2,1,0:T(8,128)S(1)} %bitcast.16), channel_id=1, replica_groups=mesh['zh'=8,'zl'=2,'y'=4,'x'=4,'c'=2] {'y','x','c'}, dimensions={0} | all-to-all | bytes 524288 | tf_op jit(solution)/shard_map/scatter_sums/all_to_all | solution.py:544
  44.2 0.0 copy-done.8
  44.2 0.0 copy-done.7
  44.2 0.0 copy-done.4
  44.2 0.0 copy-done.6
  44.2 0.6 readout.1
  44.9 12.5 %all_to_all.31 = f32[32,16,128]{2,1,0:T(8,128)S(1)} all-to-all(f32[32,16,128]{2,1,0:T(8,128)S(1)} %get-tuple-element.56), channel_id=1, replica_groups=mesh['zh'=8,'zl'=2,'y'=4,'x'=4,'c'=2] {'y','x','c'}, dimensions={0} | all-to-all | bytes 524288 | tf_op jit(solution)/shard_map/gather_grads/all_to_all | solution.py:559
  57.3 0.0 copy-done.1
  57.3 3.3 %backward.1 = bf16[1536,128]{1,0:T(8,128)(2,1)S(1)} custom-call(bf16[64,3328]{1,0:T(8,128)(2,1)S(1)} %copy-done.1, bf16[64,3328]{1,0:T(8,128)(2,1)S(1)} %collective-permute-done.theirs_ref, f32[1600,128]{1,0:T(8,128)S(1)} %get-tuple-element.41.mixed_ref, f32[1600,128]{1,0:T(8,128)S(1)} %get-tuple-element.49.their_mixed_ref, ...), custom_call_target="tpu_custom_call" | custom-call | tf_op jit(solution)/shard_map/backward/pallas_call | solution.py:564
  60.6 14.9 %all_to_all.32.parts_ref = bf16[64,24,128]{2,1,0:T(8,128)(2,1)S(1)} all-to-all(bf16[64,24,128]{2,1,0:T(8,128)(2,1)S(1)} %bitcast.14), channel_id=1, replica_groups=mesh['zh'=8,'zl'=2,'y'=4,'x'=4,'c'=2] {'zl','y','x','c'}, dimensions={0} | all-to-all | bytes 786432 | tf_op jit(solution)/shard_map/reduce_grads/all_to_all | solution.py:467
  75.5 0.1 sum_near.1
  75.5 19.9 %all_to_all.33.parts_ref = bf16[8,24,128]{2,1,0:T(8,128)(2,1)S(1)} all-to-all(bf16[8,24,128]{2,1,0:T(8,128)(2,1)S(1)} %sum_near.1), channel_id=1, replica_groups=mesh['zh'=8,'zl'=2,'y'=4,'x'=4,'c'=2] {'zh'}, dimensions={0} | all-to-all | bytes 98304 | tf_op jit(solution)/shard_map/reduce_grads/all_to_all | solution.py:469
  95.5 16.9 %all_to_all.34 = bf16[64,24,128]{2,1,0:T(8,128)(2,1)S(1)} all-to-all(bf16[64,24,128]{2,1,0:T(8,128)(2,1)S(1)} %sum_depth.1), channel_id=1, replica_groups=mesh['zh'=8,'zl'=2,'y'=4,'x'=4,'c'=2] {'zl','y','x','c'}, dimensions={0} | all-to-all | bytes 786432 | tf_op jit(solution)/shard_map/reduce_grads/all_to_all | solution.py:471
  112.4 0.9 unpack.1
  (3 shorter events, 0.0 us)
Async XLA Ops:
  0.6 43.6 %copy-start.8 = (f32[128]{0:T(128)S(1)}, f32[128]{0:T(128)}, u32[]{:S(2)}) copy-start(f32[128]{0:T(128)} %param.27) | copy-start | bytes 1540
  0.7 43.5 %copy-start.7 = (f32[128]{0:T(128)S(1)}, f32[128]{0:T(128)}, u32[]{:S(2)}) copy-start(f32[128]{0:T(128)} %param.26) | copy-start | bytes 1540
  0.7 43.5 %copy-start.4 = (f32[128,128]{1,0:T(8,128)S(1)}, f32[128,128]{1,0:T(8,128)}, u32[]{:S(2)}) copy-start(f32[128,128]{1,0:T(8,128)} %w_hidden_ref.1) | copy-start | bytes 196612
  0.7 43.5 %copy-start.6 = (f32[128]{0:T(128)S(1)}, f32[128]{0:T(128)}, u32[]{:S(2)}) copy-start(f32[128]{0:T(128)} %param.20) | copy-start | bytes 1540
  2.7 20.7 %collective-permute-start = (bf16[64,3328]{1,0:T(8,128)(2,1)}, bf16[64,3328]{1,0:T(8,128)(2,1)S(1)}, u32[]{:S(2)}, u32[]{:S(2)}) collective-permute-start(bf16[64,3328]{1,0:T(8,128)(2,1)} %get-tuple-element.39.atoms_ref), channel_id=1, source_target_pairs={{0,480},{8,488},{16,48},{24,56},{32,0},{40,8},{48,80},{56,88},{64,... | collective-permute-start | bytes 1277960 | tf_op jit(solution)/shard_map/exchange_atoms/ppermute | solution.py:461
  14.6 8.1 %all-to-all-start = ((f32[4,32,2,128]{3,2,1,0:T(2,128)}), f32[4,32,2,128]{3,2,1,0:T(2,128)S(1)}, u32[]{:S(2)}, u32[]{:S(2)}) async-start(f32[4,32,2,128]{3,2,1,0:T(2,128)} %get-tuple-element.42), calls=%async_computation | async-start | bytes 262144 | tf_op jit(solution)/shard_map/gather_pairs/all_to_all | solution.py:515
  18.0 1.0 copy-start
  19.0 0.9 copy-start.2
  19.9 0.9 copy-start.3
  20.8 0.8 copy-start.5
  21.6 35.7 %copy-start.1 = (bf16[64,3328]{1,0:T(8,128)(2,1)S(1)}, bf16[64,3328]{1,0:T(8,128)(2,1)}, u32[]{:S(2)}) copy-start(bf16[64,3328]{1,0:T(8,128)(2,1)} %get-tuple-element.39.atoms_ref) | copy-start | bytes 1277956

commit v8 on v7

--- a/solution.py
+++ b/solution.py
@@ -33,6 +33,10 @@
 BASES = 8
 KINDS = 8
 PAYLOAD = 1536
+EMBED_ROW = DEGREES * BASES
+INTS_ROW = EMBED_ROW + KINDS
+CONST_ROW = INTS_ROW + 8
+SMALL_ROWS = CONST_ROW + 8 + CHANS
 
 
 def first_rows(degree):
@@ -111,25 +115,30 @@
         rows_ref[low:high, :] = (rows.astype(F32) + added).astype(BF16)
 
 
-def lists_of(atoms_ref):
-    extra = atoms_ref[:, lanes(COMPS)].astype(F32).T
+def lists_of(ints_ref):
     count = len(OFFSETS)
-    return [extra[which : which + 1, :] for which in range(count)], extra[count : count + 1, :]
+    lists = [ints_ref[which : which + 1, 0:ATOMS] for which in range(count)]
+    return lists, ints_ref[count : count + 1, 0:ATOMS]
 
 
 def encode_kernel(
-    atoms_ref, w_deg_ref, w_gate_ref, small_ref,
-    rows_ref, owners_ref, split_ref, w_deg_out_ref, w_gate_out_ref, embed_ref, mixed_ref,
-    gates_ref,
+    feats_ref, w_deg_ref, w_gate_ref, small_ref,
+    rows_ref, owners_ref, split_ref, w_deg_out_ref, w_gate_out_ref, embed_ref, ints_ref,
+    const_ref, mixed_ref, gates_ref,
 ):
     w_deg_out_ref[...] = w_deg_ref[...]
     w_gate_out_ref[...] = w_gate_ref[...]
-    embed_ref[...] = small_ref[BASES:, lanes(0)]
-    lists, species = lists_of(atoms_ref)
+    embed_ref[...] = small_ref[EMBED_ROW:INTS_ROW, :]
+    ints_ref[...] = small_ref[INTS_ROW:CONST_ROW, :]
+    const_ref[...] = small_ref[CONST_ROW:, :]
+    lists, species = lists_of(ints_ref)
     owner_tables(lists, owners_ref)
-    split_ref[...] = stacked(small_ref[0:BASES, :], (0, 0, 1, 1, 0, 2))
+    w_radial = jnp.concatenate(
+        [small_ref[degree * BASES : (degree + 1) * BASES, :] for degree in range(DEGREES)], axis=1
+    )
+    split_ref[...] = stacked(w_radial, (0, 0, 1, 1, 0, 2))
     encode_rows(
-        atoms_ref, species, w_deg_ref, w_gate_ref, embed_ref, rows_ref, mixed_ref, gates_ref
+        feats_ref, species, w_deg_ref, w_gate_ref, embed_ref, rows_ref, mixed_ref, gates_ref
     )
 
 
@@ -147,40 +156,46 @@
 
 
 def pack_kernel(
-    harm_hbm, dist_hbm, nbr_hbm, feats_hbm, lists_hbm, species_hbm, w_radial_hbm, embed_hbm,
-    copies_hbm, atoms_hbm, small_hbm,
-    pack_ref, atoms_ref, small_ref, nbr_ref, lists_ref, species_ref, sems, out_sems,
-):
-    small_ref[...] = jnp.zeros(small_ref.shape, F32)
+    harm_hbm, dist_hbm, nbr_hbm, lists_hbm, species_hbm, w_radial_hbm, embed_hbm, w_hidden_hbm,
+    b_hidden_hbm, w_out_hbm, target_hbm, copies_hbm, ints_hbm, small_hbm,
+    pack_ref, small_ref, nbr_ref, lists_ref, species_ref, b_hidden_ref, w_out_ref, target_ref,
+    sems, out_sems,
+):
     copies = started(
-        (
-            (feats_hbm, atoms_ref.at[:, pl.ds(0, COMPS * CHANS)]),
+        [
             (harm_hbm, pack_ref.at[pl.ds(0, COMPS)]),
             (dist_hbm, pack_ref.at[COMPS]),
             (nbr_hbm, nbr_ref),
             (lists_hbm, lists_ref),
             (species_hbm, species_ref),
-            (w_radial_hbm, small_ref.at[pl.ds(0, BASES)]),
-            (embed_hbm, small_ref.at[pl.ds(BASES, KINDS), pl.ds(0, CHANS)]),
-        ),
+            (embed_hbm, small_ref.at[pl.ds(EMBED_ROW, KINDS)]),
+            (w_hidden_hbm, small_ref.at[pl.ds(CONST_ROW + 8, CHANS)]),
+            (b_hidden_hbm, b_hidden_ref),
+            (w_out_hbm, w_out_ref),
+            (target_hbm, target_ref),
+        ]
+        + [
+            (
+                w_radial_hbm.at[:, pl.ds(degree * CHANS, CHANS)],
+                small_ref.at[pl.ds(degree * BASES, BASES)],
+            )
+            for degree in range(DEGREES)
+        ],
         sems,
     )
-    for copy in copies[1:]:
+    pack_ref[COMPS + 2 :] = jnp.zeros((FIELDS - COMPS - 2, SLOTS, PROBES), F32)
+    small_ref[INTS_ROW : CONST_ROW + 8, :] = jnp.zeros((16, CHANS), F32)
+    for copy in copies:
         copy.wait()
-    extra = jnp.concatenate(
-        [
-            lists_ref[...].astype(F32),
-            species_ref[...].astype(F32),
-            jnp.zeros((CHANS - 1 - len(OFFSETS), ATOMS), F32),
-        ],
-        axis=0,
-    )
-    atoms_ref[:, lanes(COMPS)] = extra.T.astype(BF16)
+    count = len(OFFSETS)
+    small_ref[INTS_ROW : INTS_ROW + count, 0:ATOMS] = lists_ref[...].astype(F32)
+    small_ref[INTS_ROW + count : INTS_ROW + count + 1, 0:ATOMS] = species_ref[...].astype(F32)
+    small_ref[CONST_ROW : CONST_ROW + 3, :] = jnp.concatenate(
+        [b_hidden_ref[...], w_out_ref[...], target_ref[...]], axis=0
+    )
     pack_ref[COMPS + 1] = nbr_ref[...].astype(F32)
-    pack_ref[COMPS + 2 :] = jnp.zeros((FIELDS - COMPS - 2, SLOTS, PROBES), F32)
-    copies[0].wait()
     writes = started(
-        [(atoms_ref, atoms_hbm), (small_ref, small_hbm)]
+        [(small_ref.at[pl.ds(INTS_ROW, 8)], ints_hbm), (small_ref, small_hbm)]
         + [(pack_ref, copies_hbm.at[row]) for row in range(ROWS)],
         out_sems,
     )
@@ -195,8 +210,8 @@
 
 
 def pair_kernel(
-    packs_ref, theirs_ref, rows_ref, owners_ref, split_ref, w_deg_ref, w_gate_ref, embed_ref,
-    out_ref, spread_ref, halo_ref, sums_ref, radial_ref, their_mixed_ref, their_gates_ref,
+    packs_ref, theirs_ref, their_ints_ref, rows_ref, owners_ref, split_ref, w_deg_ref,
+    w_gate_ref, embed_ref, out_ref, spread_ref, halo_ref, sums_ref, radial_ref, their_mixed_ref, their_gates_ref,
     their_rows_ref, their_owners_ref,
 ):
     shards, chunk = out_ref.shape[1], out_ref.shape[2]
@@ -224,7 +239,7 @@
 
     for row in range(ROWS):
         spread_pairs(spread_ref, owners_ref, row * SPAN, row, own_row)
-    their_lists, their_species = lists_of(theirs_ref)
+    their_lists, their_species = lists_of(their_ints_ref)
     owner_tables(their_lists, their_owners_ref)
     encode_rows(
         theirs_ref, their_species, w_deg_ref, w_gate_ref, embed_ref, their_rows_ref,
@@ -292,20 +307,19 @@
 
 
 def readout_kernel(
-    scale, parts_ref, target_ref, w_hidden_ref, b_hidden_ref, w_out_ref,
-    up_ref, head_ref, density_ref, column_ref,
+    scale, parts_ref, const_ref, up_ref, head_ref, density_ref, column_ref
 ):
     chunk = parts_ref.shape[1]
     shard = lax.axis_index("x") * lax.axis_size("c") + lax.axis_index("c")
     start = pl.multiple_of(shard * chunk, chunk)
-    column_ref[...] = jnp.broadcast_to(target_ref[...], (PROBES, PROBES)).T
+    column_ref[...] = jnp.broadcast_to(const_ref[2:3, :], (PROBES, PROBES)).T
     target = column_ref[pl.ds(start, chunk), :]
     summed = parts_ref[0]
     for index in range(1, parts_ref.shape[0]):
         summed = summed + parts_ref[index]
-    w_hidden = w_hidden_ref[...]
-    w_out = w_out_ref[...]
-    hidden_pre = matmul(summed, w_hidden, PRECISE) + b_hidden_ref[...]
+    w_hidden = const_ref[8:, :]
+    w_out = const_ref[1:2, :]
+    hidden_pre = matmul(summed, w_hidden, PRECISE) + const_ref[0:1, :]
     activated = jax.nn.silu(hidden_pre)
     density = jnp.sum(activated * w_out, axis=1, keepdims=True)
     error = density - target
@@ -332,8 +346,8 @@
 
 
 def backward_kernel(
-    atoms_ref, theirs_ref, mixed_ref, their_mixed_ref, gates_ref, their_gates_ref, radial_ref,
-    head_ref, density_ref, up_ref, sums_ref, spread_ref, halo_ref, payload_ref,
+    atoms_ref, theirs_ref, ints_ref, their_ints_ref, mixed_ref, their_mixed_ref, gates_ref, their_gates_ref,
+    radial_ref, head_ref, density_ref, up_ref, sums_ref, spread_ref, halo_ref, payload_ref,
 ):
     shards = up_ref.shape[1]
     first = plane_halves()[1]
@@ -349,7 +363,7 @@
     scalar = jnp.concatenate([atoms_ref[:, lanes(0)], theirs_ref[:, lanes(0)]], axis=0)
     gates = jnp.concatenate([gates_ref[...], their_gates_ref[...]], axis=0)
     kinds = jnp.concatenate(
-        [kind_rows(lists_of(ref)[1]) for ref in (atoms_ref, theirs_ref)], axis=1
+        [kind_rows(lists_of(ref)[1]) for ref in (ints_ref, their_ints_ref)], axis=1
     )
     basis_split = sums_ref[DEGREES * CHANS :, :]
     radial_grads = []
@@ -483,15 +497,18 @@
     lists = send_rows[0, 0]
     far = pl.BlockSpec(memory_space=pl.ANY)
     field_shape = (FIELDS, SLOTS, PROBES)
+    with jax.named_scope("exchange_atoms"):
+        theirs = to_partner(atom_feats)
+    rows_of = [row.reshape(1, CHANS) for row in (b_hidden, w_out, target)]
     operands = (
-        harmonics, distances, neighbours, atom_feats, lists, species, w_radial, embed
+        harmonics, distances, neighbours, lists, species, w_radial, embed, w_hidden, *rows_of
     )
     held = [
         shape((ROWS,) + field_shape),
-        shape((ATOMS, (COMPS + 1) * CHANS), BF16),
-        shape((BASES + KINDS, DEGREES * CHANS)),
+        shape((8, CHANS)),
+        shape((SMALL_ROWS, CHANS)),
     ]
-    copies, atoms, small = call(
+    copies, ints, small = call(
         pack_kernel,
         held,
         "pack",
@@ -500,21 +517,23 @@
         out_specs=[far] * len(held),
         scratch_shapes=[
             pltpu.VMEM(field_shape, F32),
-            pltpu.VMEM(held[1].shape, BF16),
             pltpu.VMEM(held[2].shape, F32),
             pltpu.VMEM((SLOTS, PROBES), jnp.int32),
             pltpu.VMEM(lists.shape, jnp.int32),
             pltpu.VMEM(species.shape, jnp.int32),
-            pltpu.SemaphoreType.DMA((len(operands),)),
+        ]
+        + [pltpu.VMEM((1, CHANS), F32)] * 3
+        + [
+            pltpu.SemaphoreType.DMA((len(operands) - 1 + DEGREES,)),
             pltpu.SemaphoreType.DMA((2 + ROWS,)),
         ],
     )(*operands)
-    with jax.named_scope("exchange_atoms"):
-        theirs = to_partner(atoms)
+    with jax.named_scope("exchange_lists"):
+        their_ints = to_partner(ints)
     with jax.named_scope("gather_pairs"):
         packs = lax.all_to_all(copies, "y", 0, 0)
     mixed_shapes = [shape((COMPS * ATOMS, CHANS)), shape((ATOMS, (DEGREES - 1) * CHANS))]
-    rows, owners, split, w_deg_near, w_gate_near, embed_near, mixed, gates = call(
+    rows, owners, split, w_deg_near, w_gate_near, embed_near, own_ints, consts, mixed, gates = call(
         encode_kernel,
         [
             shape((COMPS * ATOMS, CHANS), BF16),
@@ -523,10 +542,12 @@
             shape(w_deg.shape, BF16),
             shape(w_gate.shape, BF16),
             shape(embed.shape),
+            shape(ints.shape),
+            shape((SMALL_ROWS - CONST_ROW, CHANS)),
         ]
         + mixed_shapes,
         "encode",
-    )(atoms, w_deg, w_gate, small)
+    )(atom_feats, w_deg, w_gate, small)
     values, spread, halo, sums, radial, their_mixed, their_gates = call(
         pair_kernel,
         [
@@ -539,7 +560,9 @@
         + mixed_shapes,
         "pair_sums",
         scratch_shapes=[pltpu.VMEM(rows.shape, BF16), pltpu.VMEM(owners.shape, BF16)],
-    )(packs, theirs, rows, owners, split, w_deg_near, w_gate_near, embed_near)
+    )(
+        packs, theirs, their_ints, rows, owners, split, w_deg_near, w_gate_near, embed_near
+    )
     with jax.named_scope("scatter_sums"):
         parts = lax.all_to_all(values.reshape(ROWS * shards, chunk, CHANS), PLANE, 0, 0)
     up, head, density_row = call(
@@ -551,15 +574,12 @@
         ],
         "readout",
         scratch_shapes=[pltpu.VMEM((PROBES, PROBES), F32)],
-    )(
-        parts, target.reshape(1, PROBES), w_hidden, b_hidden.reshape(1, CHANS),
-        w_out.reshape(1, CHANS),
-    )
+    )(parts, consts)
     with jax.named_scope("gather_grads"):
         ups = lax.all_to_all(up, PLANE, 0, 0).reshape(ROWS, shards, chunk, CHANS)
     operands = (
-        atoms, theirs, mixed, their_mixed, gates, their_gates, radial, head, density_row, ups,
-        sums, spread, halo,
+        atom_feats, theirs, own_ints, their_ints, mixed, their_mixed, gates, their_gates, radial,
+        head, density_row, ups, sums, spread, halo,
     )
     payload = call(backward_kernel, shape((PAYLOAD, CHANS), BF16), "backward")(*operands)
     with jax.named_scope("reduce_grads"):

time: 114 us -> 117 us (1.026)
  local copies, waits for them, and re-layouts: 3.62 us -> 6.67 us
  starting transfers between devices: 15.3 us -> 18.1 us
  waiting for transfers between devices: 1.36 us -> 0.01 us
    unnamed x18, local copies, waits for them, and re-layouts: 3.62 us -> 6.67 us
    ppermute x1 -> x2, starting transfers between devices: 12 us -> 14.7 us  [to_partner(): return lax.ppermute(block, SLAB, route)]
    all_to_all x1, blocking collectives: 18 us -> 16.2 us  [on_device(): lax.all_to_all(values.reshape(ROWS * shards, chunk, CHANS), PLANE, 0, 0)]
  transfers between devices with their start and end apart: 2 -> 3, of which waited for: 2 -> 0; matrix products, arithmetic and copies ran while one was open for 0% -> 0% of each run, Pallas kernels for 0% -> 2%
where the time goes in v8:
time: 117 us; the launch traced here: 116 us
  blocking collectives  81.1 us (69%)
  starting transfers between devices  18.1 us (15%)
  Pallas kernels  9.93 us (8%)
  local copies, waits for them, and re-layouts  6.67 us (6%)
    all_to_all x1, blocking collectives, reduce_all(): parts = lax.all_to_all(copies, 'zh', 0, 0)  20.6 us
    all_to_all x1, blocking collectives, reduce_all(): return lax.all_to_all(copies, NEAR, 0, 0).reshape(PAYLOAD, CHANS)  16.9 us
    all_to_all x1, blocking collectives, on_device(): lax.all_to_all(values.reshape(ROWS * shards, chunk, CHANS), PLANE, 0, 0)  16.2 us
    all_to_all x1, blocking collectives, reduce_all(): parts = lax.all_to_all(payload.reshape(count, rows, CHANS), NEAR, 0, 0)  14.9 us
    ppermute x2, starting transfers between devices, to_partner(): return lax.ppermute(block, SLAB, route)  14.7 us
    all_to_all x1, blocking collectives, on_device(): ups = lax.all_to_all(up, PLANE, 0, 0).reshape(ROWS, shards, chunk, CHANS)  12.5 us
    unnamed x18, local copies, waits for them, and re-layouts  6.67 us
    all_to_all x1, starting transfers between devices, on_device(): packs = lax.all_to_all(copies, 'y', 0, 0)  3.34 us
  transfers between devices with their start and end apart: 3, of which 0 were waited for; matrix products, arithmetic and copies ran while one was open for 0% of the time, Pallas kernels for 2%

profile of v8, /device:TPU:1, one launch (start us, length us, event | category | flops | bytes accessed | tf_op | source)
XLA Modules:
  0.0 116.5 jit_solution(8703931114268831068)
XLA Ops:
  0.6 12.0 %collective-permute-start = (bf16[64,3200]{1,0:T(8,128)(2,1)}, bf16[64,3200]{1,0:T(8,128)(2,1)S(1)}, u32[]{:S(2)}, u32[]{:S(2)}) collective-permute-start(bf16[64,3200]{1,0:T(8,128)(2,1)} %atoms_ref.1), channel_id=1, source_target_pairs={{0,480},{8,488},{16,48},{24,56},{32,0},{40,8},{48,80},{56,88},{64,... | collective-permute-start | bytes 1228808 | tf_op jit(solution)/shard_map/exchange_atoms/ppermute | solution.py:475
  12.6 1.8 %pack.1 = (f32[4,32,2,128]{3,2,1,0:T(2,128)}, f32[8,128]{1,0:T(8,128)}, f32[192,128]{1,0:T(8,128)}) custom-call(f32[25,2,128]{2,1,0:T(2,128)} %harm_hbm.1, f32[2,128]{1,0:T(2,128)} %dist_hbm.1, s32[2,128]{1,0:T(2,128)} %nbr_hbm.1, s32[4,64]{1,0:T(4,128)} %bitcast.17, s32[1,64]{1,0:T(1,128)} %bitcast.18, f32[8,640]{1,0:T(8,128)} %w_radial_hbm.1, ...), custom_call_target="tpu_custom_call" | custom-call | tf_op jit(solution)/shard_map/pack/pallas_call | solution.py:511
  14.4 3.3 %all-to-all-start = ((f32[4,32,2,128]{3,2,1,0:T(2,128)}), f32[4,32,2,128]{3,2,1,0:T(2,128)S(1)}, u32[]{:S(2)}, u32[]{:S(2)}) async-start(f32[4,32,2,128]{3,2,1,0:T(2,128)} %get-tuple-element.45), calls=%async_computation | async-start | bytes 262144 | tf_op jit(solution)/shard_map/gather_pairs/all_to_all | solution.py:534
  17.8 2.8 %collective-permute-start.1 = (f32[8,128]{1,0:T(8,128)}, f32[8,128]{1,0:T(8,128)S(1)}, u32[]{:S(2)}, u32[]{:S(2)}) collective-permute-start(f32[8,128]{1,0:T(8,128)} %get-tuple-element.43), channel_id=1, source_target_pairs={{0,480},{8,488},{16,48},{24,56},{32,0},{40,8},{48,80},{56,88},{64,... | collective-permute-start | bytes 12296 | tf_op jit(solution)/shard_map/exchange_lists/ppermute | solution.py:475
  20.6 0.0 copy-start
  20.6 1.0 copy-done
  21.6 0.0 copy-start.2
  21.6 0.9 copy-done.2
  22.5 0.0 copy-start.3
  22.5 0.9 copy-done.3
  23.4 0.9 copy-done.4
  24.3 0.4 encode.1
  24.7 0.0 copy-start.5
  24.7 0.6 copy-done.5
  25.3 0.6 copy-done.7
  25.9 0.0 collective-permute-done.1.their_ints_ref
  25.9 0.0 all-to-all-done.packs_ref
  25.9 0.0 collective-permute-done.theirs_ref
  25.9 0.0 copy-start.8
  25.9 0.8 copy-done.8
  26.8 2.8 %pair_sums.1 = (f32[4,8,16,128]{3,2,1,0:T(8,128)S(1)}, bf16[1600,1024]{1,0:T(8,128)(2,1)S(1)}, bf16[1600,512]{1,0:T(8,128)(2,1)S(1)}, bf16[656,1536]{1,0:T(8,128...) custom-call(f32[4,32,2,128]{3,2,1,0:T(2,128)S(1)} %all-to-all-done.packs_ref, ...), custom_call_target="tpu_custom_call" | custom-call | tf_op jit(solution)/shard_map/pair_sums/pallas_call | solution.py:551
  29.6 16.2 %all_to_all.30.parts_ref = f32[32,16,128]{2,1,0:T(8,128)S(1)} all-to-all(f32[32,16,128]{2,1,0:T(8,128)S(1)} %bitcast.16), channel_id=1, replica_groups=mesh['zh'=8,'zl'=2,'y'=4,'x'=4,'c'=2] {'y','x','c'}, dimensions={0} | all-to-all | bytes 524288 | tf_op jit(solution)/shard_map/scatter_sums/all_to_all | solution.py:567
  45.8 0.9 copy-done.6
  46.6 0.6 readout.1
  47.3 12.5 %all_to_all.31 = f32[32,16,128]{2,1,0:T(8,128)S(1)} all-to-all(f32[32,16,128]{2,1,0:T(8,128)S(1)} %get-tuple-element.60), channel_id=1, replica_groups=mesh['zh'=8,'zl'=2,'y'=4,'x'=4,'c'=2] {'y','x','c'}, dimensions={0} | all-to-all | bytes 524288 | tf_op jit(solution)/shard_map/gather_grads/all_to_all | solution.py:579
  59.7 0.0 copy-done.1
  59.7 3.3 %backward.1 = bf16[1536,128]{1,0:T(8,128)(2,1)S(1)} custom-call(bf16[64,3200]{1,0:T(8,128)(2,1)S(1)} %copy-done.1, bf16[64,3200]{1,0:T(8,128)(2,1)S(1)} %collective-permute-done.theirs_ref, f32[8,128]{1,0:T(8,128)S(1)} %get-tuple-element.42.ints_ref, f32[8,128]{1,0:T(8,128)S(1)} %collective-permute-done.1.their_ints_ref, ...), custom_call_target="tpu_custom_call" | custom-call | tf_op jit(solution)/shard_map/backward/pallas_call | solution.py:584
  63.0 14.9 %all_to_all.32.parts_ref = bf16[64,24,128]{2,1,0:T(8,128)(2,1)S(1)} all-to-all(bf16[64,24,128]{2,1,0:T(8,128)(2,1)S(1)} %bitcast.13), channel_id=1, replica_groups=mesh['zh'=8,'zl'=2,'y'=4,'x'=4,'c'=2] {'zl','y','x','c'}, dimensions={0} | all-to-all | bytes 786432 | tf_op jit(solution)/shard_map/reduce_grads/all_to_all | solution.py:481
  77.9 0.1 sum_near.1
  78.0 20.6 %all_to_all.33.parts_ref = bf16[8,24,128]{2,1,0:T(8,128)(2,1)S(1)} all-to-all(bf16[8,24,128]{2,1,0:T(8,128)(2,1)S(1)} %sum_near.1), channel_id=1, replica_groups=mesh['zh'=8,'zl'=2,'y'=4,'x'=4,'c'=2] {'zh'}, dimensions={0} | all-to-all | bytes 98304 | tf_op jit(solution)/shard_map/reduce_grads/all_to_all | solution.py:483
  98.6 16.9 %all_to_all.34 = bf16[64,24,128]{2,1,0:T(8,128)(2,1)S(1)} all-to-all(bf16[64,24,128]{2,1,0:T(8,128)(2,1)S(1)} %sum_depth.1), channel_id=1, replica_groups=mesh['zh'=8,'zl'=2,'y'=4,'x'=4,'c'=2] {'zl','y','x','c'}, dimensions={0} | all-to-all | bytes 786432 | tf_op jit(solution)/shard_map/reduce_grads/all_to_all | solution.py:485
  115.6 0.9 unpack.1
  (5 shorter events, 0.0 us)
Async XLA Ops:
  0.6 25.3 %collective-permute-start = (bf16[64,3200]{1,0:T(8,128)(2,1)}, bf16[64,3200]{1,0:T(8,128)(2,1)S(1)}, u32[]{:S(2)}, u32[]{:S(2)}) collective-permute-start(bf16[64,3200]{1,0:T(8,128)(2,1)} %atoms_ref.1), channel_id=1, source_target_pairs={{0,480},{8,488},{16,48},{24,56},{32,0},{40,8},{48,80},{56,88},{64,... | collective-permute-start | bytes 1228808 | tf_op jit(solution)/shard_map/exchange_atoms/ppermute | solution.py:475
  14.4 11.5 %all-to-all-start = ((f32[4,32,2,128]{3,2,1,0:T(2,128)}), f32[4,32,2,128]{3,2,1,0:T(2,128)S(1)}, u32[]{:S(2)}, u32[]{:S(2)}) async-start(f32[4,32,2,128]{3,2,1,0:T(2,128)} %get-tuple-element.45), calls=%async_computation | async-start | bytes 262144 | tf_op jit(solution)/shard_map/gather_pairs/all_to_all | solution.py:534
  17.8 8.1 %collective-permute-start.1 = (f32[8,128]{1,0:T(8,128)}, f32[8,128]{1,0:T(8,128)S(1)}, u32[]{:S(2)}, u32[]{:S(2)}) collective-permute-start(f32[8,128]{1,0:T(8,128)} %get-tuple-element.43), channel_id=1, source_target_pairs={{0,480},{8,488},{16,48},{24,56},{32,0},{40,8},{48,80},{56,88},{64,... | collective-permute-start | bytes 12296 | tf_op jit(solution)/shard_map/exchange_lists/ppermute | solution.py:475
  20.6 1.0 copy-start
  21.6 0.9 copy-start.2
  22.5 0.9 copy-start.3
  23.4 0.9 copy-start.4
  24.3 35.5 %copy-start.1 = (bf16[64,3200]{1,0:T(8,128)(2,1)S(1)}, bf16[64,3200]{1,0:T(8,128)(2,1)}, u32[]{:S(2)}) copy-start(bf16[64,3200]{1,0:T(8,128)(2,1)} %atoms_ref.1) | copy-start | bytes 1228804
  24.7 0.6 copy-start.5
  25.3 0.6 copy-start.7
  25.9 0.8 copy-start.8
  45.8 0.9 copy-start.6

commit v9 on v8

--- a/solution.py
+++ b/solution.py
@@ -121,27 +121,6 @@
     return lists, ints_ref[count : count + 1, 0:ATOMS]
 
 
-def encode_kernel(
-    feats_ref, w_deg_ref, w_gate_ref, small_ref,
-    rows_ref, owners_ref, split_ref, w_deg_out_ref, w_gate_out_ref, embed_ref, ints_ref,
-    const_ref, mixed_ref, gates_ref,
-):
-    w_deg_out_ref[...] = w_deg_ref[...]
-    w_gate_out_ref[...] = w_gate_ref[...]
-    embed_ref[...] = small_ref[EMBED_ROW:INTS_ROW, :]
-    ints_ref[...] = small_ref[INTS_ROW:CONST_ROW, :]
-    const_ref[...] = small_ref[CONST_ROW:, :]
-    lists, species = lists_of(ints_ref)
-    owner_tables(lists, owners_ref)
-    w_radial = jnp.concatenate(
-        [small_ref[degree * BASES : (degree + 1) * BASES, :] for degree in range(DEGREES)], axis=1
-    )
-    split_ref[...] = stacked(w_radial, (0, 0, 1, 1, 0, 2))
-    encode_rows(
-        feats_ref, species, w_deg_ref, w_gate_ref, embed_ref, rows_ref, mixed_ref, gates_ref
-    )
-
-
 def parts_of(values):
     high = values.astype(BF16)
     rest = values - high.astype(F32)
@@ -203,6 +182,12 @@
         write.wait()
 
 
+def stage_kernel(*refs):
+    half = len(refs) // 2
+    for source, target in zip(refs[:half], refs[half:]):
+        target[...] = source[...]
+
+
 def plane_halves():
     row = lax.axis_index("y")
     upper = jnp.where(row > 1, 1, 0)
@@ -210,10 +195,23 @@
 
 
 def pair_kernel(
-    packs_ref, theirs_ref, their_ints_ref, rows_ref, owners_ref, split_ref, w_deg_ref,
-    w_gate_ref, embed_ref, out_ref, spread_ref, halo_ref, sums_ref, radial_ref, their_mixed_ref, their_gates_ref,
-    their_rows_ref, their_owners_ref,
+    packs_ref, theirs_ref, their_ints_ref, feats_ref, w_deg_ref, w_gate_ref, small_ref,
+    out_ref, spread_ref, halo_ref, sums_ref, radial_ref, ints_ref, const_ref,
+    mixed_ref, gates_ref, their_mixed_ref, their_gates_ref,
+    rows_ref, owners_ref, their_rows_ref, their_owners_ref, embed_ref,
 ):
+    embed_ref[...] = small_ref[EMBED_ROW:INTS_ROW, :]
+    ints_ref[...] = small_ref[INTS_ROW:CONST_ROW, :]
+    const_ref[...] = small_ref[CONST_ROW:, :]
+    w_radial = jnp.concatenate(
+        [small_ref[degree * BASES : (degree + 1) * BASES, :] for degree in range(DEGREES)], axis=1
+    )
+    radial_split = stacked(w_radial, (0, 0, 1, 1, 0, 2))
+    lists, species = lists_of(ints_ref)
+    owner_tables(lists, owners_ref)
+    encode_rows(
+        feats_ref, species, w_deg_ref, w_gate_ref, embed_ref, rows_ref, mixed_ref, gates_ref
+    )
     shards, chunk = out_ref.shape[1], out_ref.shape[2]
     own_row, first, partner_row = plane_halves()
     sub = lax.broadcasted_iota(jnp.int32, (ATOMS, PROBES), 0).astype(F32)
@@ -262,7 +260,7 @@
     total = None
     for degree in range(DEGREES):
         low, high = first_rows(degree)
-        radial = along_first(split_ref[:, lanes(degree)], basis_split)
+        radial = along_first(radial_split[:, lanes(degree)], basis_split)
         radial_ref[lanes(degree), :] = radial
         sums = jnp.concatenate(
             [
@@ -533,22 +531,18 @@
     with jax.named_scope("gather_pairs"):
         packs = lax.all_to_all(copies, "y", 0, 0)
     mixed_shapes = [shape((COMPS * ATOMS, CHANS)), shape((ATOMS, (DEGREES - 1) * CHANS))]
-    rows, owners, split, w_deg_near, w_gate_near, embed_near, own_ints, consts, mixed, gates = call(
-        encode_kernel,
-        [
-            shape((COMPS * ATOMS, CHANS), BF16),
-            shape((1 + len(OFFSETS), ATOMS, ATOMS), BF16),
-            shape((6 * BASES, DEGREES * CHANS), BF16),
-            shape(w_deg.shape, BF16),
-            shape(w_gate.shape, BF16),
-            shape(embed.shape),
-            shape(ints.shape),
-            shape((SMALL_ROWS - CONST_ROW, CHANS)),
-        ]
-        + mixed_shapes,
-        "encode",
-    )(atom_feats, w_deg, w_gate, small)
-    values, spread, halo, sums, radial, their_mixed, their_gates = call(
+    tables = [
+        pltpu.VMEM((COMPS * ATOMS, CHANS), BF16),
+        pltpu.VMEM((1 + len(OFFSETS), ATOMS, ATOMS), BF16),
+    ]
+    operands = (atom_feats, w_deg, w_gate, small)
+    feats, *weights = call(
+        stage_kernel, [shape(operand.shape, operand.dtype) for operand in operands], "stage"
+    )(*operands)
+    (
+        values, spread, halo, sums, radial, own_ints, consts,
+        mixed, gates, their_mixed, their_gates,
+    ) = call(
         pair_kernel,
         [
             shape((ROWS, shards, chunk, CHANS)),
@@ -556,13 +550,13 @@
             shape((COMPS * ATOMS, HALO_PAIRS), BF16),
             shape((DEGREES * CHANS + 2 * BASES, PAIRS), BF16),
             shape((DEGREES * CHANS, PAIRS)),
+            shape(ints.shape),
+            shape((SMALL_ROWS - CONST_ROW, CHANS)),
         ]
-        + mixed_shapes,
+        + mixed_shapes * 2,
         "pair_sums",
-        scratch_shapes=[pltpu.VMEM(rows.shape, BF16), pltpu.VMEM(owners.shape, BF16)],
-    )(
-        packs, theirs, their_ints, rows, owners, split, w_deg_near, w_gate_near, embed_near
-    )
+        scratch_shapes=tables * 2 + [pltpu.VMEM(embed.shape, F32)],
+    )(packs, theirs, their_ints, feats, *weights)
     with jax.named_scope("scatter_sums"):
         parts = lax.all_to_all(values.reshape(ROWS * shards, chunk, CHANS), PLANE, 0, 0)
     up, head, density_row = call(
@@ -578,7 +572,7 @@
     with jax.named_scope("gather_grads"):
         ups = lax.all_to_all(up, PLANE, 0, 0).reshape(ROWS, shards, chunk, CHANS)
     operands = (
-        atom_feats, theirs, own_ints, their_ints, mixed, their_mixed, gates, their_gates, radial,
+        feats, theirs, own_ints, their_ints, mixed, their_mixed, gates, their_gates, radial,
         head, density_row, ups, sums, spread, halo,
     )
     payload = call(backward_kernel, shape((PAYLOAD, CHANS), BF16), "backward")(*operands)

time: 117 us -> 114 us (0.974)
  local copies, waits for them, and re-layouts: 6.67 us -> 3.71 us
    unnamed x18 -> x8, local copies, waits for them, and re-layouts: 6.67 us -> 3.71 us
    all_to_all x1, blocking collectives: 20.6 us -> 19.4 us  [reduce_all(): parts = lax.all_to_all(copies, 'zh', 0, 0)]
    all_to_all x1, blocking collectives: 16.2 us -> 17.4 us  [on_device(): lax.all_to_all(values.reshape(ROWS * shards, chunk, CHANS), PLANE, 0, 0)]
where the time goes in v9:
time: 114 us; the launch traced here: 113 us
  blocking collectives  81.1 us (71%)
  starting transfers between devices  18.1 us (16%)
  Pallas kernels  9.83 us (9%)
  local copies, waits for them, and re-layouts  3.71 us (3%)
    all_to_all x1, blocking collectives, reduce_all(): parts = lax.all_to_all(copies, 'zh', 0, 0)  19.4 us
    all_to_all x1, blocking collectives, on_device(): lax.all_to_all(values.reshape(ROWS * shards, chunk, CHANS), PLANE, 0, 0)  17.4 us
    all_to_all x1, blocking collectives, reduce_all(): return lax.all_to_all(copies, NEAR, 0, 0).reshape(PAYLOAD, CHANS)  16.9 us
    all_to_all x1, blocking collectives, reduce_all(): parts = lax.all_to_all(payload.reshape(count, rows, CHANS), NEAR, 0, 0)  14.9 us
    ppermute x2, starting transfers between devices, to_partner(): return lax.ppermute(block, SLAB, route)  14.7 us
    all_to_all x1, blocking collectives, on_device(): ups = lax.all_to_all(up, PLANE, 0, 0).reshape(ROWS, shards, chunk, CHANS)  12.5 us
    unnamed x8, local copies, waits for them, and re-layouts  3.71 us
    all_to_all x1, starting transfers between devices, on_device(): packs = lax.all_to_all(copies, 'y', 0, 0)  3.34 us
  transfers between devices with their start and end apart: 3, of which 0 were waited for; matrix products, arithmetic and copies ran while one was open for 0% of the time, Pallas kernels for 2%

profile of v9, /device:TPU:1, one launch (start us, length us, event | category | flops | bytes accessed | tf_op | source)
XLA Modules:
  0.0 113.4 jit_solution(12775820400289041032)
XLA Ops:
  0.6 12.0 %collective-permute-start = (bf16[64,3200]{1,0:T(8,128)(2,1)}, bf16[64,3200]{1,0:T(8,128)(2,1)S(1)}, u32[]{:S(2)}, u32[]{:S(2)}) collective-permute-start(bf16[64,3200]{1,0:T(8,128)(2,1)} %refs_0_.1), channel_id=1, source_target_pairs={{0,480},{8,488},{16,48},{24,56},{32,0},{40,8},{48,80},{56,88},{64,... | collective-permute-start | bytes 1228808 | tf_op jit(solution)/shard_map/exchange_atoms/ppermute | solution.py:473
  12.6 1.8 %pack.1 = (f32[4,32,2,128]{3,2,1,0:T(2,128)}, f32[8,128]{1,0:T(8,128)}, f32[192,128]{1,0:T(8,128)}) custom-call(f32[25,2,128]{2,1,0:T(2,128)} %harm_hbm.1, f32[2,128]{1,0:T(2,128)} %dist_hbm.1, s32[2,128]{1,0:T(2,128)} %nbr_hbm.1, s32[4,64]{1,0:T(4,128)} %bitcast.17, s32[1,64]{1,0:T(1,128)} %bitcast.18, f32[8,640]{1,0:T(8,128)} %w_radial_hbm.1, ...), custom_call_target="tpu_custom_call" | custom-call | tf_op jit(solution)/shard_map/pack/pallas_call | solution.py:509
  14.4 3.3 %all-to-all-start = ((f32[4,32,2,128]{3,2,1,0:T(2,128)}), f32[4,32,2,128]{3,2,1,0:T(2,128)S(1)}, u32[]{:S(2)}, u32[]{:S(2)}) async-start(f32[4,32,2,128]{3,2,1,0:T(2,128)} %get-tuple-element.41), calls=%async_computation | async-start | bytes 262144 | tf_op jit(solution)/shard_map/gather_pairs/all_to_all | solution.py:532
  17.8 2.8 %collective-permute-start.1 = (f32[8,128]{1,0:T(8,128)}, f32[8,128]{1,0:T(8,128)S(1)}, u32[]{:S(2)}, u32[]{:S(2)}) collective-permute-start(f32[8,128]{1,0:T(8,128)} %get-tuple-element.42), channel_id=1, source_target_pairs={{0,480},{8,488},{16,48},{24,56},{32,0},{40,8},{48,80},{56,88},{64,... | collective-permute-start | bytes 12296 | tf_op jit(solution)/shard_map/exchange_lists/ppermute | solution.py:473
  20.6 0.0 copy-start
  20.6 1.0 copy-done
  21.6 0.0 copy-start.1
  21.6 0.9 copy-done.1
  22.5 0.0 copy-start.2
  22.5 0.9 copy-done.2
  23.4 0.0 copy-start.3
  23.4 0.9 copy-done.3
  24.3 0.1 stage.1
  24.3 0.0 collective-permute-done.1.their_ints_ref
  24.3 0.0 all-to-all-done.packs_ref
  24.3 0.0 collective-permute-done.theirs_ref
  24.4 3.0 %pair_sums.1 = (f32[4,8,16,128]{3,2,1,0:T(8,128)S(1)}, bf16[1600,1024]{1,0:T(8,128)(2,1)S(1)}, bf16[1600,512]{1,0:T(8,128)(2,1)S(1)}, bf16[656,1536]{1,0:T(8,128...) custom-call(f32[4,32,2,128]{3,2,1,0:T(2,128)S(1)} %all-to-all-done.p, ...), custom_call_target="tpu_custom_call" | custom-call | tf_op jit(solution)/shard_map/pair_sums/pallas_call | solution.py:545
  27.4 17.4 %all_to_all.30.parts_ref = f32[32,16,128]{2,1,0:T(8,128)S(1)} all-to-all(f32[32,16,128]{2,1,0:T(8,128)S(1)} %bitcast.16), channel_id=1, replica_groups=mesh['zh'=8,'zl'=2,'y'=4,'x'=4,'c'=2] {'y','x','c'}, dimensions={0} | all-to-all | bytes 524288 | tf_op jit(solution)/shard_map/scatter_sums/all_to_all | solution.py:561
  44.8 0.6 readout.1
  45.4 12.5 %all_to_all.31 = f32[32,16,128]{2,1,0:T(8,128)S(1)} all-to-all(f32[32,16,128]{2,1,0:T(8,128)S(1)} %get-tuple-element.56), channel_id=1, replica_groups=mesh['zh'=8,'zl'=2,'y'=4,'x'=4,'c'=2] {'y','x','c'}, dimensions={0} | all-to-all | bytes 524288 | tf_op jit(solution)/shard_map/gather_grads/all_to_all | solution.py:573
  57.9 3.3 %backward.1 = bf16[1536,128]{1,0:T(8,128)(2,1)S(1)} custom-call(bf16[64,3200]{1,0:T(8,128)(2,1)S(1)} %get-tuple-element.40.feats_ref.atoms_ref, bf16[64,3200]{1,0:T(8,128)(2,1)S(1)} %collective-permute-done.theirs_ref, f32[8,128]{1,0:T(8,128)S(1)} %get-tuple-element.46.ints_ref, f32[8,128]{1,0:T(8,128)S(1)} %collective-permute-done.1.their_ints_ref, ...), custom_call_target="tpu_custom_call" | custom-call | tf_op jit(solution)/shard_map/backward/pallas_call | solution.py:578
  61.2 14.9 %all_to_all.32.parts_ref = bf16[64,24,128]{2,1,0:T(8,128)(2,1)S(1)} all-to-all(bf16[64,24,128]{2,1,0:T(8,128)(2,1)S(1)} %bitcast.13), channel_id=1, replica_groups=mesh['zh'=8,'zl'=2,'y'=4,'x'=4,'c'=2] {'zl','y','x','c'}, dimensions={0} | all-to-all | bytes 786432 | tf_op jit(solution)/shard_map/reduce_grads/all_to_all | solution.py:479
  76.0 0.1 sum_near.1
  76.1 19.4 %all_to_all.33.parts_ref = bf16[8,24,128]{2,1,0:T(8,128)(2,1)S(1)} all-to-all(bf16[8,24,128]{2,1,0:T(8,128)(2,1)S(1)} %sum_near.1), channel_id=1, replica_groups=mesh['zh'=8,'zl'=2,'y'=4,'x'=4,'c'=2] {'zh'}, dimensions={0} | all-to-all | bytes 98304 | tf_op jit(solution)/shard_map/reduce_grads/all_to_all | solution.py:481
  95.6 16.9 %all_to_all.34 = bf16[64,24,128]{2,1,0:T(8,128)(2,1)S(1)} all-to-all(bf16[64,24,128]{2,1,0:T(8,128)(2,1)S(1)} %sum_depth.1), channel_id=1, replica_groups=mesh['zh'=8,'zl'=2,'y'=4,'x'=4,'c'=2] {'zl','y','x','c'}, dimensions={0} | all-to-all | bytes 786432 | tf_op jit(solution)/shard_map/reduce_grads/all_to_all | solution.py:483
  112.5 0.9 unpack.1
  (1 shorter events, 0.0 us)
Async XLA Ops:
  0.6 23.7 %collective-permute-start = (bf16[64,3200]{1,0:T(8,128)(2,1)}, bf16[64,3200]{1,0:T(8,128)(2,1)S(1)}, u32[]{:S(2)}, u32[]{:S(2)}) collective-permute-start(bf16[64,3200]{1,0:T(8,128)(2,1)} %refs_0_.1), channel_id=1, source_target_pairs={{0,480},{8,488},{16,48},{24,56},{32,0},{40,8},{48,80},{56,88},{64,... | collective-permute-start | bytes 1228808 | tf_op jit(solution)/shard_map/exchange_atoms/ppermute | solution.py:473
  14.4 9.9 %all-to-all-start = ((f32[4,32,2,128]{3,2,1,0:T(2,128)}), f32[4,32,2,128]{3,2,1,0:T(2,128)S(1)}, u32[]{:S(2)}, u32[]{:S(2)}) async-start(f32[4,32,2,128]{3,2,1,0:T(2,128)} %get-tuple-element.41), calls=%async_computation | async-start | bytes 262144 | tf_op jit(solution)/shard_map/gather_pairs/all_to_all | solution.py:532
  17.8 6.5 %collective-permute-start.1 = (f32[8,128]{1,0:T(8,128)}, f32[8,128]{1,0:T(8,128)S(1)}, u32[]{:S(2)}, u32[]{:S(2)}) collective-permute-start(f32[8,128]{1,0:T(8,128)} %get-tuple-element.42), channel_id=1, source_target_pairs={{0,480},{8,488},{16,48},{24,56},{32,0},{40,8},{48,80},{56,88},{64,... | collective-permute-start | bytes 12296 | tf_op jit(solution)/shard_map/exchange_lists/ppermute | solution.py:473
  20.6 1.0 copy-start
  21.6 0.9 copy-start.1
  22.5 0.9 copy-start.2
  23.4 0.9 copy-start.3

commit v10 on v9

--- a/solution.py
+++ b/solution.py
@@ -129,6 +129,14 @@
     return high, middle, low
 
 
+def halves(values, axis):
+    return jnp.concatenate(parts_of(values)[0:2], axis=axis)
+
+
+def folded(values):
+    return values[:, 0:CHANS] + values[:, CHANS:]
+
+
 def stacked(values, order):
     parts = [part.astype(F32) for part in parts_of(values)]
     return jnp.concatenate([parts[index] for index in order], axis=0).astype(BF16)
@@ -198,7 +206,7 @@
     packs_ref, theirs_ref, their_ints_ref, feats_ref, w_deg_ref, w_gate_ref, small_ref,
     out_ref, spread_ref, halo_ref, sums_ref, radial_ref, ints_ref, const_ref,
     mixed_ref, gates_ref, their_mixed_ref, their_gates_ref,
-    rows_ref, owners_ref, their_rows_ref, their_owners_ref, embed_ref,
+    rows_ref, owners_ref, their_rows_ref, their_owners_ref, embed_ref, values_ref,
 ):
     embed_ref[...] = small_ref[EMBED_ROW:INTS_ROW, :]
     ints_ref[...] = small_ref[INTS_ROW:CONST_ROW, :]
@@ -279,13 +287,13 @@
         return both.T
 
     for row in range(ROWS):
-        value = value_of(row)
+        values_ref[row] = value_of(row)
+    for row in range(HALO):
+        values_ref[first + row] += value_of(ROWS + row)
+    for row in range(ROWS):
         for shard in range(shards):
-            out_ref[row, shard] = value[shard * chunk : (shard + 1) * chunk, :]
-    for row in range(HALO):
-        value = value_of(ROWS + row)
-        for shard in range(shards):
-            out_ref[first + row, shard] += value[shard * chunk : (shard + 1) * chunk, :]
+            part = values_ref[row, shard * chunk : (shard + 1) * chunk, :]
+            out_ref[row, shard] = part.astype(BF16)
 
 
 def silu_slope(values):
@@ -312,9 +320,9 @@
     start = pl.multiple_of(shard * chunk, chunk)
     column_ref[...] = jnp.broadcast_to(const_ref[2:3, :], (PROBES, PROBES)).T
     target = column_ref[pl.ds(start, chunk), :]
-    summed = parts_ref[0]
+    summed = parts_ref[0].astype(F32)
     for index in range(1, parts_ref.shape[0]):
-        summed = summed + parts_ref[index]
+        summed = summed + parts_ref[index].astype(F32)
     w_hidden = const_ref[8:, :]
     w_out = const_ref[1:2, :]
     hidden_pre = matmul(summed, w_hidden, PRECISE) + const_ref[0:1, :]
@@ -327,7 +335,7 @@
     mask = (spot == lax.broadcasted_iota(jnp.int32, (chunk, PROBES), 1)).astype(F32)
     upstream = along_last(pre_grad, w_hidden, PRECISE)
     for copy in range(up_ref.shape[0]):
-        up_ref[copy] = upstream
+        up_ref[copy] = upstream.astype(BF16)
     density_ref[...] = jnp.sum(mask * density, axis=0, keepdims=True)
     head_ref[0:CHANS, :] = along_first(summed, pre_grad, PRECISE)
     bias = jnp.sum(pre_grad, axis=0, keepdims=True)
@@ -351,7 +359,7 @@
     first = plane_halves()[1]
 
     def block_of(row):
-        parts = [up_ref[row, shard] for shard in range(shards)]
+        parts = [up_ref[row, shard].astype(F32) for shard in range(shards)]
         return [jnp.concatenate(parts, axis=0).T] * SLOTS
 
     blocks = []
@@ -368,11 +376,11 @@
     for degree in range(DEGREES):
         low, high = first_rows(degree)
         size = high - low
-        inner = (radial_ref[lanes(degree), :] * upstream).astype(BF16)
+        inner = halves(radial_ref[lanes(degree), :] * upstream, 0)
         grads = jnp.concatenate(
             [
-                along_last(spread_ref[low:high, :], inner[:, 0:OWN_PAIRS]),
-                along_last(halo_ref[low:high, :], inner[:, OWN_PAIRS:]),
+                folded(along_last(spread_ref[low:high, :], inner[:, 0:OWN_PAIRS])),
+                folded(along_last(halo_ref[low:high, :], inner[:, OWN_PAIRS:])),
             ],
             axis=0,
         )
@@ -402,11 +410,11 @@
                     total = total + product[begin : begin + ATOMS, :]
                 totals.append(total)
             total = jnp.concatenate(totals, axis=0)
-            pre = (total * gate * (1.0 - gate)).astype(BF16)
+            pre = halves(total * gate * (1.0 - gate), 1)
             start = (DEGREES + degree - 1) * CHANS
-            payload_ref[start : start + CHANS, :] = along_first(scalar, pre).astype(BF16)
-        payload_ref[degree * CHANS : (degree + 1) * CHANS, :] = along_first(
-            rows, mixed_grad.astype(BF16)
+            payload_ref[start : start + CHANS, :] = folded(along_first(scalar, pre)).astype(BF16)
+        payload_ref[degree * CHANS : (degree + 1) * CHANS, :] = folded(
+            along_first(rows, halves(mixed_grad, 1))
         ).astype(BF16)
     base = (2 * DEGREES - 1) * CHANS
     payload_ref[base : base + CHANS + 16, :] = head_ref[...].astype(BF16)
@@ -545,7 +553,7 @@
     ) = call(
         pair_kernel,
         [
-            shape((ROWS, shards, chunk, CHANS)),
+            shape((ROWS, shards, chunk, CHANS), BF16),
             shape((COMPS * ATOMS, OWN_PAIRS), BF16),
             shape((COMPS * ATOMS, HALO_PAIRS), BF16),
             shape((DEGREES * CHANS + 2 * BASES, PAIRS), BF16),
@@ -555,14 +563,15 @@
         ]
         + mixed_shapes * 2,
         "pair_sums",
-        scratch_shapes=tables * 2 + [pltpu.VMEM(embed.shape, F32)],
+        scratch_shapes=tables * 2
+        + [pltpu.VMEM(embed.shape, F32), pltpu.VMEM((ROWS, PROBES, CHANS), F32)],
     )(packs, theirs, their_ints, feats, *weights)
     with jax.named_scope("scatter_sums"):
         parts = lax.all_to_all(values.reshape(ROWS * shards, chunk, CHANS), PLANE, 0, 0)
     up, head, density_row = call(
         functools.partial(readout_kernel, scale),
         [
-            shape((ROWS * shards, chunk, CHANS)),
+            shape((ROWS * shards, chunk, CHANS), BF16),
             shape((CHANS + 16, CHANS)),
             shape((1, PROBES)),
         ],

time: 114 us -> 112 us (0.982)
  blocking collectives: 81.1 us -> 78.7 us
    all_to_all x1, blocking collectives: 17.4 us -> 16.1 us  [on_device(): lax.all_to_all(values.reshape(ROWS * shards, chunk, CHANS), PLANE, 0, 0)]
    all_to_all x1, blocking collectives: 12.5 us -> 11.3 us  [on_device(): ups = lax.all_to_all(up, PLANE, 0, 0).reshape(ROWS, shards, chunk, CHANS)]
where the time goes in v10:
time: 112 us; the launch traced here: 111 us
  blocking collectives  78.7 us (70%)
  starting transfers between devices  18.1 us (16%)
  Pallas kernels  9.99 us (9%)
  local copies, waits for them, and re-layouts  3.71 us (3%)
    all_to_all x1, blocking collectives, reduce_all(): parts = lax.all_to_all(copies, 'zh', 0, 0)  19.4 us
    all_to_all x1, blocking collectives, reduce_all(): return lax.all_to_all(copies, NEAR, 0, 0).reshape(PAYLOAD, CHANS)  16.9 us
    all_to_all x1, blocking collectives, on_device(): lax.all_to_all(values.reshape(ROWS * shards, chunk, CHANS), PLANE, 0, 0)  16.1 us
    all_to_all x1, blocking collectives, reduce_all(): parts = lax.all_to_all(payload.reshape(count, rows, CHANS), NEAR, 0, 0)  15 us
    ppermute x2, starting transfers between devices, to_partner(): return lax.ppermute(block, SLAB, route)  14.7 us
    all_to_all x1, blocking collectives, on_device(): ups = lax.all_to_all(up, PLANE, 0, 0).reshape(ROWS, shards, chunk, CHANS)  11.3 us
    unnamed x8, local copies, waits for them, and re-layouts  3.71 us
    pallas_call x1, Pallas kernels, on_device(): call(backward_kernel, shape((PAYLOAD, CHANS), BF16), 'backward')(*operands)  3.4 us
  transfers between devices with their start and end apart: 3, of which 0 were waited for; matrix products, arithmetic and copies ran while one was open for 0% of the time, Pallas kernels for 2%

profile of v10, /device:TPU:1, one launch (start us, length us, event | category | flops | bytes accessed | tf_op | source)
XLA Modules:
  0.0 111.2 jit_solution(14603477284492729079)
XLA Ops:
  0.6 12.0 %collective-permute-start = (bf16[64,3200]{1,0:T(8,128)(2,1)}, bf16[64,3200]{1,0:T(8,128)(2,1)S(1)}, u32[]{:S(2)}, u32[]{:S(2)}) collective-permute-start(bf16[64,3200]{1,0:T(8,128)(2,1)} %refs_0_.1), channel_id=1, source_target_pairs={{0,480},{8,488},{16,48},{24,56},{32,0},{40,8},{48,80},{56,88},{64,... | collective-permute-start | bytes 1228808 | tf_op jit(solution)/shard_map/exchange_atoms/ppermute | solution.py:481
  12.6 1.8 %pack.1 = (f32[4,32,2,128]{3,2,1,0:T(2,128)}, f32[8,128]{1,0:T(8,128)}, f32[192,128]{1,0:T(8,128)}) custom-call(f32[25,2,128]{2,1,0:T(2,128)} %harm_hbm.1, f32[2,128]{1,0:T(2,128)} %dist_hbm.1, s32[2,128]{1,0:T(2,128)} %nbr_hbm.1, s32[4,64]{1,0:T(4,128)} %bitcast.17, s32[1,64]{1,0:T(1,128)} %bitcast.18, f32[8,640]{1,0:T(8,128)} %w_radial_hbm.1, ...), custom_call_target="tpu_custom_call" | custom-call | tf_op jit(solution)/shard_map/pack/pallas_call | solution.py:517
  14.4 3.3 %all-to-all-start = ((f32[4,32,2,128]{3,2,1,0:T(2,128)}), f32[4,32,2,128]{3,2,1,0:T(2,128)S(1)}, u32[]{:S(2)}, u32[]{:S(2)}) async-start(f32[4,32,2,128]{3,2,1,0:T(2,128)} %get-tuple-element.41), calls=%async_computation | async-start | bytes 262144 | tf_op jit(solution)/shard_map/gather_pairs/all_to_all | solution.py:540
  17.8 2.8 %collective-permute-start.1 = (f32[8,128]{1,0:T(8,128)}, f32[8,128]{1,0:T(8,128)S(1)}, u32[]{:S(2)}, u32[]{:S(2)}) collective-permute-start(f32[8,128]{1,0:T(8,128)} %get-tuple-element.42), channel_id=1, source_target_pairs={{0,480},{8,488},{16,48},{24,56},{32,0},{40,8},{48,80},{56,88},{64,... | collective-permute-start | bytes 12296 | tf_op jit(solution)/shard_map/exchange_lists/ppermute | solution.py:481
  20.6 0.0 copy-start
  20.6 1.0 copy-done
  21.6 0.0 copy-start.1
  21.6 0.9 copy-done.1
  22.5 0.0 copy-start.2
  22.5 0.9 copy-done.2
  23.4 0.0 copy-start.3
  23.4 0.9 copy-done.3
  24.3 0.1 stage.1
  24.3 0.0 collective-permute-done.1.their_ints_ref
  24.3 0.0 all-to-all-done.packs_ref
  24.3 0.0 collective-permute-done.theirs_ref
  24.4 3.1 %pair_sums.1 = (bf16[4,8,16,128]{3,2,1,0:T(8,128)(2,1)S(1)}, bf16[1600,1024]{1,0:T(8,128)(2,1)S(1)}, bf16[1600,512]{1,0:T(8,128)(2,1)S(1)}, bf16[656,1536]{1,0:T...) custom-call(f32[4,32,2,128]{3,2,1,0:T(2,128)S(1)} %all-to-all-done.p, ...), custom_call_target="tpu_custom_call" | custom-call | tf_op jit(solution)/shard_map/pair_sums/pallas_call | solution.py:553
  27.4 16.1 %all_to_all.30.parts_ref = bf16[32,16,128]{2,1,0:T(8,128)(2,1)S(1)} all-to-all(bf16[32,16,128]{2,1,0:T(8,128)(2,1)S(1)} %bitcast.16), channel_id=1, replica_groups=mesh['zh'=8,'zl'=2,'y'=4,'x'=4,'c'=2] {'y','x','c'}, dimensions={0} | all-to-all | bytes 262144 | tf_op jit(solution)/shard_map/scatter_sums/all_to_all | solution.py:570
  43.5 0.6 readout.1
  44.2 11.3 %all_to_all.31 = bf16[32,16,128]{2,1,0:T(8,128)(2,1)S(1)} all-to-all(bf16[32,16,128]{2,1,0:T(8,128)(2,1)S(1)} %get-tuple-element.56), channel_id=1, replica_groups=mesh['zh'=8,'zl'=2,'y'=4,'x'=4,'c'=2] {'y','x','c'}, dimensions={0} | all-to-all | bytes 262144 | tf_op jit(solution)/shard_map/gather_grads/all_to_all | solution.py:582
  55.4 3.4 %backward.1 = bf16[1536,128]{1,0:T(8,128)(2,1)S(1)} custom-call(bf16[64,3200]{1,0:T(8,128)(2,1)S(1)} %get-tuple-element.40.feats_ref.atoms_ref, bf16[64,3200]{1,0:T(8,128)(2,1)S(1)} %collective-permute-done.theirs_ref, f32[8,128]{1,0:T(8,128)S(1)} %get-tuple-element.46.ints_ref, f32[8,128]{1,0:T(8,128)S(1)} %collective-permute-done.1.their_ints_ref, ...), custom_call_target="tpu_custom_call" | custom-call | tf_op jit(solution)/shard_map/backward/pallas_call | solution.py:587
  58.9 15.0 %all_to_all.32.parts_ref = bf16[64,24,128]{2,1,0:T(8,128)(2,1)S(1)} all-to-all(bf16[64,24,128]{2,1,0:T(8,128)(2,1)S(1)} %bitcast.13), channel_id=1, replica_groups=mesh['zh'=8,'zl'=2,'y'=4,'x'=4,'c'=2] {'zl','y','x','c'}, dimensions={0} | all-to-all | bytes 786432 | tf_op jit(solution)/shard_map/reduce_grads/all_to_all | solution.py:487
  73.8 0.1 sum_near.1
  73.9 19.4 %all_to_all.33.parts_ref = bf16[8,24,128]{2,1,0:T(8,128)(2,1)S(1)} all-to-all(bf16[8,24,128]{2,1,0:T(8,128)(2,1)S(1)} %sum_near.1), channel_id=1, replica_groups=mesh['zh'=8,'zl'=2,'y'=4,'x'=4,'c'=2] {'zh'}, dimensions={0} | all-to-all | bytes 98304 | tf_op jit(solution)/shard_map/reduce_grads/all_to_all | solution.py:489
  93.4 16.9 %all_to_all.34 = bf16[64,24,128]{2,1,0:T(8,128)(2,1)S(1)} all-to-all(bf16[64,24,128]{2,1,0:T(8,128)(2,1)S(1)} %sum_depth.1), channel_id=1, replica_groups=mesh['zh'=8,'zl'=2,'y'=4,'x'=4,'c'=2] {'zl','y','x','c'}, dimensions={0} | all-to-all | bytes 786432 | tf_op jit(solution)/shard_map/reduce_grads/all_to_all | solution.py:491
  110.3 0.9 unpack.1
  (1 shorter events, 0.0 us)
Async XLA Ops:
  0.6 23.7 %collective-permute-start = (bf16[64,3200]{1,0:T(8,128)(2,1)}, bf16[64,3200]{1,0:T(8,128)(2,1)S(1)}, u32[]{:S(2)}, u32[]{:S(2)}) collective-permute-start(bf16[64,3200]{1,0:T(8,128)(2,1)} %refs_0_.1), channel_id=1, source_target_pairs={{0,480},{8,488},{16,48},{24,56},{32,0},{40,8},{48,80},{56,88},{64,... | collective-permute-start | bytes 1228808 | tf_op jit(solution)/shard_map/exchange_atoms/ppermute | solution.py:481
  14.4 9.9 %all-to-all-start = ((f32[4,32,2,128]{3,2,1,0:T(2,128)}), f32[4,32,2,128]{3,2,1,0:T(2,128)S(1)}, u32[]{:S(2)}, u32[]{:S(2)}) async-start(f32[4,32,2,128]{3,2,1,0:T(2,128)} %get-tuple-element.41), calls=%async_computation | async-start | bytes 262144 | tf_op jit(solution)/shard_map/gather_pairs/all_to_all | solution.py:540
  17.8 6.5 %collective-permute-start.1 = (f32[8,128]{1,0:T(8,128)}, f32[8,128]{1,0:T(8,128)S(1)}, u32[]{:S(2)}, u32[]{:S(2)}) collective-permute-start(f32[8,128]{1,0:T(8,128)} %get-tuple-element.42), channel_id=1, source_target_pairs={{0,480},{8,488},{16,48},{24,56},{32,0},{40,8},{48,80},{56,88},{64,... | collective-permute-start | bytes 12296 | tf_op jit(solution)/shard_map/exchange_lists/ppermute | solution.py:481
  20.6 1.0 copy-start
  21.6 0.9 copy-start.1
  22.5 0.9 copy-start.2
  23.4 0.9 copy-start.3

commit v11 on v10

--- a/solution.py
+++ b/solution.py
@@ -264,7 +264,7 @@
     phase = math.pi * dist / CUTOFF
     envelope = 0.5 * (jnp.cos(phase) + 1.0) / dist
     basis_split = stacked(jnp.sin(phase * orders) * envelope, (0, 1, 0, 1, 2, 0))
-    sums_ref[DEGREES * CHANS :, :] = basis_split[0 : 2 * BASES, :]
+    sums_ref[DEGREES * CHANS :, :] = basis_split[0 : 2 * BASES, :].astype(F32)
     total = None
     for degree in range(DEGREES):
         low, high = first_rows(degree)
@@ -277,7 +277,7 @@
             ],
             axis=1,
         )
-        sums_ref[lanes(degree), :] = sums.astype(BF16)
+        sums_ref[lanes(degree), :] = sums
         term = radial * sums
         total = term if total is None else total + term
 
@@ -371,7 +371,7 @@
     kinds = jnp.concatenate(
         [kind_rows(lists_of(ref)[1]) for ref in (ints_ref, their_ints_ref)], axis=1
     )
-    basis_split = sums_ref[DEGREES * CHANS :, :]
+    basis_split = sums_ref[DEGREES * CHANS :, :].astype(BF16)
     radial_grads = []
     for degree in range(DEGREES):
         low, high = first_rows(degree)
@@ -384,8 +384,9 @@
             ],
             axis=0,
         )
-        product = (sums_ref[lanes(degree), :].astype(F32) * upstream).astype(BF16)
+        product = halves(sums_ref[lanes(degree), :] * upstream, 0)
         both = along_last(product, basis_split)
+        both = both[0:CHANS, :] + both[CHANS:, :]
         radial_grads.append((both[:, 0:BASES] + both[:, BASES : 2 * BASES]).T)
         rows = jnp.concatenate(
             [component_rows(atoms_ref, degree), component_rows(theirs_ref, degree)], axis=0
@@ -556,7 +557,7 @@
             shape((ROWS, shards, chunk, CHANS), BF16),
             shape((COMPS * ATOMS, OWN_PAIRS), BF16),
             shape((COMPS * ATOMS, HALO_PAIRS), BF16),
-            shape((DEGREES * CHANS + 2 * BASES, PAIRS), BF16),
+            shape((DEGREES * CHANS + 2 * BASES, PAIRS)),
             shape((DEGREES * CHANS, PAIRS)),
             shape(ints.shape),
             shape((SMALL_ROWS - CONST_ROW, CHANS)),

time: 112 us -> 112 us (level)
  no operation moved by 1% of the time
where the time goes in v11:
time: 112 us
  blocking collectives  78.7 us (70%)
  starting transfers between devices  18.1 us (16%)
  Pallas kernels  10.6 us (9%)
  local copies, waits for them, and re-layouts  3.71 us (3%)
    all_to_all x1, blocking collectives, reduce_all(): parts = lax.all_to_all(copies, 'zh', 0, 0)  19.4 us
    all_to_all x1, blocking collectives, reduce_all(): return lax.all_to_all(copies, NEAR, 0, 0).reshape(PAYLOAD, CHANS)  16.9 us
    all_to_all x1, blocking collectives, on_device(): lax.all_to_all(values.reshape(ROWS * shards, chunk, CHANS), PLANE, 0, 0)  16.1 us
    all_to_all x1, blocking collectives, reduce_all(): parts = lax.all_to_all(payload.reshape(count, rows, CHANS), NEAR, 0, 0)  15 us
    ppermute x2, starting transfers between devices, to_partner(): return lax.ppermute(block, SLAB, route)  14.7 us
    all_to_all x1, blocking collectives, on_device(): ups = lax.all_to_all(up, PLANE, 0, 0).reshape(ROWS, shards, chunk, CHANS)  11.3 us
    pallas_call x1, Pallas kernels, on_device(): call(backward_kernel, shape((PAYLOAD, CHANS), BF16), 'backward')(*operands)  3.94 us
    unnamed x8, local copies, waits for them, and re-layouts  3.71 us
  transfers between devices with their start and end apart: 3, of which 0 were waited for; matrix products, arithmetic and copies ran while one was open for 0% of the time, Pallas kernels for 2%

profile of v11, /device:TPU:1, one launch (start us, length us, event | category | flops | bytes accessed | tf_op | source)
XLA Modules:
  0.0 111.8 jit_solution(8547440407443876847)
XLA Ops:
  0.6 12.0 %collective-permute-start = (bf16[64,3200]{1,0:T(8,128)(2,1)}, bf16[64,3200]{1,0:T(8,128)(2,1)S(1)}, u32[]{:S(2)}, u32[]{:S(2)}) collective-permute-start(bf16[64,3200]{1,0:T(8,128)(2,1)} %refs_0_.1), channel_id=1, source_target_pairs={{0,480},{8,488},{16,48},{24,56},{32,0},{40,8},{48,80},{56,88},{64,... | collective-permute-start | bytes 1228808 | tf_op jit(solution)/shard_map/exchange_atoms/ppermute | solution.py:482
  12.6 1.8 %pack.1 = (f32[4,32,2,128]{3,2,1,0:T(2,128)}, f32[8,128]{1,0:T(8,128)}, f32[192,128]{1,0:T(8,128)}) custom-call(f32[25,2,128]{2,1,0:T(2,128)} %harm_hbm.1, f32[2,128]{1,0:T(2,128)} %dist_hbm.1, s32[2,128]{1,0:T(2,128)} %nbr_hbm.1, s32[4,64]{1,0:T(4,128)} %bitcast.17, s32[1,64]{1,0:T(1,128)} %bitcast.18, f32[8,640]{1,0:T(8,128)} %w_radial_hbm.1, ...), custom_call_target="tpu_custom_call" | custom-call | tf_op jit(solution)/shard_map/pack/pallas_call | solution.py:518
  14.4 3.3 %all-to-all-start = ((f32[4,32,2,128]{3,2,1,0:T(2,128)}), f32[4,32,2,128]{3,2,1,0:T(2,128)S(1)}, u32[]{:S(2)}, u32[]{:S(2)}) async-start(f32[4,32,2,128]{3,2,1,0:T(2,128)} %get-tuple-element.41), calls=%async_computation | async-start | bytes 262144 | tf_op jit(solution)/shard_map/gather_pairs/all_to_all | solution.py:541
  17.8 2.8 %collective-permute-start.1 = (f32[8,128]{1,0:T(8,128)}, f32[8,128]{1,0:T(8,128)S(1)}, u32[]{:S(2)}, u32[]{:S(2)}) collective-permute-start(f32[8,128]{1,0:T(8,128)} %get-tuple-element.42), channel_id=1, source_target_pairs={{0,480},{8,488},{16,48},{24,56},{32,0},{40,8},{48,80},{56,88},{64,... | collective-permute-start | bytes 12296 | tf_op jit(solution)/shard_map/exchange_lists/ppermute | solution.py:482
  20.6 0.0 copy-start
  20.6 1.0 copy-done
  21.6 0.0 copy-start.1
  21.6 0.9 copy-done.1
  22.5 0.0 copy-start.2
  22.5 0.9 copy-done.2
  23.4 0.0 copy-start.3
  23.4 0.9 copy-done.3
  24.3 0.1 stage.1
  24.3 0.0 collective-permute-done.1.their_ints_ref
  24.3 0.0 all-to-all-done.packs_ref
  24.3 0.0 collective-permute-done.theirs_ref
  24.4 3.1 %pair_sums.1 = (bf16[4,8,16,128]{3,2,1,0:T(8,128)(2,1)S(1)}, bf16[1600,1024]{1,0:T(8,128)(2,1)S(1)}, bf16[1600,512]{1,0:T(8,128)(2,1)S(1)}, f32[656,1536]{1,0:T(...) custom-call(f32[4,32,2,128]{3,2,1,0:T(2,128)S(1)} %all-to-all-done.p, ...), custom_call_target="tpu_custom_call" | custom-call | tf_op jit(solution)/shard_map/pair_sums/pallas_call | solution.py:554
  27.5 16.1 %all_to_all.30.parts_ref = bf16[32,16,128]{2,1,0:T(8,128)(2,1)S(1)} all-to-all(bf16[32,16,128]{2,1,0:T(8,128)(2,1)S(1)} %bitcast.16), channel_id=1, replica_groups=mesh['zh'=8,'zl'=2,'y'=4,'x'=4,'c'=2] {'y','x','c'}, dimensions={0} | all-to-all | bytes 262144 | tf_op jit(solution)/shard_map/scatter_sums/all_to_all | solution.py:571
  43.6 0.6 readout.1
  44.3 11.3 %all_to_all.31 = bf16[32,16,128]{2,1,0:T(8,128)(2,1)S(1)} all-to-all(bf16[32,16,128]{2,1,0:T(8,128)(2,1)S(1)} %get-tuple-element.56), channel_id=1, replica_groups=mesh['zh'=8,'zl'=2,'y'=4,'x'=4,'c'=2] {'y','x','c'}, dimensions={0} | all-to-all | bytes 262144 | tf_op jit(solution)/shard_map/gather_grads/all_to_all | solution.py:583
  55.5 3.9 %backward.1 = bf16[1536,128]{1,0:T(8,128)(2,1)S(1)} custom-call(bf16[64,3200]{1,0:T(8,128)(2,1)S(1)} %get-tuple-element.40.feats_ref.atoms_ref, bf16[64,3200]{1,0:T(8,128)(2,1)S(1)} %collective-permute-done.theirs_ref, f32[8,128]{1,0:T(8,128)S(1)} %get-tuple-element.46.ints_ref, f32[8,128]{1,0:T(8,128)S(1)} %collective-permute-done.1.their_ints_ref, ...), custom_call_target="tpu_custom_call" | custom-call | tf_op jit(solution)/shard_map/backward/pallas_call | solution.py:588
  59.5 15.0 %all_to_all.32.parts_ref = bf16[64,24,128]{2,1,0:T(8,128)(2,1)S(1)} all-to-all(bf16[64,24,128]{2,1,0:T(8,128)(2,1)S(1)} %bitcast.14), channel_id=1, replica_groups=mesh['zh'=8,'zl'=2,'y'=4,'x'=4,'c'=2] {'zl','y','x','c'}, dimensions={0} | all-to-all | bytes 786432 | tf_op jit(solution)/shard_map/reduce_grads/all_to_all | solution.py:488
  74.4 0.1 sum_near.1
  74.5 19.4 %all_to_all.33.parts_ref = bf16[8,24,128]{2,1,0:T(8,128)(2,1)S(1)} all-to-all(bf16[8,24,128]{2,1,0:T(8,128)(2,1)S(1)} %sum_near.1), channel_id=1, replica_groups=mesh['zh'=8,'zl'=2,'y'=4,'x'=4,'c'=2] {'zh'}, dimensions={0} | all-to-all | bytes 98304 | tf_op jit(solution)/shard_map/reduce_grads/all_to_all | solution.py:490
  94.0 16.9 %all_to_all.34 = bf16[64,24,128]{2,1,0:T(8,128)(2,1)S(1)} all-to-all(bf16[64,24,128]{2,1,0:T(8,128)(2,1)S(1)} %sum_depth.1), channel_id=1, replica_groups=mesh['zh'=8,'zl'=2,'y'=4,'x'=4,'c'=2] {'zl','y','x','c'}, dimensions={0} | all-to-all | bytes 786432 | tf_op jit(solution)/shard_map/reduce_grads/all_to_all | solution.py:492
  110.9 0.9 unpack.1
  (1 shorter events, 0.0 us)
Async XLA Ops:
  0.6 23.7 %collective-permute-start = (bf16[64,3200]{1,0:T(8,128)(2,1)}, bf16[64,3200]{1,0:T(8,128)(2,1)S(1)}, u32[]{:S(2)}, u32[]{:S(2)}) collective-permute-start(bf16[64,3200]{1,0:T(8,128)(2,1)} %refs_0_.1), channel_id=1, source_target_pairs={{0,480},{8,488},{16,48},{24,56},{32,0},{40,8},{48,80},{56,88},{64,... | collective-permute-start | bytes 1228808 | tf_op jit(solution)/shard_map/exchange_atoms/ppermute | solution.py:482
  14.4 9.9 %all-to-all-start = ((f32[4,32,2,128]{3,2,1,0:T(2,128)}), f32[4,32,2,128]{3,2,1,0:T(2,128)S(1)}, u32[]{:S(2)}, u32[]{:S(2)}) async-start(f32[4,32,2,128]{3,2,1,0:T(2,128)} %get-tuple-element.41), calls=%async_computation | async-start | bytes 262144 | tf_op jit(solution)/shard_map/gather_pairs/all_to_all | solution.py:541
  17.8 6.5 %collective-permute-start.1 = (f32[8,128]{1,0:T(8,128)}, f32[8,128]{1,0:T(8,128)S(1)}, u32[]{:S(2)}, u32[]{:S(2)}) collective-permute-start(f32[8,128]{1,0:T(8,128)} %get-tuple-element.42), channel_id=1, source_target_pairs={{0,480},{8,488},{16,48},{24,56},{32,0},{40,8},{48,80},{56,88},{64,... | collective-permute-start | bytes 12296 | tf_op jit(solution)/shard_map/exchange_lists/ppermute | solution.py:482
  20.6 1.0 copy-start
  21.6 0.9 copy-start.1
  22.5 0.9 copy-start.2
  23.4 0.9 copy-start.3
